TPU v7x, 512 devices: a whole 4x4x16 slice. The times are simulated.
512 devices in a mesh: dp: 2 (over y_hi), fsdp: 32 (over z, core), tensor: 8 (over y_lo, x).
Axes of the slice: x: 4, y: 4 (y_hi: 2, y_lo: 2; y = y_hi * 2 + y_lo), z: 16, core: 2. Of those that a mesh axis runs over, the one named last changes fastest.
Arguments:
- tokens: bfloat16 [1024, 8192], P(('dp', 'fsdp'), 'tensor'), may hold values from -6 to 6
- base_weight: bfloat16 [2, 8192, 24576], P(None, 'tensor', 'fsdp'), may hold values from -0.0625 to 0.0625
- factor_b: bfloat16 [2, 8192, 64], P(None, 'tensor'), may hold values from -0.0625 to 0.0625
- factor_a: bfloat16 [2, 64, 24576], P(None, None, 'fsdp'), may hold values from -0.75 to 0.75
- magnitude: float32 [2, 24576], P(None, 'fsdp'), may hold values from 0.5 to 2
- cotangent: bfloat16 [1024, 24576], P(('dp', 'tensor'), 'fsdp'), may hold values from -6 to 6
Outputs:
- grad_a: float32 [2, 64, 24576], P(None, None, 'fsdp')
- grad_b: float32 [2, 8192, 64], P(None, 'tensor')
- grad_m: float32 [2, 24576], P(None, 'fsdp')
All inputs are finite; a program needn't handle non-finite values.
Results may differ from a plain program's by a relative error of at most 0.0003.
Values may be sent and summed in bfloat16 or wider, within the bound.
No kernel may reach another device: no remote copies, remote signals or barrier semaphores. Data moves between devices by JAX's collectives and lax.ppermute only.
A program may use at most 64 MiB of HBM per device.

v0:
```python
import jax
import jax.numpy as jnp
from jax import lax
from jax.sharding import PartitionSpec as P


def per_device(tokens, base_weight, factor_b, factor_a, magnitude, cotangent):
    highest = lax.Precision.HIGHEST
    gathered = lax.all_gather(tokens, "fsdp", axis=0, tiled=True)
    group_rows = gathered.shape[0]
    owned = group_rows // lax.axis_size("tensor")
    columns = base_weight.shape[2]
    rank = factor_a.shape[1]
    groups = float(lax.axis_size("dp"))
    a_wide = factor_a.astype(jnp.float32)
    combined = base_weight.astype(jnp.float32) + jnp.einsum(
        "kdr,krf->kdf", factor_b, factor_a, preferred_element_type=jnp.float32
    )
    sq_part = jnp.sum(combined * combined, axis=1)
    base_own = lax.psum_scatter(
        jnp.einsum(
            "td,kdf->tkf", gathered, base_weight, preferred_element_type=jnp.float32
        ).reshape(lax.axis_size("tensor") * owned, 2 * columns),
        "tensor",
        scatter_dimension=0,
        tiled=True,
    )
    low_all = jnp.einsum("td,kdr->tkr", gathered, factor_b, preferred_element_type=jnp.float32)
    low_total = lax.psum(low_all, "tensor")
    low_own = lax.dynamic_slice_in_dim(low_total, lax.axis_index("tensor") * owned, owned, 0)
    sq_total = lax.psum(sq_part, "tensor")
    norm = jnp.sqrt(sq_total + 1e-06)
    pre = base_own.reshape(owned, 2, columns) + jnp.einsum(
        "tkr,krf->tkf", low_own, a_wide, precision=highest
    )
    scale = magnitude / norm
    outputs = pre * scale[None]
    gate = outputs[:, 0]
    up_val = outputs[:, 1]
    sig = jax.nn.sigmoid(gate)
    grad_h = cotangent.astype(jnp.float32)
    dout = jnp.stack(
        [grad_h * up_val * sig * (1.0 + gate * (1.0 - sig)), grad_h * gate * sig], axis=1
    )
    dpre = dout * scale[None]
    m_local = jnp.sum(dout * pre, axis=0)
    token_a = jnp.einsum("tkr,tkf->krf", low_own, dpre, precision=highest)
    cross = jnp.einsum("kdr,kdf->krf", factor_b.astype(jnp.float32), combined, precision=highest)
    grad_m = lax.psum(m_local, ("dp", "tensor")) / norm
    coeff = -grad_m * magnitude / (norm * norm)
    grad_a = lax.psum(token_a + cross * coeff[:, None, :] / groups, ("dp", "tensor"))
    back_part = jnp.einsum("tkf,krf->tkr", dpre, a_wide, precision=highest).reshape(owned, 2 * rank)
    back_all = lax.all_gather(back_part, "tensor", axis=0, tiled=True)
    token_b = lax.dot_general(
        gathered.astype(jnp.float32), back_all, (((0,), (0,)), ((), ())), precision=highest
    )
    token_b = jnp.transpose(token_b.reshape(token_b.shape[0], 2, rank), (1, 0, 2))
    value_b = jnp.einsum("kdf,krf->kdr", combined * coeff[:, None, :], a_wide, precision=highest)
    grad_b = lax.psum(token_b + value_b / groups, ("dp", "fsdp"))
    return (grad_a, grad_b, grad_m)


def solution(mesh):
    return jax.shard_map(
        per_device,
        mesh=mesh,
        in_specs=(
            P(("dp", "fsdp"), "tensor"),
            P(None, "tensor", "fsdp"),
            P(None, "tensor", None),
            P(None, None, "fsdp"),
            P(None, "fsdp"),
            P(("dp", "tensor"), "fsdp"),
        ),
        out_specs=(P(None, None, "fsdp"), P(None, "tensor", None), P(None, "fsdp")),
        check_vma=False,
    )
```

profile of v0, /device:TPU:1, one launch (start us, length us, event | category | flops | bytes accessed | tf_op | source)
XLA Modules:
  0.0 960.3 jit_solution(12255233197271741485)
XLA Ops:
  7.2 0.0 copy-start
  7.2 0.0 all-gather.2.cloned.1.call-start
  7.2 0.7 all-gather.2.cloned.1.call-update
  7.9 0.0 reduce-scatter.4.cloned.1.call-start
  8.0 78.6 %all-gather.2.cloned.1.call-done = bf16[512,1024]{1,0:T(8,128)(2,1)} async-done(((bf16[16,1024]{1,0:T(8,128)(2,1)}), bf16[512,1024]{1,0:T(8,128)(2,1)}) %all-gather.2.cloned.1.call-update) | async-done | bytes 1048592 | tf_op jit(solution)/shard_map/all_gather | solution.py:9
  86.5 5.7 fusion.12
  92.3 0.0 copy-start.1
  92.3 0.0 copy-start.2
  92.3 3.7 copy.24
  95.9 0.0 reduce-scatter.4.cloned.1.call-update
  96.0 0.0 copy-start.4
  96.0 0.0 all-reduce.4.cloned.1.call-start
  96.0 0.0 copy-done
  96.0 0.0 copy-done.1
  96.1 1.3 fusion.14
  97.3 0.0 all-reduce.4.cloned.1.call-update
  97.3 0.0 copy-start.3
  97.3 0.0 all-reduce.6.cloned.1.call-start
  97.4 0.0 copy-done.2
  97.4 5.6 multiply_reduce_fusion
  103.0 16.7 %psum.36 = f32[2,768]{1,0:T(2,128)S(1)} all-reduce(f32[2,768]{1,0:T(2,128)S(1)} %get-tuple-element.7), channel_id=1, replica_groups=mesh['dp'=2,'fsdp'=32,'tensor'=8] {'tensor'}, use_global_device_ids=true, to_apply=%region_3.0 | all-reduce | flops 1536 | bytes 12288 | tf_op jit(solution)/shard_map/psum | solution.py:31
  119.8 0.0 copy-done.4
  119.8 23.1 %reduce-scatter.4.cloned.1.call-done = f32[64,1536]{1,0:T(8,128)} async-done(((f32[512,1536]{1,0:T(8,128)}), f32[64,1536]{1,0:T(8,128)}) %reduce-scatter.4.cloned.1.call-update) | async-done | bytes 393232
  142.9 1.3 copy.25
  144.2 0.3 copy.17
  144.5 90.7 %all-reduce.4.cloned.1.call-done = f32[512,2,64]{2,0,1:T(8,128)} async-done(((f32[512,2,64]{2,0,1:T(8,128)}), f32[512,2,64]{2,0,1:T(8,128)}) %all-reduce.4.cloned.1.call-update) | async-done | bytes 262160 | tf_op jit(solution)/shard_map/psum | solution.py:29
  235.2 1.1 broadcast_multiply_fusion
  236.3 0.0 copy-done.3
  236.3 0.1 fusion.20
  236.4 0.3 convolution_bitcast_fusion.1
  236.8 0.1 multiply_reduce_fusion.1
  236.8 31.5 %psum.37 = f32[2,768]{1,0:T(2,128)S(1)} all-reduce(f32[2,768]{1,0:T(2,128)S(1)} %multiply_reduce_fusion.1), channel_id=1, replica_groups=mesh['dp'=2,'fsdp'=32,'tensor'=8] {'dp','tensor'}, use_global_device_ids=true, to_apply=%region_5.0 | all-reduce | flops 1536 | bytes 12288 | tf_op jit(solution)/shard_map/psum | solution.py:49
  268.4 0.6 multiply_divide_fusion
  269.0 0.1 copy.19
  269.1 0.1 reshape.22
  269.2 22.3 %all_gather.7 = f32[512,128]{1,0:T(8,128)S(1)} all-gather(f32[64,128]{1,0:T(8,128)S(1)} %reshape.22), channel_id=1, replica_groups=mesh['dp'=2,'fsdp'=32,'tensor'=8] {'tensor'}, dimensions={0}, use_global_device_ids=true | all-gather | bytes 294912 | tf_op jit(solution)/shard_map/all_gather | solution.py:53
  291.5 5.2 fusion.11
  296.6 2.1 convolution_add_fusion
  298.7 0.0 all-reduce.6.cloned.1.call-update
  298.8 0.2 all-reduce.8.cloned.1.call-start
  299.0 0.6 fusion.34
  299.6 7.0 fusion.6
  306.7 0.0 all-reduce.8.cloned.1.call-update
  306.7 121.6 %all-reduce.6.cloned.1.call-done = f32[2,64,768]{2,1,0:T(8,128)} async-done(((f32[2,64,768]{2,1,0:T(8,128)}), f32[2,64,768]{2,1,0:T(8,128)}) %all-reduce.6.cloned.1.call-update) | async-done | bytes 393232 | tf_op jit(solution)/shard_map/psum | solution.py:51
  428.3 521.8 %all-reduce.8.cloned.1.call-done = f32[2,1024,64]{1,2,0:T(8,128)} async-done(((f32[2,1024,64]{1,2,0:T(8,128)}), f32[2,1024,64]{1,2,0:T(8,128)}) %all-reduce.8.cloned.1.call-update) | async-done | bytes 524304 | tf_op jit(solution)/shard_map/psum | solution.py:59
  950.1 1.8 copy.29
  951.8 1.9 copy.30
  (1 shorter events, 0.0 us)
Async XLA Ops:
  7.2 88.9 %copy-start = (bf16[2,1024,64]{1,2,0:T(8,128)(2,1)S(1)}, bf16[2,1024,64]{1,2,0:T(8,128)(2,1)}, u32[]{:S(2)}) copy-start(bf16[2,1024,64]{1,2,0:T(8,128)(2,1)} %param.8) | copy-start | bytes 786436
  7.2 79.4 %all-gather.2.cloned.1.call-start = ((), (), s32[]{:S(2)}) async-start(), calls=%async_computation.1 | async-start | bytes 1081344 | tf_op jit(solution)/shard_map/all_gather | solution.py:9
  7.9 135.0 %reduce-scatter.4.cloned.1.call-start = ((), (), s32[]{:S(2)}) async-start(), calls=%async_computation.5 | async-start | bytes 3538944
  92.3 3.8 copy-start.1
  92.3 5.1 copy-start.2
  96.0 23.8 %copy-start.4 = (f32[2,768]{1,0:T(2,128)S(1)}, f32[2,768]{1,0:T(2,128)}, u32[]{:S(2)}) copy-start(f32[2,768]{1,0:T(2,128)} %param.10) | copy-start | bytes 18436
  96.0 139.2 %all-reduce.4.cloned.1.call-start = ((), (), s32[]{:S(2)}) async-start(), calls=%async_computation.2 | async-start | bytes 1048576 | tf_op jit(solution)/shard_map/psum | solution.py:29
  97.3 139.0 %copy-start.3 = (bf16[64,768]{1,0:T(8,128)(2,1)S(1)}, bf16[64,768]{1,0:T(8,128)(2,1)}, u32[]{:S(2)}) copy-start(bf16[64,768]{1,0:T(8,128)(2,1)} %param.11) | copy-start | bytes 294916
  97.3 330.9 %all-reduce.6.cloned.1.call-start = ((), (), s32[]{:S(2)}) async-start(), calls=%async_computation.3 | async-start | bytes 786432 | tf_op jit(solution)/shard_map/psum | solution.py:51
  298.8 651.3 %all-reduce.8.cloned.1.call-start = ((), (), s32[]{:S(2)}) async-start(), calls=%async_computation.4 | async-start | bytes 1048576 | tf_op jit(solution)/shard_map/psum | solution.py:59
Sparse Core Ops, SparseCore 0:
  10.1 76.3 all-gather.1
  96.1 46.7 reduce-scatter.3
  146.4 88.6 all-reduce.3
  298.9 129.3 all-reduce.5
  431.9 518.1 all-reduce.7
where the time goes:
time: 961 us; the launch traced here: 960 us
  waiting for transfers between devices  837 us (87%)
  blocking collectives  70.6 us (7%)
  matrix products  29 us (3%)
  between operations  13.9 us (1%)
    psum x1, waiting for transfers between devices, per_device(): grad_b = lax.psum(token_b + value_b / groups, ('dp', 'fsdp'))  522 us
    psum x1, waiting for transfers between devices, per_device(): lax.psum(token_a + cross * coeff[:, None, :] / groups, ('dp', 'tensor'))  122 us
    psum x1, waiting for transfers between devices, per_device(): low_total = lax.psum(low_all, 'tensor')  90.7 us
    all_gather x1, waiting for transfers between devices, per_device(): gathered = lax.all_gather(tokens, 'fsdp', axis=0, tiled=True)  78.6 us
    psum x1, blocking collectives, per_device(): grad_m = lax.psum(m_local, ('dp', 'tensor')) / norm  31.5 us
    unnamed x6, waiting for transfers between devices  23.9 us
    all_gather x1, blocking collectives, per_device(): back_all = lax.all_gather(back_part, 'tensor', axis=0, tiled=True)  22.3 us
  transfers between devices with their start and end apart: 5, of which 5 were waited for; matrix products, arithmetic and copies ran while one was open for 2% of the time, Pallas kernels for 0%

commit v1 on v0

v1 whole, which is shorter than its diff:
```python
import jax
import jax.numpy as jnp
from jax import lax
from jax.sharding import Mesh, PartitionSpec as P

F32 = jnp.float32
BF16 = jnp.bfloat16
GROUP = ("dp", "tensor")


def split2(x):
    hi = x.astype(BF16)
    return hi, (x - hi.astype(F32)).astype(BF16)


def per_device(tokens, base, b, a, magnitude, cotangent):
    highest = lax.Precision.HIGHEST
    dp = lax.axis_index("dp")
    core = lax.axis_index("core")
    depth, columns = base.shape[1:]
    rank = a.shape[1]
    shards = lax.axis_size("tensor")
    zs = lax.axis_size("z")
    own = 2 * zs * tokens.shape[0] // shards
    half = own // 2
    swap = [(0, 1), (1, 0)]
    a_wide = a.astype(F32)

    g_own = lax.all_gather(tokens, "z", axis=0, tiled=True)
    g_other = lax.ppermute(g_own, "core", swap)

    combined = base.astype(F32) + jnp.einsum(
        "kdr,krf->kdf", b, a, preferred_element_type=F32
    )
    sq = jnp.sum(combined * combined, axis=1)
    cross = jnp.einsum("kdr,kdf->krf", b.astype(F32), combined, precision=highest)

    def forward(g):
        pre = jnp.einsum("td,kdf->tkf", g, base, preferred_element_type=F32)
        low = jnp.einsum("td,kdr->tkr", g, b, preferred_element_type=F32)
        return jnp.concatenate(
            [pre.reshape(-1, 2 * columns), low.reshape(-1, 2 * rank)], axis=1
        ).reshape(shards, half, 2 * (columns + rank))

    sq_row = jnp.pad(sq.reshape(1, 1, 2 * columns), ((0, 0), (0, 7), (0, 2 * rank)))
    payload = jnp.concatenate(
        [forward(g_own), forward(g_other), jnp.broadcast_to(sq_row, (shards,) + sq_row.shape[1:])],
        axis=1,
    )
    total = jnp.sum(lax.all_to_all(payload, "tensor", 0, 0), axis=0)
    base_own = total[:own, : 2 * columns].reshape(own, 2, columns)
    low = total[:own, 2 * columns :].reshape(own, 2, rank)
    norm = jnp.sqrt(total[own, : 2 * columns].reshape(2, columns) + 1e-06)

    pre = base_own + jnp.einsum("tkr,krf->tkf", low, a_wide, precision=highest)
    scale = magnitude / norm
    out = pre * scale[None]
    gate, up = out[:, 0], out[:, 1]
    sig = jax.nn.sigmoid(gate)
    cot = cotangent.reshape(2, 2, half // 2, columns)
    cot = jnp.where(core == 0, cot, cot[:, ::-1])
    grad_h = jnp.swapaxes(cot, 0, 1).reshape(own, columns).astype(F32)
    dout = jnp.stack(
        [grad_h * up * sig * (1.0 + gate * (1.0 - sig)), grad_h * gate * sig], axis=1
    )
    dpre = dout * scale[None]
    m_part = jnp.sum(dout * pre, axis=0)
    a_part = jnp.einsum("tkr,tkf->krf", low, dpre, precision=highest)
    back = jnp.einsum("tkf,krf->tkr", dpre, a_wide, precision=highest).reshape(own, 2 * rank)

    members = 2 * shards
    rows = 2 * rank // members
    tiles = columns // 128

    def tiled(x):
        return x.reshape(members, -1, tiles, 128).swapaxes(1, 2).reshape(members, -1, 128)

    def untiled(x):
        return x.reshape(x.shape[0], tiles, -1, 128).swapaxes(1, 2).reshape(x.shape[0], -1, columns)

    cross_half = lax.dynamic_index_in_dim(
        cross.reshape(members, 2, rows // 2, columns), dp, 1, keepdims=False
    )
    everyone = lambda x: jnp.broadcast_to(x[None], (members,) + x.shape)
    parts = [
        tiled(a_part),
        tiled(cross_half),
        everyone(jnp.pad(m_part.reshape(2 * tiles, 128), ((0, 4), (0, 0)))),
        everyone(back),
    ]
    cuts = [0]
    for part in parts:
        cuts.append(cuts[-1] + part.shape[1])
    got = lax.all_to_all(jnp.concatenate(parts, axis=1), GROUP, 0, 0)
    a_own = jnp.sum(untiled(got[:, cuts[0] : cuts[1]]), axis=0)
    cross_own = jnp.sum(
        untiled(got[:, cuts[1] : cuts[2]]).reshape(2, shards, rows // 2, columns), axis=1
    ).reshape(rows, columns)
    m_total = jnp.sum(got[:, cuts[2] : cuts[2] + 2 * tiles], axis=0).reshape(2, columns)
    backs = lax.dynamic_slice_in_dim(got[:, cuts[3] : cuts[4]], dp * shards, shards, 0)

    grad_m = m_total / norm
    coeff = -grad_m * magnitude / (norm * norm)

    my_k = lax.axis_index(GROUP) // (members // 2)
    a_rows = a_own + cross_own * lax.dynamic_index_in_dim(coeff, my_k, 0)
    grad_a = lax.all_to_all(everyone(a_rows), GROUP, 0, 0).reshape(2, rank, columns)

    token_b = lax.dot_general(
        backs[:, :half].reshape(-1, 2 * rank),
        g_own.astype(F32),
        (((0,), (0,)), ((), ())),
        precision=highest,
    ) + lax.dot_general(
        backs[:, half:].reshape(-1, 2 * rank),
        g_other.astype(F32),
        (((0,), (0,)), ((), ())),
        precision=highest,
    )
    token_b = token_b.reshape(2, rank, depth)
    weighted = lax.dynamic_index_in_dim(coeff[:, None] * a_wide, dp, 0, keepdims=False)
    value_b = lax.dot_general(
        weighted,
        lax.dynamic_index_in_dim(combined, dp, 0, keepdims=False),
        (((1,), (1,)), ((), ())),
        precision=highest,
    )
    mine = lax.dynamic_index_in_dim(token_b, core, 0, keepdims=False)
    theirs = lax.dynamic_index_in_dim(token_b, 1 - core, 0, keepdims=False)
    mine = jnp.where(core == dp, mine + value_b, mine)
    theirs = jnp.where(core == dp, theirs, theirs + value_b)
    part_b = mine + lax.ppermute(theirs, "core", swap)
    chunks = part_b.reshape(zs, -1, 128)
    piece = jnp.sum(lax.all_to_all(chunks, "z", 0, 0), axis=0)
    piece = piece + lax.ppermute(piece, "dp", swap)
    full = lax.all_to_all(jnp.broadcast_to(piece[None], chunks.shape), "z", 0, 0)
    full = full.reshape(rank, depth)
    other = lax.ppermute(full, "core", swap)
    grad_b = jnp.where(core == 0, jnp.stack([full, other]), jnp.stack([other, full]))
    return grad_a, jnp.swapaxes(grad_b, 1, 2), grad_m


def solution(mesh):
    sizes = mesh.shape
    fine = Mesh(
        mesh.devices.reshape(sizes["dp"], sizes["fsdp"] // 2, 2, sizes["tensor"]),
        ("dp", "z", "core", "tensor"),
    )
    fsdp = ("z", "core")
    return jax.shard_map(
        per_device,
        mesh=fine,
        in_specs=(
            P(("dp",) + fsdp, "tensor"),
            P(None, "tensor", fsdp),
            P(None, "tensor", None),
            P(None, None, fsdp),
            P(None, fsdp),
            P(GROUP, fsdp),
        ),
        out_specs=(P(None, None, fsdp), P(None, "tensor", None), P(None, fsdp)),
        check_vma=False,
    )
```

time: 961 us -> 250 us (0.26)
  the two profiles are of different devices: /device:TPU:1 before, /device:TPU:32 now
where the time goes in v1:
time: 250 us; the launch traced here: 249 us
  waiting for transfers between devices  90.7 us (36%)
  blocking collectives  66 us (26%)
  starting transfers between devices  41.7 us (17%)
  matrix products  26.7 us (11%)
  local copies, waits for them, and re-layouts  14.2 us (6%)
  other arithmetic  8.93 us (4%)
    all_to_all x1, waiting for transfers between devices, per_device(): total = jnp.sum(lax.all_to_all(payload, 'tensor', 0, 0), axis=0)  40.7 us
    all_gather x1, blocking collectives, per_device(): g_own = lax.all_gather(tokens, 'z', axis=0, tiled=True)  38.9 us
    all_to_all x1, blocking collectives, per_device(): piece = jnp.sum(lax.all_to_all(chunks, 'z', 0, 0), axis=0)  27 us
    all_to_all x1, waiting for transfers between devices, per_device(): got = lax.all_to_all(jnp.concatenate(parts, axis=1), GROUP, 0, 0)  19.4 us
    all_to_all x1, starting transfers between devices, per_device(): got = lax.all_to_all(jnp.concatenate(parts, axis=1), GROUP, 0, 0)  17.9 us
    all_to_all x1, waiting for transfers between devices, per_device(): lax.all_to_all(jnp.broadcast_to(piece[None], chunks.shape), 'z', 0, 0)  17.3 us
    all_to_all x1, waiting for transfers between devices, per_device(): lax.all_to_all(everyone(a_rows), GROUP, 0, 0).reshape(2, rank, columns)  7.37 us
    all_to_all x1, starting transfers between devices, per_device(): lax.all_to_all(jnp.broadcast_to(piece[None], chunks.shape), 'z', 0, 0)  6.1 us
  transfers between devices with their start and end apart: 8, of which 6 were waited for; matrix products, arithmetic and copies ran while one was open for 9% of the time, Pallas kernels for 0%

profile of v1, /device:TPU:32, one launch (start us, length us, event | category | flops | bytes accessed | tf_op | source)
XLA Modules:
  0.0 249.3 jit_solution(15751386816034121850)
XLA Ops:
  0.6 38.9 %all_gather.3 = bf16[256,1024]{1,0:T(8,128)(2,1)} all-gather(bf16[16,1024]{1,0:T(8,128)(2,1)} %param.6), channel_id=1, replica_groups=mesh['dp'=2,'z'=16,'core'=2,'tensor'=8] {'z'}, dimensions={0}, use_global_device_ids=true | all-gather | bytes 557056 | tf_op jit(solution)/shard_map/all_gather | solution.py:29
  39.6 2.2 collective-permute-start
  41.8 5.8 %multiply_reduce_fusion = (f32[2,768]{1,0:T(2,128)S(1)}, f32[2,1024,768]{2,1,0:T(8,128)}) fusion(bf16[2,1024,64]{1,2,0:T(8,128)(2,1)S(1)} %copy-done, bf16[2,64,768]{2,1,0:T(8,128)(2,1)} %param.9, bf16[2,1024,768]{2,1,0:T(8,128)(2,1)} %param.7), kind=kOutput, calls=%fused_computation | convolution fusion | flops 207616512 | bytes 9902080 | tf_op jit(solution)/shard_map/kdr,krf->kdf/dot_general | solution.py:32
  47.5 2.0 fusion.7
  49.6 2.4 copy.41
  52.0 3.3 %concatenate.22 = f32[8,32,1536]{2,1,0:T(8,128)} reshape(f32[256,2,768]{2,1,0:T(2,128)} %copy.41) | data formatting | bytes 3145728 | tf_op jit(solution)/shard_map/concatenate | solution.py:41
  55.3 0.6 pad_bitcast_fusion
  56.0 1.3 fusion.28
  57.3 2.0 fusion.5
  59.4 1.2 copy.43
  60.6 2.4 concatenate.25
  63.0 1.3 fusion.29
  64.3 0.8 broadcast_in_dim.15
  65.2 3.6 %pad_maximum_fusion = f32[8,72,1664]{2,1,0:T(8,128)} fusion(f32[8,8,1664]{2,1,0:T(8,128)S(1)} %broadcast_in_dim.15, f32[8,32,128]{2,1,0:T(8,128)S(1)} %bitcast.112, f32[8,32,1536]{2,1,0:T(8,128)} %concatenate.25, f32[8,32,128]{2,1,0:T(8,128)S(1)} %bitcast.111, f32[8,32,1536]{2,1,0:T(8,128)S(1)} %copy-done.2), kind=kLoop, calls=%fused_computation.2 | loop fusion | flops 3833856 | bytes 7667712 | tf_op jit(solution)/shard_map/concatenate | solution.py:46
  68.8 5.4 %all-to-all-start = ((f32[8,72,1664]{2,1,0:T(8,128)}), f32[8,72,1664]{2,1,0:T(8,128)}, u32[]{:S(2)}, u32[]{:S(2)}) async-start(f32[8,72,1664]{2,1,0:T(8,128)} %pad_maximum_fusion), calls=%async_computation | async-start | bytes 7667712 | tf_op jit(solution)/shard_map/all_to_all | solution.py:50
  74.2 5.1 %convolution_bitcast_fusion = f32[2,64,768]{2,1,0:T(8,128)S(1)} fusion(f32[2,1024,768]{2,1,0:T(8,128)} %get-tuple-element.12, bf16[2,1024,64]{1,2,0:T(8,128)(2,1)S(1)} %copy-done), kind=kOutput, calls=%fused_computation.8 | convolution fusion | flops 1207959552 | bytes 6946816 | tf_op jit(solution)/shard_map/kdr,kdf->krf/dot_general | solution.py:36
  79.4 0.1 reshape.137
  79.8 40.7 %all-to-all-done = f32[8,72,1664]{2,1,0:T(8,128)} async-done(((f32[8,72,1664]{2,1,0:T(8,128)}), f32[8,72,1664]{2,1,0:T(8,128)}, u32[]{:S(2)}, u32[]{:S(2)}) %all-to-all-start) | async-done | bytes 3833888 | tf_op jit(solution)/shard_map/all_to_all | solution.py:50
  120.5 2.3 reduce_sum.70
  122.9 0.1 copy.60
  123.1 0.4 broadcast_multiply_fusion
  123.5 0.1 fusion.14
  123.6 0.5 fusion.10
  124.0 0.3 convolution_bitcast_fusion.2
  124.4 0.1 multiply_reduce_fusion.1
  124.5 0.1 broadcast_in_dim.17
  124.7 1.1 pad_maximum_fusion.1
  125.8 17.9 %all-to-all-start.1 = ((f32[16,152,128]{2,1,0:T(8,128)}), f32[16,152,128]{2,1,0:T(8,128)S(1)}, u32[]{:S(2)}, u32[]{:S(2)}) async-start(f32[16,152,128]{2,1,0:T(8,128)} %pad_maximum_fusion.1), calls=%async_computation.1 | async-start | bytes 2490368 | tf_op jit(solution)/shard_map/all_to_all | solution.py:94
  143.8 19.4 %all-to-all-done.1 = f32[16,152,128]{2,1,0:T(8,128)S(1)} async-done(((f32[16,152,128]{2,1,0:T(8,128)}), f32[16,152,128]{2,1,0:T(8,128)S(1)}, u32[]{:S(2)}, u32[]{:S(2)}) %all-to-all-start.1) | async-done | bytes 1245216 | tf_op jit(solution)/shard_map/all_to_all | solution.py:94
  163.3 1.5 fusion.30
  164.8 0.6 multiply_divide_fusion
  165.4 1.5 convolution_add_fusion
  166.9 5.0 %add_select_fusion = (f32[64,1024]{1,0:T(8,128)S(1)}, f32[64,1024]{1,0:T(8,128)S(1)}) fusion(f32[2,64,1024]{2,1,0:T(8,128)S(1)} %bitcast.97, s32[]{:T(128)S(6)} %select_n.65, pred[]{:T(512)S(6)} %eq.9, f32[2,1024,768]{2,1,0:T(8,128)} %get-tuple-element.12, s32[]{:T(128)S(6)} %select_n.57, f32[1,768]{1,0:T(1,128)S(1)} %get-tuple-element.9, ...), kind=kOutput, calls=%fused_computation.20 | convolution fusion | flops 604209152 | bytes 4035584 | tf_op jit(solution)/shard_map/dot_general | solution.py:122
  171.9 1.9 collective-permute-start.1
  173.8 1.5 collective-permute-done.1
  175.4 27.0 %all_to_all.25 = f32[16,32,128]{2,1,0:T(8,128)S(1)} all-to-all(f32[16,32,128]{2,1,0:T(8,128)S(1)} %reshape.148), channel_id=1, replica_groups=mesh['dp'=2,'z'=16,'core'=2,'tensor'=8] {'z'}, dimensions={0} | all-to-all | bytes 524288 | tf_op jit(solution)/shard_map/all_to_all | solution.py:134
  202.4 2.8 %collective-permute-start.2 = (f32[32,128]{1,0:T(8,128)S(1)}, f32[32,128]{1,0:T(8,128)S(1)}, u32[]{:S(2)}, u32[]{:S(2)}) collective-permute-start(f32[32,128]{1,0:T(8,128)S(1)} %reduce_sum.78), channel_id=1, source_target_pairs={{0,256},{256,0},{1,257},{257,1},{2,258},{258,2},{3,259},{259,3},{4... | collective-permute-start | bytes 49160 | tf_op jit(solution)/shard_map/ppermute | solution.py:135
  205.2 4.4 %collective-permute-done.2 = f32[32,128]{1,0:T(8,128)S(1)} collective-permute-done((f32[32,128]{1,0:T(8,128)S(1)}, f32[32,128]{1,0:T(8,128)S(1)}, u32[]{:S(2)}, u32[]{:S(2)}) %collective-permute-start.2) | collective-permute-done | bytes 16416 | tf_op jit(solution)/shard_map/ppermute | solution.py:135
  209.6 0.7 broadcast_in_dim.20
  210.3 6.1 %all-to-all-start.4 = ((f32[16,32,128]{2,1,0:T(8,128)}), f32[16,32,128]{2,1,0:T(8,128)S(1)}, u32[]{:S(2)}, u32[]{:S(2)}) async-start(f32[16,32,128]{2,1,0:T(8,128)} %broadcast_in_dim.20), calls=%async_computation.4 | async-start | bytes 524288 | tf_op jit(solution)/shard_map/all_to_all | solution.py:136
  216.5 0.1 reduce_sum.76
  216.7 17.3 %all-to-all-done.4 = f32[16,32,128]{2,1,0:T(8,128)S(1)} async-done(((f32[16,32,128]{2,1,0:T(8,128)}), f32[16,32,128]{2,1,0:T(8,128)S(1)}, u32[]{:S(2)}, u32[]{:S(2)}) %all-to-all-start.4) | async-done | bytes 262176 | tf_op jit(solution)/shard_map/all_to_all | solution.py:136
  234.0 0.8 broadcast_in_dim.19
  234.8 3.6 %all-to-all-start.2 = ((f32[16,8,768]{2,1,0:T(8,128)}), f32[16,8,768]{2,1,0:T(8,128)S(1)}, u32[]{:S(2)}, u32[]{:S(2)}) async-start(f32[16,8,768]{2,1,0:T(8,128)} %broadcast_in_dim.19), calls=%async_computation.2 | async-start | bytes 786432 | tf_op jit(solution)/shard_map/all_to_all | solution.py:107
  238.4 1.9 collective-permute-start.3
  240.3 7.4 %all-to-all-done.2 = f32[16,8,768]{2,1,0:T(8,128)S(1)} async-done(((f32[16,8,768]{2,1,0:T(8,128)}), f32[16,8,768]{2,1,0:T(8,128)S(1)}, u32[]{:S(2)}, u32[]{:S(2)}) %all-to-all-start.2) | async-done | bytes 393248 | tf_op jit(solution)/shard_map/all_to_all | solution.py:107
  247.8 0.8 fusion.4
  248.6 0.7 copy.66
  (50 shorter events, 1.0 us)
Async XLA Ops:
  0.6 41.1 %copy-start = (bf16[2,1024,64]{1,2,0:T(8,128)(2,1)S(1)}, bf16[2,1024,64]{1,2,0:T(8,128)(2,1)}, u32[]{:S(2)}) copy-start(bf16[2,1024,64]{1,2,0:T(8,128)(2,1)} %param.8) | copy-start | bytes 786436
  39.6 7.9 %copy-start.1 = (bf16[2,1024,768]{2,1,0:T(8,128)(2,1)S(1)}, bf16[2,1024,768]{2,1,0:T(8,128)(2,1)}, u32[]{:S(2)}) copy-start(bf16[2,1024,768]{2,1,0:T(8,128)(2,1)} %param.7) | copy-start | bytes 9437188
  39.6 17.7 %collective-permute-start = (bf16[256,1024]{1,0:T(8,128)(2,1)}, bf16[256,1024]{1,0:T(8,128)(2,1)}, u32[]{:S(2)}, u32[]{:S(2)}) collective-permute-start(bf16[256,1024]{1,0:T(8,128)(2,1)} %all_gather.3), channel_id=1, source_target_pairs={{0,8},{8,0},{1,9},{9,1},{2,10},{10,2},{3,11},{11,3},{4,12},{12,4},... | collective-permute-start | bytes 1572872 | tf_op jit(solution)/shard_map/ppermute | solution.py:30
  59.3 5.8 %copy-start.2 = (f32[8,32,1536]{2,1,0:T(8,128)S(1)}, f32[8,32,1536]{2,1,0:T(8,128)}, u32[]{:S(2)}) copy-start(f32[8,32,1536]{2,1,0:T(8,128)} %concatenate.22) | copy-start | bytes 4718596
  68.8 5.5 %copy-start.4 = (bf16[64,768]{1,0:T(8,128)(2,1)S(1)}, bf16[64,768]{1,0:T(8,128)(2,1)}, u32[]{:S(2)}) copy-start(bf16[64,768]{1,0:T(8,128)(2,1)} %param.11) | copy-start | bytes 294916
  68.8 51.8 %all-to-all-start = ((f32[8,72,1664]{2,1,0:T(8,128)}), f32[8,72,1664]{2,1,0:T(8,128)}, u32[]{:S(2)}, u32[]{:S(2)}) async-start(f32[8,72,1664]{2,1,0:T(8,128)} %pad_maximum_fusion), calls=%async_computation | async-start | bytes 7667712 | tf_op jit(solution)/shard_map/all_to_all | solution.py:50
  79.6 43.4 %copy-start.5 = (f32[2,768]{1,0:T(2,128)S(1)}, f32[2,768]{1,0:T(2,128)}, u32[]{:S(2)}) copy-start(f32[2,768]{1,0:T(2,128)} %param.10) | copy-start | bytes 18436
  79.6 43.4 %copy-start.3 = (bf16[2,64,768]{2,1,0:T(8,128)(2,1)S(1)}, bf16[2,64,768]{2,1,0:T(8,128)(2,1)}, u32[]{:S(2)}) copy-start(bf16[2,64,768]{2,1,0:T(8,128)(2,1)} %param.9) | copy-start | bytes 589828
  125.8 37.3 %all-to-all-start.1 = ((f32[16,152,128]{2,1,0:T(8,128)}), f32[16,152,128]{2,1,0:T(8,128)S(1)}, u32[]{:S(2)}, u32[]{:S(2)}) async-start(f32[16,152,128]{2,1,0:T(8,128)} %pad_maximum_fusion.1), calls=%async_computation.1 | async-start | bytes 2490368 | tf_op jit(solution)/shard_map/all_to_all | solution.py:94
  171.9 3.4 %collective-permute-start.1 = (f32[64,1024]{1,0:T(8,128)S(1)}, f32[64,1024]{1,0:T(8,128)S(1)}, u32[]{:S(2)}, u32[]{:S(2)}) collective-permute-start(f32[64,1024]{1,0:T(8,128)S(1)} %get-tuple-element.15), channel_id=1, source_target_pairs={{0,8},{8,0},{1,9},{9,1},{2,10},{10,2},{3,11},{11,3},{4,12},{12,4},... | collective-permute-start | bytes 786440 | tf_op jit(solution)/shard_map/ppermute | solution.py:132
  202.4 7.1 %collective-permute-start.2 = (f32[32,128]{1,0:T(8,128)S(1)}, f32[32,128]{1,0:T(8,128)S(1)}, u32[]{:S(2)}, u32[]{:S(2)}) collective-permute-start(f32[32,128]{1,0:T(8,128)S(1)} %reduce_sum.78), channel_id=1, source_target_pairs={{0,256},{256,0},{1,257},{257,1},{2,258},{258,2},{3,259},{259,3},{4... | collective-permute-start | bytes 49160 | tf_op jit(solution)/shard_map/ppermute | solution.py:135
  210.3 23.7 %all-to-all-start.4 = ((f32[16,32,128]{2,1,0:T(8,128)}), f32[16,32,128]{2,1,0:T(8,128)S(1)}, u32[]{:S(2)}, u32[]{:S(2)}) async-start(f32[16,32,128]{2,1,0:T(8,128)} %broadcast_in_dim.20), calls=%async_computation.4 | async-start | bytes 524288 | tf_op jit(solution)/shard_map/all_to_all | solution.py:136
  234.8 12.9 %all-to-all-start.2 = ((f32[16,8,768]{2,1,0:T(8,128)}), f32[16,8,768]{2,1,0:T(8,128)S(1)}, u32[]{:S(2)}, u32[]{:S(2)}) async-start(f32[16,8,768]{2,1,0:T(8,128)} %broadcast_in_dim.19), calls=%async_computation.2 | async-start | bytes 786432 | tf_op jit(solution)/shard_map/all_to_all | solution.py:107
  238.4 9.4 %collective-permute-start.3 = (f32[64,1024]{1,0:T(8,128)S(1)}, f32[64,1024]{1,0:T(8,128)S(1)}, u32[]{:S(2)}, u32[]{:S(2)}) collective-permute-start(f32[64,1024]{1,0:T(8,128)S(1)} %reshape.149), channel_id=1, source_target_pairs={{0,8},{8,0},{1,9},{9,1},{2,10},{10,2},{3,11},{11,3},{4,12},{12,4},... | collective-permute-start | bytes 786440 | tf_op jit(solution)/shard_map/ppermute | solution.py:138

commit v2 on v0

v2 whole, which is shorter than its diff:
```python
import functools
import math

import jax
import jax.numpy as jnp
from jax import lax
from jax.experimental import pallas as pl
from jax.experimental.pallas import tpu as pltpu
from jax.sharding import Mesh, PartitionSpec as P

F32 = jnp.float32
BF16 = jnp.bfloat16
GROUP = ("dp", "tensor")
PARAMS = pltpu.CompilerParams(vmem_limit_bytes=48 * 2**20)
VMEM = pl.BlockSpec(memory_space=pltpu.VMEM)
SMEM = pl.BlockSpec(memory_space=pltpu.SMEM)

BEND = 4096.0
POWER = 250.0 / math.log2(1.0 + BEND)
SHIFT = 125.0 * math.log(2.0)


def encode(x, peak):
    size = jnp.exp(POWER * jnp.log(1.0 + jnp.abs(x) * (BEND / peak)) - SHIFT)
    return jnp.where(x < 0, -size, size).astype(BF16)


def decode(code, peak):
    code = code.astype(F32)
    size = (jnp.exp((jnp.log(jnp.abs(code)) + SHIFT) * (1.0 / POWER)) - 1.0) * (peak / BEND)
    return jnp.where(code < 0, -size, size)


def peak_of(x):
    peak = jnp.max(jnp.max(jnp.abs(x), axis=1, keepdims=True), axis=0, keepdims=True)
    return (jnp.maximum(peak, 1e-20) * 1.01).astype(BF16).astype(F32)


def split(x):
    hi = x.astype(BF16)
    return hi, (x - hi.astype(F32)).astype(BF16)


def dot(x, y, dims=((1,), (0,))):
    return lax.dot_general(x, y, (dims, ((), ())), preferred_element_type=F32)


NT = ((1,), (1,))
TN = ((0,), (0,))


def weights_kernel(base_ref, bt_ref, a_ref, cross_ref, extra_ref):
    depth, columns = base_ref.shape[1:]
    rank = a_ref.shape[1]
    tiles = columns // 128
    step = 256
    extra_ref[...] = jnp.zeros_like(extra_ref)
    for k in range(2):
        sq = jnp.zeros((1, columns), F32)
        cross = jnp.zeros((rank, columns), F32)
        for at in range(0, depth, step):
            rows = slice(at, at + step)
            bt = bt_ref[k, :, rows]
            combined = base_ref[k, rows, :].astype(F32) + dot(bt, a_ref[k], TN)
            sq += jnp.sum(combined * combined, axis=0, keepdims=True)
            hi, lo = split(combined)
            cross += dot(bt, hi) + dot(bt, lo)
        cross_ref[k * rank : (k + 1) * rank, :] = cross
        for piece in range(3):
            part = sq.astype(BF16).astype(F32)
            sq = sq - part
            for i in range(tiles):
                row = 2 * tiles * piece + tiles * k + i
                extra_ref[row : row + 1, :] = part[:, 128 * i : 128 * (i + 1)]


def forward_kernel(own_ref, other_ref, base_ref, bt_ref, extra_ref, out_ref):
    shards, owned, _ = out_ref.shape
    columns = base_ref.shape[2]
    half = owned // 2
    rank = bt_ref.shape[0]
    peaks = jnp.zeros((16, 128), F32)
    line = lax.broadcasted_iota(jnp.int32, (16, 128), 0)
    row = 0
    for side, ref in enumerate((own_ref, other_ref)):
        where = slice(side * half, (side + 1) * half)
        for k in range(3):
            if k < 2:
                value = dot(ref[...], base_ref[k])
                lanes = slice(k * columns, (k + 1) * columns)
            else:
                value = dot(ref[...], bt_ref[...], NT)
                lanes = slice(2 * columns, 2 * columns + rank)
            peak = peak_of(value)
            out_ref[:, where, lanes] = encode(value, peak).reshape(shards, half, value.shape[1])
            peaks = jnp.where(line == row, peak, peaks)
            row += 1
    tail = jnp.concatenate([extra_ref[...], peaks], axis=0).astype(BF16)
    out_ref[:, :, 2 * columns + rank :] = jnp.broadcast_to(tail[None], (shards,) + tail.shape)


def local_kernel(place_ref, got_ref, cot_ref, a_ref, mag_ref, cross_ref, out_ref, norm_ref):
    dp, core = place_ref[0], place_ref[1]
    shards, owned, _ = got_ref.shape
    rank, columns = a_ref.shape[1:]
    tiles = columns // 128
    half = owned // 2
    tail = 2 * columns + 2 * rank
    peak_rows = 3 * 2 * tiles + 12

    totals = []
    for k in range(3):
        lanes = slice(k * columns, (k + 1) * columns) if k < 2 else slice(2 * columns, tail)
        sides = []
        for side in range(2):
            total = None
            for source in range(shards):
                peaks = got_ref[source, peak_rows : peak_rows + 16, tail:].astype(F32)
                at = 3 * side + k
                value = decode(
                    got_ref[source, side * half : (side + 1) * half, lanes],
                    peaks[at : at + 1, 0:1],
                )
                total = value if total is None else total + value
            sides.append(total)
        totals.append(jnp.concatenate(sides, axis=0))
    extra = got_ref[0, :48, tail:].astype(F32)
    for source in range(1, shards):
        extra += got_ref[source, :48, tail:].astype(F32)
    pieces = extra[24:36] + extra[12:24] + extra[0:12]

    low = totals[2]
    low_hi, low_lo = split(low)
    outs, pres, scales = [], [], []
    for k in range(2):
        sq = jnp.concatenate(
            [pieces[tiles * k + i : tiles * k + i + 1] for i in range(tiles)], axis=1
        )
        norm = jnp.sqrt(sq + 1e-06)
        norm_ref[k : k + 1, :] = norm
        mine = slice(k * rank, (k + 1) * rank)
        pre = totals[k] + (dot(low_hi[:, mine], a_ref[k]) + dot(low_lo[:, mine], a_ref[k]))
        scale = mag_ref[k : k + 1, :] / norm
        pres.append(pre)
        scales.append(scale)
        outs.append(pre * scale)
    gate, up = outs
    quarter = half // 2
    cot = jnp.concatenate(
        [
            cot_ref[pl.ds(pl.multiple_of(start + side * quarter, quarter), quarter), :]
            for side in (core, 1 - core)
            for start in (0, half)
        ],
        axis=0,
    ).astype(F32)
    sig = 1.0 / (1.0 + jnp.exp(-gate))
    douts = (cot * up * sig * (1.0 + gate * (1.0 - sig)), cot * gate * sig)
    members = out_ref.shape[0]
    rows = 2 * rank // members
    at_cross = tiles * rows
    at_m = at_cross + tiles * rows // 2
    at_back = at_m + 16
    out_ref[:, at_m:at_back, :] = jnp.zeros((members, at_back - at_m, 128), F32)
    backs = []
    for k in range(2):
        mine = slice(k * rank, (k + 1) * rank)
        m = jnp.sum(douts[k] * pres[k], axis=0, keepdims=True)
        dpre = douts[k] * scales[k]
        hi, lo = split(dpre)
        grad_a = (
            dot(low_hi[:, mine], hi, TN) + dot(low_hi[:, mine], lo, TN) + dot(low_lo[:, mine], hi, TN)
        )
        backs.append(dot(hi, a_ref[k], NT) + dot(lo, a_ref[k], NT))
        for i in range(tiles):
            lanes = slice(128 * i, 128 * (i + 1))
            row = at_m + tiles * k + i
            out_ref[:, row : row + 1, :] = jnp.broadcast_to(m[None, :, lanes], (members, 1, 128))
            for j in range(members // 2):
                out_ref[k * members // 2 + j, rows * i : rows * (i + 1), :] = grad_a[
                    rows * j : rows * (j + 1), lanes
                ]
    for i in range(tiles // 2):
        lanes = pl.ds(pl.multiple_of((dp * (tiles // 2) + i) * 128, 128), 128)
        out_ref[:, at_cross + rows * i : at_cross + rows * (i + 1), :] = cross_ref[:, lanes].reshape(
            members, rows, 128
        )
    back = jnp.concatenate(backs, axis=1)
    out_ref[:, at_back:, :] = jnp.broadcast_to(back[None], (members,) + back.shape)


def coefficient_kernel(place_ref, got_ref, norm_ref, mag_ref, rows_ref, grad_m_ref, coeff_ref):
    members, rows, columns = rows_ref.shape
    tiles = columns // 128
    at_cross = tiles * rows
    at_m = at_cross + tiles * rows // 2
    m = jnp.sum(got_ref[:, at_m : at_m + 16, :], axis=0)
    for k in range(2):
        norm = norm_ref[k : k + 1, :]
        m_row = jnp.concatenate([m[tiles * k + i : tiles * k + i + 1] for i in range(tiles)], axis=1)
        grad_m = m_row / norm
        grad_m_ref[k : k + 1, :] = grad_m
        coeff_ref[k : k + 1, :] = -grad_m * mag_ref[k : k + 1, :] / (norm * norm)
    coeff = jnp.where(place_ref[0] == 0, coeff_ref[0:1, :], coeff_ref[1:2, :])
    for i in range(tiles):
        lanes = slice(128 * i, 128 * (i + 1))
        token = jnp.sum(got_ref[:, rows * i : rows * (i + 1), :], axis=0)
        source, tile = divmod(i, tiles // 2)
        at = at_cross + rows * tile
        sources = slice(source * members // 2, (source + 1) * members // 2)
        cross = jnp.sum(got_ref[sources, at : at + rows, :], axis=0)
        own = token + cross * coeff[:, lanes]
        rows_ref[:, :, lanes] = jnp.broadcast_to(own[None], (members, rows, 128))


def width_kernel(
    place_ref, got_ref, coeff_ref, own_ref, other_ref, base_ref, bt_ref, a_ref, mine_ref, theirs_ref, sum_ref
):
    dp, core = place_ref[0], place_ref[1]
    members = got_ref.shape[0]
    shards = members // 2
    rank = a_ref.shape[1]
    owned = 2 * own_ref.shape[0] // shards
    half = owned // 2
    at_back = got_ref.shape[1] - owned
    total = None
    for side, ref in enumerate((own_ref, other_ref)):
        rows = pl.ds(at_back + side * half, half)
        back = got_ref[pl.ds(dp * shards, shards), rows, :].reshape(shards * half, 2 * rank)
        hi, lo = split(back)
        both = dot(jnp.concatenate([hi, lo], axis=1), ref[...], TN)
        part = both[: 2 * rank] + both[2 * rank :]
        total = part if total is None else total + part
    sum_ref[...] = total
    a = a_ref[dp]
    hi, lo = split(a.astype(F32) * coeff_ref[pl.ds(dp, 1), :])
    weighted = jnp.concatenate([hi, lo], axis=0)
    both = dot(weighted, base_ref[dp], NT)
    small = dot(weighted, a, NT)
    small_hi, small_lo = split(small[:rank] + small[rank:])
    value = (both[:rank] + both[rank:]) + (dot(small_hi, bt_ref[dp]) + dot(small_lo, bt_ref[dp]))
    mine = pl.ds(pl.multiple_of(dp * rank, rank), rank)
    sum_ref[mine, :] += value
    width = mine_ref.shape[1]
    mine_ref[...] = sum_ref[:, pl.ds(pl.multiple_of(core * width, width), width)]
    theirs_ref[...] = sum_ref[:, pl.ds(pl.multiple_of((1 - core) * width, width), width)]


def call(kernel, outs, in_specs, flops=0, size=0, scratch=()):
    return pl.pallas_call(
        kernel,
        out_shape=outs,
        in_specs=in_specs,
        out_specs=[VMEM] * len(outs) if isinstance(outs, (list, tuple)) else VMEM,
        scratch_shapes=scratch,
        compiler_params=PARAMS,
        cost_estimate=pl.CostEstimate(flops=flops, bytes_accessed=size, transcendentals=0),
    )


def shape(dims, dtype=F32):
    return jax.ShapeDtypeStruct(dims, dtype)


def per_device(tokens, base, b, a, magnitude, cotangent):
    dp = lax.axis_index("dp")
    core = lax.axis_index("core")
    member = lax.axis_index(GROUP)
    depth, columns = base.shape[1:]
    rank = a.shape[1]
    shards = lax.axis_size("tensor")
    members = 2 * shards
    zs = lax.axis_size("z")
    own = 2 * zs * tokens.shape[0] // shards
    rows = 2 * rank // members
    tiles = columns // 128
    swap = [(0, 1), (1, 0)]
    bt = jnp.swapaxes(b, 1, 2)
    place = jnp.stack([dp, core]).astype(jnp.int32)
    my_k = jnp.reshape(member // shards, (1,)).astype(jnp.int32)

    g_own = lax.all_gather(tokens, "z", axis=0, tiled=True)
    g_other = lax.ppermute(g_own, "core", swap)
    cross, extra = call(
        weights_kernel,
        [shape((2 * rank, columns)), shape((48, 128))],
        [VMEM] * 3,
        flops=2 * 2 * depth * columns * rank * 3,
        size=4 * 2**20,
    )(base, bt, a)
    payload = call(
        forward_kernel,
        shape((shards, own, 2 * columns + 4 * rank), BF16),
        [VMEM] * 5,
        flops=2 * shards * own * depth * 2 * (columns + rank),
        size=8 * 2**20,
    )(g_own, g_other, base, bt.reshape(2 * rank, depth), extra)
    got = lax.all_to_all(payload, "tensor", 0, 0)

    height = tiles * rows + tiles * rows // 2 + 16 + own
    sends, norm = call(
        local_kernel,
        [shape((members, height, 128)), shape((2, columns))],
        [SMEM] + [VMEM] * 5,
        flops=2**27,
        size=4 * 2**20,
    )(place, got, cotangent, a, magnitude, cross)
    got = lax.all_to_all(sends, GROUP, 0, 0)

    a_rows, grad_m, coeff = call(
        coefficient_kernel,
        [shape((members, rows, columns)), shape((2, columns)), shape((2, columns))],
        [SMEM] + [VMEM] * 3,
        size=2 * 2**20,
    )(my_k, got, norm, magnitude)
    grad_a = lax.all_to_all(a_rows, GROUP, 0, 0).reshape(2, rank, columns)
    mine, theirs = call(
        width_kernel,
        [shape((2 * rank, depth // 2))] * 2,
        [SMEM] + [VMEM] * 7,
        flops=2**30,
        size=8 * 2**20,
        scratch=[pltpu.VMEM((2 * rank, depth), F32)],
    )(place, got, coeff, g_own, g_other, base, bt, a)

    part = mine + lax.ppermute(theirs, "core", swap)
    chunks = part.reshape(zs, 2 * rank // zs, depth // 2)
    piece = jnp.sum(lax.all_to_all(chunks, "z", 0, 0), axis=0)
    piece = piece + lax.ppermute(piece, "dp", swap)
    full = lax.all_to_all(jnp.broadcast_to(piece[None], chunks.shape), "z", 0, 0)
    full = full.reshape(2 * rank, depth // 2)
    other = lax.ppermute(full, "core", swap)
    grad_b = jnp.where(
        core == 0, jnp.concatenate([full, other], axis=1), jnp.concatenate([other, full], axis=1)
    )
    return grad_a, jnp.swapaxes(grad_b.reshape(2, rank, depth), 1, 2), grad_m


def solution(mesh):
    sizes = mesh.shape
    fine = Mesh(
        mesh.devices.reshape(sizes["dp"], sizes["fsdp"] // 2, 2, sizes["tensor"]),
        ("dp", "z", "core", "tensor"),
    )
    fsdp = ("z", "core")
    return jax.shard_map(
        per_device,
        mesh=fine,
        in_specs=(
            P(("dp",) + fsdp, "tensor"),
            P(None, "tensor", fsdp),
            P(None, "tensor", None),
            P(None, None, fsdp),
            P(None, fsdp),
            P(GROUP, fsdp),
        ),
        out_specs=(P(None, None, fsdp), P(None, "tensor", None), P(None, fsdp)),
        check_vma=False,
    )
```

time: 961 us -> 197 us (0.20)
  the two profiles are of different devices: /device:TPU:1 before, /device:TPU:32 now
where the time goes in v2:
time: 197 us; the launch traced here: 196 us
  blocking collectives  86.9 us (44%)
  waiting for transfers between devices  57.4 us (29%)
  starting transfers between devices  26.2 us (13%)
  Pallas kernels  16.2 us (8%)
  local copies, waits for them, and re-layouts  7.71 us (4%)
    all_gather x1, blocking collectives, per_device(): g_own = lax.all_gather(tokens, 'z', axis=0, tiled=True)  36.3 us
    all_to_all x1, blocking collectives, per_device(): piece = jnp.sum(lax.all_to_all(chunks, 'z', 0, 0), axis=0)  27.1 us
    all_to_all x1, waiting for transfers between devices, per_device(): got = lax.all_to_all(payload, 'tensor', 0, 0)  24.7 us
    all_to_all x1, blocking collectives, per_device(): lax.all_to_all(jnp.broadcast_to(piece[None], chunks.shape), 'z', 0, 0)  23.5 us
    all_to_all x1, waiting for transfers between devices, per_device(): got = lax.all_to_all(sends, GROUP, 0, 0)  19.4 us
    all_to_all x1, starting transfers between devices, per_device(): got = lax.all_to_all(sends, GROUP, 0, 0)  8.65 us
    unnamed x19, local copies, waits for them, and re-layouts  7.69 us
    all_to_all x1, waiting for transfers between devices, per_device(): grad_a = lax.all_to_all(a_rows, GROUP, 0, 0).reshape(2, rank, columns)  7.42 us
  transfers between devices with their start and end apart: 7, of which 5 were waited for; matrix products, arithmetic and copies ran while one was open for 0% of the time, Pallas kernels for 2%

profile of v2, /device:TPU:32, one launch (start us, length us, event | category | flops | bytes accessed | tf_op | source)
XLA Modules:
  0.0 196.2 jit_solution(1307674516541731312)
XLA Ops:
  0.6 36.3 %all_gather.3.own_ref = bf16[256,1024]{1,0:T(8,128)(2,1)S(1)} all-gather(bf16[16,1024]{1,0:T(8,128)(2,1)} %param.6), channel_id=1, replica_groups=mesh['dp'=2,'z'=16,'core'=2,'tensor'=8] {'z'}, dimensions={0}, use_global_device_ids=true | all-gather | bytes 557056 | tf_op jit(solution)/shard_map/all_gather | solution.py:282
  36.9 1.9 collective-permute-start
  38.8 0.0 copy-start
  38.8 1.9 copy-done
  40.7 0.0 copy-start.2
  40.7 0.9 copy-done.2
  41.7 0.0 copy-start.5
  41.7 0.9 copy-done.5
  42.6 3.2 %shard_map.85 = (f32[128,768]{1,0:T(8,128)S(1)}, f32[48,128]{1,0:T(8,128)S(1)}) custom-call(bf16[2,1024,768]{2,1,0:T(8,128)(2,1)S(1)} %copy-done, bf16[2,64,1024]{2,1,0:T(8,128)(2,1)S(1)} %bitcast.14, bf16[2,64,768]{2,1,0:T(8,128)(2,1)S(1)} %copy-done.2), custom_call_target="tpu_custom_call" | custom-call | flops 603979776 | bytes 4194304 | tf_op jit(solution)/shard_map/pallas_call | solution.py:284
  45.9 0.0 collective-permute-done.other_ref
  45.9 6.1 %shard_map.86 = bf16[8,64,1792]{2,1,0:T(8,128)(2,1)S(1)} custom-call(bf16[256,1024]{1,0:T(8,128)(2,1)S(1)} %all_gather.3.own_ref, bf16[256,1024]{1,0:T(8,128)(2,1)S(1)} %collective-permute-done.other_ref, bf16[2,1024,768]{2,1,0:T(8,128)(2,1)} %base_ref.5, bf16[128,1024]{1,0:T(8,128)(2,1)S(1)} %bitcast.15, f32[48,128]{1,0:T(8,128)S(1)} %get-tuple-element.12.extra_ref), custom_call_target="tpu_custom_call" | custom-call | flops 1744830464 | bytes 8388608 | tf_op jit(solution)/shard_map/pallas_call | solution.py:291
  52.0 0.0 copy-start.1
  52.0 1.2 copy-done.1
  53.2 0.0 copy-start.3
  53.2 0.0 copy-start.8
  53.2 5.4 %all-to-all-start = ((bf16[8,64,1792]{2,1,0:T(8,128)(2,1)}), bf16[8,64,1792]{2,1,0:T(8,128)(2,1)S(1)}, u32[]{:S(2)}, u32[]{:S(2)}) async-start(bf16[8,64,1792]{2,1,0:T(8,128)(2,1)} %copy-done.1), calls=%async_computation | async-start | bytes 3670016 | tf_op jit(solution)/shard_map/all_to_all | solution.py:298
  58.7 0.1 pad_add_fusion.place_ref
  58.8 24.7 %all-to-all-done.got_ref = bf16[8,64,1792]{2,1,0:T(8,128)(2,1)S(1)} async-done(((bf16[8,64,1792]{2,1,0:T(8,128)(2,1)}), bf16[8,64,1792]{2,1,0:T(8,128)(2,1)S(1)}, u32[]{:S(2)}, u32[]{:S(2)}) %all-to-all-start) | async-done | bytes 1835040 | tf_op jit(solution)/shard_map/all_to_all | solution.py:298
  83.5 0.0 copy-done.3
  83.5 0.0 copy-done.8
  83.5 0.0 copy-start.7
  83.5 0.9 copy-done.7
  84.4 3.0 %shard_map.87 = (f32[16,152,128]{2,1,0:T(8,128)S(1)}, f32[2,768]{1,0:T(2,128)S(1)}) custom-call(s32[2]{0:T(128)S(1)} %pad_add_fusion.place_ref, bf16[8,64,1792]{2,1,0:T(8,128)(2,1)S(1)} %all-to-all-done.got_ref, bf16[64,768]{1,0:T(8,128)(2,1)S(1)} %copy-done.7, bf16[2,64,768]{2,1,0:T(8,128)(2,1)S(1)} %copy-done.3, f32[2,768]{1,0:T(2,128)S(1)} %copy-done.8, ...), custom_call_target="tpu_custom_call" | custom-call | flops 134217728 | bytes 4194304 | tf_op jit(solution)/shard_map/pallas_call | solution.py:301
  87.3 0.0 copy-start.4
  87.4 1.0 copy-done.4
  88.4 0.0 copy-start.6
  88.4 8.7 %all-to-all-start.1 = ((f32[16,152,128]{2,1,0:T(8,128)}), f32[16,152,128]{2,1,0:T(8,128)S(1)}, u32[]{:S(2)}, u32[]{:S(2)}) async-start(f32[16,152,128]{2,1,0:T(8,128)} %copy-done.4), calls=%async_computation.1 | async-start | bytes 2490368 | tf_op jit(solution)/shard_map/all_to_all | solution.py:308
  97.1 19.4 %all-to-all-done.1.got_ref = f32[16,152,128]{2,1,0:T(8,128)S(1)} async-done(((f32[16,152,128]{2,1,0:T(8,128)}), f32[16,152,128]{2,1,0:T(8,128)S(1)}, u32[]{:S(2)}, u32[]{:S(2)}) %all-to-all-start.1) | async-done | bytes 1245216 | tf_op jit(solution)/shard_map/all_to_all | solution.py:308
  116.5 0.8 shard_map.88
  117.3 0.0 copy-done.6
  117.3 3.1 %shard_map.89 = (f32[128,512]{1,0:T(8,128)S(1)}, f32[128,512]{1,0:T(8,128)S(1)}) custom-call(s32[2]{0:T(128)S(1)} %pad_add_fusion.place_ref, f32[16,152,128]{2,1,0:T(8,128)S(1)} %all-to-all-done.1.got_ref, f32[2,768]{1,0:T(2,128)S(1)} %get-tuple-element.17.coeff_ref, bf16[256,1024]{1,0:T(8,128)(2,1)S(1)} %all_gather.3.own_ref, ...), custom_call_target="tpu_custom_call" | custom-call | flops 1073741824 | bytes 8388608 | tf_op jit(solution)/shard_map/pallas_call | solution.py:317
  120.4 1.9 collective-permute-start.1
  122.3 1.5 collective-permute-done.1
  123.9 27.1 %all_to_all.25 = f32[16,8,512]{2,1,0:T(8,128)S(1)} all-to-all(f32[16,8,512]{2,1,0:T(8,128)S(1)} %add_bitcast_fusion), channel_id=1, replica_groups=mesh['dp'=2,'z'=16,'core'=2,'tensor'=8] {'z'}, dimensions={0} | all-to-all | bytes 524288 | tf_op jit(solution)/shard_map/all_to_all | solution.py:328
  151.0 2.8 %collective-permute-start.2 = (f32[8,512]{1,0:T(8,128)S(1)}, f32[8,512]{1,0:T(8,128)S(1)}, u32[]{:S(2)}, u32[]{:S(2)}) collective-permute-start(f32[8,512]{1,0:T(8,128)S(1)} %reduce_sum.9), channel_id=1, source_target_pairs={{0,256},{256,0},{1,257},{257,1},{2,258},{258,2},{3,259},{259,3},{4... | collective-permute-start | bytes 49160 | tf_op jit(solution)/shard_map/ppermute | solution.py:329
  153.8 4.4 %collective-permute-done.2 = f32[8,512]{1,0:T(8,128)S(1)} collective-permute-done((f32[8,512]{1,0:T(8,128)S(1)}, f32[8,512]{1,0:T(8,128)S(1)}, u32[]{:S(2)}, u32[]{:S(2)}) %collective-permute-start.2) | collective-permute-done | bytes 16416 | tf_op jit(solution)/shard_map/ppermute | solution.py:329
  158.2 23.5 %all_to_all.26 = f32[16,8,512]{2,1,0:T(8,128)S(1)} all-to-all(f32[16,8,512]{2,1,0:T(8,128)S(1)} %broadcast_in_dim.2), channel_id=1, replica_groups=mesh['dp'=2,'z'=16,'core'=2,'tensor'=8] {'z'}, dimensions={0} | all-to-all | bytes 524288 | tf_op jit(solution)/shard_map/all_to_all | solution.py:330
  181.7 3.6 %all-to-all-start.2 = ((f32[16,8,768]{2,1,0:T(8,128)}), f32[16,8,768]{2,1,0:T(8,128)S(1)}, u32[]{:S(2)}, u32[]{:S(2)}) async-start(f32[16,8,768]{2,1,0:T(8,128)} %get-tuple-element.16), calls=%async_computation.2 | async-start | bytes 786432 | tf_op jit(solution)/shard_map/all_to_all | solution.py:316
  185.3 1.9 collective-permute-start.3
  187.2 7.4 %all-to-all-done.2 = f32[16,8,768]{2,1,0:T(8,128)S(1)} async-done(((f32[16,8,768]{2,1,0:T(8,128)}), f32[16,8,768]{2,1,0:T(8,128)S(1)}, u32[]{:S(2)}, u32[]{:S(2)}) %all-to-all-start.2) | async-done | bytes 393248 | tf_op jit(solution)/shard_map/all_to_all | solution.py:316
  194.6 0.0 collective-permute-done.3
  194.6 0.8 fusion
  195.5 0.7 copy.10
  (4 shorter events, 0.1 us)
Async XLA Ops:
  36.9 8.9 %collective-permute-start = (bf16[256,1024]{1,0:T(8,128)(2,1)S(1)}, bf16[256,1024]{1,0:T(8,128)(2,1)S(1)}, u32[]{:S(2)}, u32[]{:S(2)}) collective-permute-start(bf16[256,1024]{1,0:T(8,128)(2,1)S(1)} %all_gather.3.own_ref), channel_id=1, source_target_pairs={{0,8},{8,0},{1,9},{9,1},{2,10},{10,2},{3,11},{11,3},{4,12},{12,4},... | collective-permute-start | bytes 1572872 | tf_op jit(solution)/shard_map/ppermute | solution.py:283
  38.8 1.9 copy-start
  40.7 0.9 copy-start.2
  41.7 0.9 copy-start.5
  52.0 1.2 copy-start.1
  53.2 30.2 %copy-start.3 = (bf16[2,64,768]{2,1,0:T(8,128)(2,1)S(1)}, bf16[2,64,768]{2,1,0:T(8,128)(2,1)}, u32[]{:S(2)}) copy-start(bf16[2,64,768]{2,1,0:T(8,128)(2,1)} %a_ref.5) | copy-start | bytes 589828
  53.2 30.2 %copy-start.8 = (f32[2,768]{1,0:T(2,128)S(1)}, f32[2,768]{1,0:T(2,128)}, u32[]{:S(2)}) copy-start(f32[2,768]{1,0:T(2,128)} %mag_ref.3) | copy-start | bytes 18436
  53.2 30.2 %all-to-all-start = ((bf16[8,64,1792]{2,1,0:T(8,128)(2,1)}), bf16[8,64,1792]{2,1,0:T(8,128)(2,1)S(1)}, u32[]{:S(2)}, u32[]{:S(2)}) async-start(bf16[8,64,1792]{2,1,0:T(8,128)(2,1)} %copy-done.1), calls=%async_computation | async-start | bytes 3670016 | tf_op jit(solution)/shard_map/all_to_all | solution.py:298
  83.5 0.9 copy-start.7
  87.3 1.0 copy-start.4
  88.4 28.9 %copy-start.6 = (bf16[2,1024,64]{1,2,0:T(8,128)(2,1)S(1)}, bf16[2,1024,64]{1,2,0:T(8,128)(2,1)}, u32[]{:S(2)}) copy-start(bf16[2,1024,64]{1,2,0:T(8,128)(2,1)} %param.8) | copy-start | bytes 786436
  88.4 28.1 %all-to-all-start.1 = ((f32[16,152,128]{2,1,0:T(8,128)}), f32[16,152,128]{2,1,0:T(8,128)S(1)}, u32[]{:S(2)}, u32[]{:S(2)}) async-start(f32[16,152,128]{2,1,0:T(8,128)} %copy-done.4), calls=%async_computation.1 | async-start | bytes 2490368 | tf_op jit(solution)/shard_map/all_to_all | solution.py:308
  120.4 3.4 %collective-permute-start.1 = (f32[128,512]{1,0:T(8,128)S(1)}, f32[128,512]{1,0:T(8,128)S(1)}, u32[]{:S(2)}, u32[]{:S(2)}) collective-permute-start(f32[128,512]{1,0:T(8,128)S(1)} %get-tuple-element.19), channel_id=1, source_target_pairs={{0,8},{8,0},{1,9},{9,1},{2,10},{10,2},{3,11},{11,3},{4,12},{12,4},... | collective-permute-start | bytes 786440 | tf_op jit(solution)/shard_map/ppermute | solution.py:326
  151.0 7.1 %collective-permute-start.2 = (f32[8,512]{1,0:T(8,128)S(1)}, f32[8,512]{1,0:T(8,128)S(1)}, u32[]{:S(2)}, u32[]{:S(2)}) collective-permute-start(f32[8,512]{1,0:T(8,128)S(1)} %reduce_sum.9), channel_id=1, source_target_pairs={{0,256},{256,0},{1,257},{257,1},{2,258},{258,2},{3,259},{259,3},{4... | collective-permute-start | bytes 49160 | tf_op jit(solution)/shard_map/ppermute | solution.py:329
  181.7 12.9 %all-to-all-start.2 = ((f32[16,8,768]{2,1,0:T(8,128)}), f32[16,8,768]{2,1,0:T(8,128)S(1)}, u32[]{:S(2)}, u32[]{:S(2)}) async-start(f32[16,8,768]{2,1,0:T(8,128)} %get-tuple-element.16), calls=%async_computation.2 | async-start | bytes 786432 | tf_op jit(solution)/shard_map/all_to_all | solution.py:316
  185.3 9.4 %collective-permute-start.3 = (f32[128,512]{1,0:T(8,128)S(1)}, f32[128,512]{1,0:T(8,128)S(1)}, u32[]{:S(2)}, u32[]{:S(2)}) collective-permute-start(f32[128,512]{1,0:T(8,128)S(1)} %bitcast.18), channel_id=1, source_target_pairs={{0,8},{8,0},{1,9},{9,1},{2,10},{10,2},{3,11},{11,3},{4,12},{12,4},... | collective-permute-start | bytes 786440 | tf_op jit(solution)/shard_map/ppermute | solution.py:332

commit v3 on v2

--- a/solution.py
+++ b/solution.py
@@ -1,4 +1,3 @@
-import functools
 import math
 
 import jax
@@ -11,7 +10,7 @@
 F32 = jnp.float32
 BF16 = jnp.bfloat16
 GROUP = ("dp", "tensor")
-PARAMS = pltpu.CompilerParams(vmem_limit_bytes=48 * 2**20)
+PARAMS = pltpu.CompilerParams(vmem_limit_bytes=24 * 2**20)
 VMEM = pl.BlockSpec(memory_space=pltpu.VMEM)
 SMEM = pl.BlockSpec(memory_space=pltpu.SMEM)
 
@@ -22,7 +21,7 @@
 
 def encode(x, peak):
     size = jnp.exp(POWER * jnp.log(1.0 + jnp.abs(x) * (BEND / peak)) - SHIFT)
-    return jnp.where(x < 0, -size, size).astype(BF16)
+    return jnp.where(x < 0, -size, size)
 
 
 def decode(code, peak):
@@ -92,7 +91,8 @@
                 value = dot(ref[...], bt_ref[...], NT)
                 lanes = slice(2 * columns, 2 * columns + rank)
             peak = peak_of(value)
-            out_ref[:, where, lanes] = encode(value, peak).reshape(shards, half, value.shape[1])
+            code = encode(value, peak).astype(BF16)
+            out_ref[:, where, lanes] = code.reshape(shards, half, value.shape[1])
             peaks = jnp.where(line == row, peak, peaks)
             row += 1
     tail = jnp.concatenate([extra_ref[...], peaks], axis=0).astype(BF16)
@@ -158,43 +158,54 @@
     douts = (cot * up * sig * (1.0 + gate * (1.0 - sig)), cot * gate * sig)
     members = out_ref.shape[0]
     rows = 2 * rank // members
-    at_cross = tiles * rows
-    at_m = at_cross + tiles * rows // 2
-    at_back = at_m + 16
-    out_ref[:, at_m:at_back, :] = jnp.zeros((members, at_back - at_m, 128), F32)
-    backs = []
+    line = lax.broadcasted_iota(jnp.int32, (rows, 128), 0)
+    codes, peaks, back_codes, back_peaks, ms = [], [], [], [], []
     for k in range(2):
         mine = slice(k * rank, (k + 1) * rank)
-        m = jnp.sum(douts[k] * pres[k], axis=0, keepdims=True)
-        dpre = douts[k] * scales[k]
-        hi, lo = split(dpre)
+        ms.append(jnp.sum(douts[k] * pres[k], axis=0, keepdims=True))
+        hi, lo = split(douts[k] * scales[k])
         grad_a = (
             dot(low_hi[:, mine], hi, TN) + dot(low_hi[:, mine], lo, TN) + dot(low_lo[:, mine], hi, TN)
         )
-        backs.append(dot(hi, a_ref[k], NT) + dot(lo, a_ref[k], NT))
-        for i in range(tiles):
-            lanes = slice(128 * i, 128 * (i + 1))
-            row = at_m + tiles * k + i
-            out_ref[:, row : row + 1, :] = jnp.broadcast_to(m[None, :, lanes], (members, 1, 128))
-            for j in range(members // 2):
-                out_ref[k * members // 2 + j, rows * i : rows * (i + 1), :] = grad_a[
-                    rows * j : rows * (j + 1), lanes
-                ]
-    for i in range(tiles // 2):
-        lanes = pl.ds(pl.multiple_of((dp * (tiles // 2) + i) * 128, 128), 128)
-        out_ref[:, at_cross + rows * i : at_cross + rows * (i + 1), :] = cross_ref[:, lanes].reshape(
-            members, rows, 128
-        )
-    back = jnp.concatenate(backs, axis=1)
-    out_ref[:, at_back:, :] = jnp.broadcast_to(back[None], (members,) + back.shape)
+        back = dot(hi, a_ref[k], NT) + dot(lo, a_ref[k], NT)
+        width = columns // 2
+        cross = cross_ref[mine, pl.ds(pl.multiple_of(dp * width, width), width)]
+        peaks.append((peak_of(grad_a), peak_of(cross)))
+        codes.append((encode(grad_a, peaks[k][0]), encode(cross, peaks[k][1])))
+        back_peaks.append(peak_of(back))
+        back_codes.append(encode(back, back_peaks[k]))
+    for j in range(members):
+        k, at = divmod(j * rows, rank)
+        blocks = [
+            code[at : at + rows, 128 * i : 128 * (i + 1)]
+            for code in codes[k]
+            for i in range(code.shape[1] // 128)
+        ]
+        tail_block = jnp.zeros((rows, 128), F32)
+        for row, peak in enumerate(peaks[k] + tuple(back_peaks)):
+            tail_block = jnp.where(line == row, peak, tail_block)
+        blocks.append(tail_block)
+        for i in range(0, len(blocks), 2):
+            pair = jnp.concatenate(blocks[i : i + 2], axis=0).astype(BF16)
+            out_ref[j, rows * i : rows * (i + 2), :] = pair
+    height = rows * (tiles + tiles // 2 + 1)
+    lines = []
+    for piece in range(2):
+        for k in range(2):
+            part = ms[k].astype(BF16).astype(F32)
+            ms[k] = ms[k] - part
+            lines += [part[:, 128 * i : 128 * (i + 1)] for i in range(tiles)]
+    lines.append(jnp.zeros((32 - len(lines), 128), F32))
+    rest = jnp.concatenate(lines + [jnp.concatenate(back_codes, axis=1)], axis=0).astype(BF16)
+    out_ref[:, height:, :] = jnp.broadcast_to(rest[None], (members,) + rest.shape)
 
 
 def coefficient_kernel(place_ref, got_ref, norm_ref, mag_ref, rows_ref, grad_m_ref, coeff_ref):
     members, rows, columns = rows_ref.shape
     tiles = columns // 128
-    at_cross = tiles * rows
-    at_m = at_cross + tiles * rows // 2
-    m = jnp.sum(got_ref[:, at_m : at_m + 16, :], axis=0)
+    height = rows * (tiles + tiles // 2 + 1)
+    m = jnp.sum(got_ref[:, height : height + 32, :].astype(F32), axis=0)
+    m = m[: 2 * tiles] + m[2 * tiles : 4 * tiles]
     for k in range(2):
         norm = norm_ref[k : k + 1, :]
         m_row = jnp.concatenate([m[tiles * k + i : tiles * k + i + 1] for i in range(tiles)], axis=1)
@@ -202,14 +213,21 @@
         grad_m_ref[k : k + 1, :] = grad_m
         coeff_ref[k : k + 1, :] = -grad_m * mag_ref[k : k + 1, :] / (norm * norm)
     coeff = jnp.where(place_ref[0] == 0, coeff_ref[0:1, :], coeff_ref[1:2, :])
+    tokens = [jnp.zeros((rows, 128), F32)] * tiles
+    crosses = [jnp.zeros((rows, 128), F32)] * tiles
+    for j in range(members):
+        blocks = got_ref[j, :height, :].astype(F32)
+        peaks = blocks[height - rows :]
+        token = decode(blocks[: rows * tiles], peaks[0:1, 0:1])
+        cross = decode(blocks[rows * tiles : height - rows], peaks[1:2, 0:1])
+        for i in range(tiles):
+            tokens[i] = tokens[i] + token[rows * i : rows * (i + 1)]
+        first = j * 2 // members * (tiles // 2)
+        for i in range(tiles // 2):
+            crosses[first + i] = crosses[first + i] + cross[rows * i : rows * (i + 1)]
     for i in range(tiles):
         lanes = slice(128 * i, 128 * (i + 1))
-        token = jnp.sum(got_ref[:, rows * i : rows * (i + 1), :], axis=0)
-        source, tile = divmod(i, tiles // 2)
-        at = at_cross + rows * tile
-        sources = slice(source * members // 2, (source + 1) * members // 2)
-        cross = jnp.sum(got_ref[sources, at : at + rows, :], axis=0)
-        own = token + cross * coeff[:, lanes]
+        own = tokens[i] + crosses[i] * coeff[:, lanes]
         rows_ref[:, :, lanes] = jnp.broadcast_to(own[None], (members, rows, 128))
 
 
@@ -223,10 +241,16 @@
     owned = 2 * own_ref.shape[0] // shards
     half = owned // 2
     at_back = got_ref.shape[1] - owned
+    backs = []
+    lane = lax.broadcasted_iota(jnp.int32, (1, 2 * rank), 1)
+    for j in range(shards):
+        source = dp * shards + j
+        peaks = got_ref[source, at_back - 48 : at_back - 32, :].astype(F32)
+        peak = jnp.where(lane < rank, peaks[10:11, 0:1], peaks[11:12, 0:1])
+        backs.append(decode(got_ref[source, at_back:, :], peak))
     total = None
     for side, ref in enumerate((own_ref, other_ref)):
-        rows = pl.ds(at_back + side * half, half)
-        back = got_ref[pl.ds(dp * shards, shards), rows, :].reshape(shards * half, 2 * rank)
+        back = jnp.concatenate([b[side * half : (side + 1) * half] for b in backs], axis=0)
         hi, lo = split(back)
         both = dot(jnp.concatenate([hi, lo], axis=1), ref[...], TN)
         part = both[: 2 * rank] + both[2 * rank :]
@@ -265,7 +289,6 @@
 def per_device(tokens, base, b, a, magnitude, cotangent):
     dp = lax.axis_index("dp")
     core = lax.axis_index("core")
-    member = lax.axis_index(GROUP)
     depth, columns = base.shape[1:]
     rank = a.shape[1]
     shards = lax.axis_size("tensor")
@@ -277,7 +300,6 @@
     swap = [(0, 1), (1, 0)]
     bt = jnp.swapaxes(b, 1, 2)
     place = jnp.stack([dp, core]).astype(jnp.int32)
-    my_k = jnp.reshape(member // shards, (1,)).astype(jnp.int32)
 
     g_own = lax.all_gather(tokens, "z", axis=0, tiled=True)
     g_other = lax.ppermute(g_own, "core", swap)
@@ -295,12 +317,13 @@
         flops=2 * shards * own * depth * 2 * (columns + rank),
         size=8 * 2**20,
     )(g_own, g_other, base, bt.reshape(2 * rank, depth), extra)
+    payload, place = lax.optimization_barrier((payload, place))
     got = lax.all_to_all(payload, "tensor", 0, 0)
 
-    height = tiles * rows + tiles * rows // 2 + 16 + own
+    height = rows * (tiles + tiles // 2 + 1) + 32 + own
     sends, norm = call(
         local_kernel,
-        [shape((members, height, 128)), shape((2, columns))],
+        [shape((members, height, 128), BF16), shape((2, columns))],
         [SMEM] + [VMEM] * 5,
         flops=2**27,
         size=4 * 2**20,
@@ -312,8 +335,7 @@
         [shape((members, rows, columns)), shape((2, columns)), shape((2, columns))],
         [SMEM] + [VMEM] * 3,
         size=2 * 2**20,
-    )(my_k, got, norm, magnitude)
-    grad_a = lax.all_to_all(a_rows, GROUP, 0, 0).reshape(2, rank, columns)
+    )(place, got, norm, magnitude)
     mine, theirs = call(
         width_kernel,
         [shape((2 * rank, depth // 2))] * 2,
@@ -326,12 +348,15 @@
     part = mine + lax.ppermute(theirs, "core", swap)
     chunks = part.reshape(zs, 2 * rank // zs, depth // 2)
     piece = jnp.sum(lax.all_to_all(chunks, "z", 0, 0), axis=0)
+    piece, a_rows = lax.optimization_barrier((piece, a_rows))
+    grad_a = lax.all_to_all(a_rows, GROUP, 0, 0).reshape(2, rank, columns)
     piece = piece + lax.ppermute(piece, "dp", swap)
+    piece, grad_a = lax.optimization_barrier((piece, grad_a))
     full = lax.all_to_all(jnp.broadcast_to(piece[None], chunks.shape), "z", 0, 0)
     full = full.reshape(2 * rank, depth // 2)
     other = lax.ppermute(full, "core", swap)
     grad_b = jnp.where(
-        core == 0, jnp.concatenate([full, other], axis=1), jnp.concatenate([other, full], axis=1)
+        place[1] == 0, jnp.concatenate([full, other], axis=1), jnp.concatenate([other, full], axis=1)
     )
     return grad_a, jnp.swapaxes(grad_b.reshape(2, rank, depth), 1, 2), grad_m
 

time: 197 us -> 180 us (0.914)
  the two profiles are of different devices: /device:TPU:32 before, /device:TPU:1 now
where the time goes in v3:
time: 180 us; the launch traced here: 179 us
  blocking collectives  121 us (67%)
  starting transfers between devices  31.6 us (18%)
  Pallas kernels  14.3 us (8%)
  local copies, waits for them, and re-layouts  5.14 us (3%)
  waiting for transfers between devices  4.64 us (3%)
    all_gather x1, blocking collectives, per_device(): g_own = lax.all_gather(tokens, 'z', axis=0, tiled=True)  32.1 us
    all_to_all x1, blocking collectives, per_device(): got = lax.all_to_all(payload, 'tensor', 0, 0)  29.2 us
    all_to_all x1, blocking collectives, per_device(): lax.all_to_all(jnp.broadcast_to(piece[None], chunks.shape), 'z', 0, 0)  24.1 us
    all_to_all x1, blocking collectives, per_device(): piece = jnp.sum(lax.all_to_all(chunks, 'z', 0, 0), axis=0)  20 us
    all_to_all x1, blocking collectives, per_device(): got = lax.all_to_all(sends, GROUP, 0, 0)  15.9 us
    ppermute x1, starting transfers between devices, per_device(): g_other = lax.ppermute(g_own, 'core', swap)  10.1 us
    ppermute x1, starting transfers between devices, per_device(): other = lax.ppermute(full, 'core', swap)  8.68 us
    ppermute x1, starting transfers between devices, per_device(): piece = piece + lax.ppermute(piece, 'dp', swap)  4.69 us
  transfers between devices with their start and end apart: 5, of which 3 were waited for; matrix products, arithmetic and copies ran while one was open for 0% of the time, Pallas kernels for 2%

profile of v3, /device:TPU:1, one launch (start us, length us, event | category | flops | bytes accessed | tf_op | source)
XLA Modules:
  0.0 179.4 jit_solution(5055350064752040852)
XLA Ops:
  0.6 32.1 %all_gather.3.own_ref = bf16[256,1024]{1,0:T(8,128)(2,1)S(1)} all-gather(bf16[16,1024]{1,0:T(8,128)(2,1)} %param.6), channel_id=1, replica_groups=mesh['dp'=2,'z'=16,'core'=2,'tensor'=8] {'z'}, dimensions={0}, use_global_device_ids=true | all-gather | bytes 557056 | tf_op jit(solution)/shard_map/all_gather | solution.py:304
  32.7 10.1 %collective-permute-start = (bf16[256,1024]{1,0:T(8,128)(2,1)S(1)}, bf16[256,1024]{1,0:T(8,128)(2,1)S(1)}, u32[]{:S(2)}, u32[]{:S(2)}) collective-permute-start(bf16[256,1024]{1,0:T(8,128)(2,1)S(1)} %all_gather.3.own_ref), channel_id=1, source_target_pairs={{0,8},{8,0},{1,9},{9,1},{2,10},{10,2},{3,11},{11,3},{4,12},{12,4},... | collective-permute-start | bytes 1572872 | tf_op jit(solution)/shard_map/ppermute | solution.py:305
  42.8 0.0 copy-start
  42.9 1.9 %copy-done = bf16[2,1024,768]{2,1,0:T(8,128)(2,1)S(1)} copy-done((bf16[2,1024,768]{2,1,0:T(8,128)(2,1)S(1)}, bf16[2,1024,768]{2,1,0:T(8,128)(2,1)}, u32[]{:S(2)}) %copy-start) | copy-done | bytes 3145752
  44.7 0.0 copy-start.2
  44.7 0.9 copy-done.2
  45.7 0.0 copy-start.4
  45.7 0.9 copy-done.4
  46.6 3.3 %shard_map.85 = (f32[128,768]{1,0:T(8,128)S(1)}, f32[48,128]{1,0:T(8,128)S(1)}) custom-call(bf16[2,1024,768]{2,1,0:T(8,128)(2,1)S(1)} %copy-done, bf16[2,64,1024]{2,1,0:T(8,128)(2,1)S(1)} %bitcast.14, bf16[2,64,768]{2,1,0:T(8,128)(2,1)S(1)} %copy-done.2), custom_call_target="tpu_custom_call" | custom-call | flops 603979776 | bytes 4194304 | tf_op jit(solution)/shard_map/pallas_call | solution.py:306
  49.9 0.1 pad_add_fusion.place_ref
  50.0 0.0 collective-permute-done.other_ref
  50.0 4.2 %shard_map.86 = bf16[8,64,1792]{2,1,0:T(8,128)(2,1)S(1)} custom-call(bf16[256,1024]{1,0:T(8,128)(2,1)S(1)} %all_gather.3.own_ref, bf16[256,1024]{1,0:T(8,128)(2,1)S(1)} %collective-permute-done.other_ref, bf16[2,1024,768]{2,1,0:T(8,128)(2,1)S(1)} %copy-done, bf16[128,1024]{1,0:T(8,128)(2,1)S(1)} %bitcast.15, f32[48,128]{1,0:T(8,128)S(1)} %get-tuple-element.18.extra_ref), custom_call_target="tpu_custom_call" | custom-call | flops 1744830464 | bytes 8388608 | tf_op jit(solution)/shard_map/pallas_call | solution.py:313
  54.2 0.0 copy-start.3
  54.2 0.0 copy-start.6
  54.2 0.0 copy-start.7
  54.2 29.2 %all_to_all.25.got_ref = bf16[8,64,1792]{2,1,0:T(8,128)(2,1)S(1)} all-to-all(bf16[8,64,1792]{2,1,0:T(8,128)(2,1)S(1)} %shard_map.86), channel_id=1, replica_groups=mesh['dp'=2,'z'=16,'core'=2,'tensor'=8] {'tensor'}, dimensions={0} | all-to-all | bytes 3670016 | tf_op jit(solution)/shard_map/all_to_all | solution.py:321
  83.5 0.0 copy-done.3
  83.5 0.0 copy-done.6
  83.5 0.0 copy-done.7
  83.5 0.0 copy-start.1
  83.5 0.0 copy-start.5
  83.5 3.3 %shard_map.87 = (bf16[16,176,128]{2,1,0:T(8,128)(2,1)S(1)}, f32[2,768]{1,0:T(2,128)S(1)}) custom-call(s32[2]{0:T(128)S(1)} %pad_add_fusion.place_ref, bf16[8,64,1792]{2,1,0:T(8,128)(2,1)S(1)} %all_to_all.25.got_ref, bf16[64,768]{1,0:T(8,128)(2,1)S(1)} %copy-done.6, bf16[2,64,768]{2,1,0:T(8,128)(2,1)S(1)} %copy-done.3, f32[2,768]{1,0:T(2,128)S(1)} %copy-done.7, ...), custom_call_target="tpu_custom_call" | custom-call | flops 134217728 | bytes 4194304 | tf_op jit(solution)/shard_map/pallas_call | solution.py:324
  86.8 15.9 %all_to_all.26.got_ref = bf16[16,176,128]{2,1,0:T(8,128)(2,1)S(1)} all-to-all(bf16[16,176,128]{2,1,0:T(8,128)(2,1)S(1)} %get-tuple-element.22), channel_id=1, replica_groups=mesh['dp'=2,'z'=16,'core'=2,'tensor'=8] {'dp','tensor'}, dimensions={0} | all-to-all | bytes 1441792 | tf_op jit(solution)/shard_map/all_to_all | solution.py:331
  102.7 1.6 shard_map.88
  104.4 0.0 copy-done.1
  104.4 0.0 copy-done.5
  104.4 1.8 %shard_map.89 = (f32[128,512]{1,0:T(8,128)S(1)}, f32[128,512]{1,0:T(8,128)S(1)}) custom-call(s32[2]{0:T(128)S(1)} %pad_add_fusion.place_ref, bf16[16,176,128]{2,1,0:T(8,128)(2,1)S(1)} %all_to_all.26.got_ref, f32[2,768]{1,0:T(2,128)S(1)} %get-tuple-element.24.coeff_ref, bf16[256,1024]{1,0:T(8,128)(2,1)S(1)} %all_gather.3.own_ref, ...), custom_call_target="tpu_custom_call" | custom-call | flops 1073741824 | bytes 8388608 | tf_op jit(solution)/shard_map/pallas_call | solution.py:339
  106.2 4.5 %collective-permute-start.1 = (f32[128,512]{1,0:T(8,128)S(1)}, f32[128,512]{1,0:T(8,128)S(1)}, u32[]{:S(2)}, u32[]{:S(2)}) collective-permute-start(f32[128,512]{1,0:T(8,128)S(1)} %get-tuple-element.26), channel_id=1, source_target_pairs={{0,8},{8,0},{1,9},{9,1},{2,10},{10,2},{3,11},{11,3},{4,12},{12,4},... | collective-permute-start | bytes 786440 | tf_op jit(solution)/shard_map/ppermute | solution.py:348
  110.8 1.1 collective-permute-done.1
  111.9 20.0 %all_to_all.27 = f32[16,8,512]{2,1,0:T(8,128)S(1)} all-to-all(f32[16,8,512]{2,1,0:T(8,128)S(1)} %add_bitcast_fusion), channel_id=1, replica_groups=mesh['dp'=2,'z'=16,'core'=2,'tensor'=8] {'z'}, dimensions={0} | all-to-all | bytes 524288 | tf_op jit(solution)/shard_map/all_to_all | solution.py:350
  131.9 3.6 %all-to-all-start.3 = ((f32[16,8,768]{2,1,0:T(8,128)}), f32[16,8,768]{2,1,0:T(8,128)S(1)}, u32[]{:S(2)}, u32[]{:S(2)}) async-start(f32[16,8,768]{2,1,0:T(8,128)} %get-tuple-element.29), calls=%async_computation.3 | async-start | bytes 786432 | tf_op jit(solution)/shard_map/all_to_all | solution.py:352
  135.5 4.7 %collective-permute-start.2 = (f32[8,512]{1,0:T(8,128)S(1)}, f32[8,512]{1,0:T(8,128)S(1)}, u32[]{:S(2)}, u32[]{:S(2)}) collective-permute-start(f32[8,512]{1,0:T(8,128)S(1)} %reduce_sum.9), channel_id=1, source_target_pairs={{0,256},{256,0},{1,257},{257,1},{2,258},{258,2},{3,259},{259,3},{4... | collective-permute-start | bytes 49160 | tf_op jit(solution)/shard_map/ppermute | solution.py:353
  140.2 2.3 %collective-permute-done.2 = f32[8,512]{1,0:T(8,128)S(1)} collective-permute-done((f32[8,512]{1,0:T(8,128)S(1)}, f32[8,512]{1,0:T(8,128)S(1)}, u32[]{:S(2)}, u32[]{:S(2)}) %collective-permute-start.2) | collective-permute-done | bytes 16416 | tf_op jit(solution)/shard_map/ppermute | solution.py:353
  142.5 1.2 all-to-all-done.3
  143.8 24.1 %all_to_all.28 = f32[16,8,512]{2,1,0:T(8,128)S(1)} all-to-all(f32[16,8,512]{2,1,0:T(8,128)S(1)} %broadcast_in_dim.2), channel_id=1, replica_groups=mesh['dp'=2,'z'=16,'core'=2,'tensor'=8] {'z'}, dimensions={0} | all-to-all | bytes 524288 | tf_op jit(solution)/shard_map/all_to_all | solution.py:355
  167.8 8.7 %collective-permute-start.3 = (f32[128,512]{1,0:T(8,128)S(1)}, f32[128,512]{1,0:T(8,128)S(1)}, u32[]{:S(2)}, u32[]{:S(2)}) collective-permute-start(f32[128,512]{1,0:T(8,128)S(1)} %bitcast.18), channel_id=1, source_target_pairs={{0,8},{8,0},{1,9},{9,1},{2,10},{10,2},{3,11},{11,3},{4,12},{12,4},... | collective-permute-start | bytes 786440 | tf_op jit(solution)/shard_map/ppermute | solution.py:357
  176.5 0.6 slice.3
  177.8 0.0 collective-permute-done.3
  177.8 0.8 fusion
  178.6 0.7 copy.10
  (4 shorter events, 0.1 us)
Async XLA Ops:
  32.7 17.3 %collective-permute-start = (bf16[256,1024]{1,0:T(8,128)(2,1)S(1)}, bf16[256,1024]{1,0:T(8,128)(2,1)S(1)}, u32[]{:S(2)}, u32[]{:S(2)}) collective-permute-start(bf16[256,1024]{1,0:T(8,128)(2,1)S(1)} %all_gather.3.own_ref), channel_id=1, source_target_pairs={{0,8},{8,0},{1,9},{9,1},{2,10},{10,2},{3,11},{11,3},{4,12},{12,4},... | collective-permute-start | bytes 1572872 | tf_op jit(solution)/shard_map/ppermute | solution.py:305
  42.8 1.9 %copy-start = (bf16[2,1024,768]{2,1,0:T(8,128)(2,1)S(1)}, bf16[2,1024,768]{2,1,0:T(8,128)(2,1)}, u32[]{:S(2)}) copy-start(bf16[2,1024,768]{2,1,0:T(8,128)(2,1)} %base_ref.5) | copy-start | bytes 9437188
  44.7 0.9 copy-start.2
  45.7 0.9 copy-start.4
  54.2 29.3 %copy-start.3 = (bf16[2,64,768]{2,1,0:T(8,128)(2,1)S(1)}, bf16[2,64,768]{2,1,0:T(8,128)(2,1)}, u32[]{:S(2)}) copy-start(bf16[2,64,768]{2,1,0:T(8,128)(2,1)} %a_ref.5) | copy-start | bytes 589828
  54.2 29.3 %copy-start.6 = (bf16[64,768]{1,0:T(8,128)(2,1)S(1)}, bf16[64,768]{1,0:T(8,128)(2,1)}, u32[]{:S(2)}) copy-start(bf16[64,768]{1,0:T(8,128)(2,1)} %cot_ref.1) | copy-start | bytes 294916
  54.2 29.3 %copy-start.7 = (f32[2,768]{1,0:T(2,128)S(1)}, f32[2,768]{1,0:T(2,128)}, u32[]{:S(2)}) copy-start(f32[2,768]{1,0:T(2,128)} %mag_ref.3) | copy-start | bytes 18436
  83.5 20.9 %copy-start.1 = (bf16[2,1024,768]{2,1,0:T(8,128)(2,1)S(1)}, bf16[2,1024,768]{2,1,0:T(8,128)(2,1)}, u32[]{:S(2)}) copy-start(bf16[2,1024,768]{2,1,0:T(8,128)(2,1)} %base_ref.5) | copy-start | bytes 9437188
  83.5 20.9 %copy-start.5 = (bf16[2,1024,64]{1,2,0:T(8,128)(2,1)S(1)}, bf16[2,1024,64]{1,2,0:T(8,128)(2,1)}, u32[]{:S(2)}) copy-start(bf16[2,1024,64]{1,2,0:T(8,128)(2,1)} %param.8) | copy-start | bytes 786436
  106.2 5.7 %collective-permute-start.1 = (f32[128,512]{1,0:T(8,128)S(1)}, f32[128,512]{1,0:T(8,128)S(1)}, u32[]{:S(2)}, u32[]{:S(2)}) collective-permute-start(f32[128,512]{1,0:T(8,128)S(1)} %get-tuple-element.26), channel_id=1, source_target_pairs={{0,8},{8,0},{1,9},{9,1},{2,10},{10,2},{3,11},{11,3},{4,12},{12,4},... | collective-permute-start | bytes 786440 | tf_op jit(solution)/shard_map/ppermute | solution.py:348
  131.9 11.8 %all-to-all-start.3 = ((f32[16,8,768]{2,1,0:T(8,128)}), f32[16,8,768]{2,1,0:T(8,128)S(1)}, u32[]{:S(2)}, u32[]{:S(2)}) async-start(f32[16,8,768]{2,1,0:T(8,128)} %get-tuple-element.29), calls=%async_computation.3 | async-start | bytes 786432 | tf_op jit(solution)/shard_map/all_to_all | solution.py:352
  135.5 7.0 %collective-permute-start.2 = (f32[8,512]{1,0:T(8,128)S(1)}, f32[8,512]{1,0:T(8,128)S(1)}, u32[]{:S(2)}, u32[]{:S(2)}) collective-permute-start(f32[8,512]{1,0:T(8,128)S(1)} %reduce_sum.9), channel_id=1, source_target_pairs={{0,256},{256,0},{1,257},{257,1},{2,258},{258,2},{3,259},{259,3},{4... | collective-permute-start | bytes 49160 | tf_op jit(solution)/shard_map/ppermute | solution.py:353
  167.8 9.9 %collective-permute-start.3 = (f32[128,512]{1,0:T(8,128)S(1)}, f32[128,512]{1,0:T(8,128)S(1)}, u32[]{:S(2)}, u32[]{:S(2)}) collective-permute-start(f32[128,512]{1,0:T(8,128)S(1)} %bitcast.18), channel_id=1, source_target_pairs={{0,8},{8,0},{1,9},{9,1},{2,10},{10,2},{3,11},{11,3},{4,12},{12,4},... | collective-permute-start | bytes 786440 | tf_op jit(solution)/shard_map/ppermute | solution.py:357

commit v4 on v3

--- a/solution.py
+++ b/solution.py
@@ -9,7 +9,8 @@
 
 F32 = jnp.float32
 BF16 = jnp.bfloat16
-GROUP = ("dp", "tensor")
+WIDTH = ("x", "y")
+GROUP = ("x", "y", "dp")
 PARAMS = pltpu.CompilerParams(vmem_limit_bytes=24 * 2**20)
 VMEM = pl.BlockSpec(memory_space=pltpu.VMEM)
 SMEM = pl.BlockSpec(memory_space=pltpu.SMEM)
@@ -38,6 +39,11 @@
 def split(x):
     hi = x.astype(BF16)
     return hi, (x - hi.astype(F32)).astype(BF16)
+
+
+def member_of(owner):
+    y, x = divmod(owner, 4)
+    return x * 2 + y
 
 
 def dot(x, y, dims=((1,), (0,))):
@@ -92,7 +98,8 @@
                 lanes = slice(2 * columns, 2 * columns + rank)
             peak = peak_of(value)
             code = encode(value, peak).astype(BF16)
-            out_ref[:, where, lanes] = code.reshape(shards, half, value.shape[1])
+            for owner in range(shards):
+                out_ref[member_of(owner), where, lanes] = code[half * owner : half * (owner + 1)]
             peaks = jnp.where(line == row, peak, peaks)
             row += 1
     tail = jnp.concatenate([extra_ref[...], peaks], axis=0).astype(BF16)
@@ -212,7 +219,7 @@
         grad_m = m_row / norm
         grad_m_ref[k : k + 1, :] = grad_m
         coeff_ref[k : k + 1, :] = -grad_m * mag_ref[k : k + 1, :] / (norm * norm)
-    coeff = jnp.where(place_ref[0] == 0, coeff_ref[0:1, :], coeff_ref[1:2, :])
+    coeff = jnp.where(place_ref[2] < 2, coeff_ref[0:1, :], coeff_ref[1:2, :])
     tokens = [jnp.zeros((rows, 128), F32)] * tiles
     crosses = [jnp.zeros((rows, 128), F32)] * tiles
     for j in range(members):
@@ -222,7 +229,7 @@
         cross = decode(blocks[rows * tiles : height - rows], peaks[1:2, 0:1])
         for i in range(tiles):
             tokens[i] = tokens[i] + token[rows * i : rows * (i + 1)]
-        first = j * 2 // members * (tiles // 2)
+        first = j % 2 * (tiles // 2)
         for i in range(tiles // 2):
             crosses[first + i] = crosses[first + i] + cross[rows * i : rows * (i + 1)]
     for i in range(tiles):
@@ -244,7 +251,7 @@
     backs = []
     lane = lax.broadcasted_iota(jnp.int32, (1, 2 * rank), 1)
     for j in range(shards):
-        source = dp * shards + j
+        source = member_of(j) * 2 + dp
         peaks = got_ref[source, at_back - 48 : at_back - 32, :].astype(F32)
         peak = jnp.where(lane < rank, peaks[10:11, 0:1], peaks[11:12, 0:1])
         backs.append(decode(got_ref[source, at_back:, :], peak))
@@ -270,6 +277,42 @@
     theirs_ref[...] = sum_ref[:, pl.ds(pl.multiple_of((1 - core) * width, width), width)]
 
 
+def sum_kernel(mine_ref, theirs_ref, out_ref):
+    zs, rows, lanes = out_ref.shape
+    part = mine_ref[...] + theirs_ref[...]
+    peak = peak_of(part)
+    out_ref[:, :, : lanes - 128] = encode(part, peak).reshape(zs, rows, lanes - 128).astype(BF16)
+    out_ref[:, :, lanes - 128 :] = jnp.broadcast_to(peak, (zs, rows, 128)).astype(BF16)
+
+
+def decoded(got_ref):
+    lanes = got_ref.shape[2] - 128
+    peaks = got_ref[:, :, lanes:].astype(F32)
+    return decode(got_ref[:, :, :lanes], peaks[:, 0:1, 0:1])
+
+
+def piece_kernel(got_ref, out_ref):
+    out_ref[...] = jnp.sum(decoded(got_ref), axis=0)
+
+
+def spread_kernel(mine_ref, theirs_ref, out_ref):
+    zs, rows, lanes = out_ref.shape
+    piece = mine_ref[...] + theirs_ref[...]
+    peak = peak_of(piece)
+    code = jnp.concatenate([encode(piece, peak), jnp.broadcast_to(peak, (rows, 128))], axis=1)
+    out_ref[...] = jnp.broadcast_to(code[None], (zs, rows, lanes)).astype(BF16)
+
+
+def last_kernel(place_ref, own_ref, other_ref, rows_ref, grad_a_ref, grad_b_ref):
+    core = place_ref[1]
+    grad_a_ref[...] = rows_ref[...]
+    rows, columns = grad_b_ref.shape
+    width = columns // 2
+    for side, ref in ((core, own_ref), (1 - core, other_ref)):
+        lanes = pl.ds(pl.multiple_of(side * width, width), width)
+        grad_b_ref[:, lanes] = decoded(ref).reshape(rows, width)
+
+
 def call(kernel, outs, in_specs, flops=0, size=0, scratch=()):
     return pl.pallas_call(
         kernel,
@@ -291,7 +334,7 @@
     core = lax.axis_index("core")
     depth, columns = base.shape[1:]
     rank = a.shape[1]
-    shards = lax.axis_size("tensor")
+    shards = lax.axis_size(WIDTH)
     members = 2 * shards
     zs = lax.axis_size("z")
     own = 2 * zs * tokens.shape[0] // shards
@@ -299,7 +342,7 @@
     tiles = columns // 128
     swap = [(0, 1), (1, 0)]
     bt = jnp.swapaxes(b, 1, 2)
-    place = jnp.stack([dp, core]).astype(jnp.int32)
+    place = jnp.stack([dp, core, lax.axis_index("x")]).astype(jnp.int32)
 
     g_own = lax.all_gather(tokens, "z", axis=0, tiled=True)
     g_other = lax.ppermute(g_own, "core", swap)
@@ -318,7 +361,7 @@
         size=8 * 2**20,
     )(g_own, g_other, base, bt.reshape(2 * rank, depth), extra)
     payload, place = lax.optimization_barrier((payload, place))
-    got = lax.all_to_all(payload, "tensor", 0, 0)
+    got = lax.all_to_all(payload, WIDTH, 0, 0)
 
     height = rows * (tiles + tiles // 2 + 1) + 32 + own
     sends, norm = call(
@@ -345,40 +388,46 @@
         scratch=[pltpu.VMEM((2 * rank, depth), F32)],
     )(place, got, coeff, g_own, g_other, base, bt, a)
 
-    part = mine + lax.ppermute(theirs, "core", swap)
-    chunks = part.reshape(zs, 2 * rank // zs, depth // 2)
-    piece = jnp.sum(lax.all_to_all(chunks, "z", 0, 0), axis=0)
+    theirs = lax.ppermute(theirs, "core", swap)
+    dims = (zs, 2 * rank // zs, depth // 2 + 128)
+    chunks = call(sum_kernel, shape(dims, BF16), [VMEM] * 2, size=2**20)(mine, theirs)
+    got = lax.all_to_all(chunks, "z", 0, 0)
+    piece = call(piece_kernel, shape((dims[1], depth // 2)), [VMEM], size=2**18)(got)
     piece, a_rows = lax.optimization_barrier((piece, a_rows))
-    grad_a = lax.all_to_all(a_rows, GROUP, 0, 0).reshape(2, rank, columns)
-    piece = piece + lax.ppermute(piece, "dp", swap)
-    piece, grad_a = lax.optimization_barrier((piece, grad_a))
-    full = lax.all_to_all(jnp.broadcast_to(piece[None], chunks.shape), "z", 0, 0)
-    full = full.reshape(2 * rank, depth // 2)
+    grad_a = lax.all_to_all(a_rows, GROUP, 0, 0).reshape(2 * rank, columns)
+    theirs = lax.ppermute(piece, "dp", swap)
+    chunks = call(spread_kernel, shape(dims, BF16), [VMEM] * 2, size=2**18)(piece, theirs)
+    chunks, grad_a = lax.optimization_barrier((chunks, grad_a))
+    full = lax.all_to_all(chunks, "z", 0, 0)
     other = lax.ppermute(full, "core", swap)
-    grad_b = jnp.where(
-        place[1] == 0, jnp.concatenate([full, other], axis=1), jnp.concatenate([other, full], axis=1)
-    )
-    return grad_a, jnp.swapaxes(grad_b.reshape(2, rank, depth), 1, 2), grad_m
+    grad_a, grad_b = call(
+        last_kernel,
+        [shape((2 * rank, columns)), shape((2 * rank, depth))],
+        [SMEM] + [VMEM] * 3,
+        size=2**21,
+    )(place, full, other, grad_a)
+    grad_b = jnp.swapaxes(grad_b.reshape(2, rank, depth), 1, 2)
+    return grad_a.reshape(2, rank, columns), grad_b, grad_m
 
 
 def solution(mesh):
     sizes = mesh.shape
     fine = Mesh(
-        mesh.devices.reshape(sizes["dp"], sizes["fsdp"] // 2, 2, sizes["tensor"]),
-        ("dp", "z", "core", "tensor"),
+        mesh.devices.reshape(sizes["dp"], sizes["fsdp"] // 2, 2, 2, sizes["tensor"] // 2),
+        ("dp", "z", "core", "y", "x"),
     )
-    fsdp = ("z", "core")
+    fsdp, tensor = ("z", "core"), ("y", "x")
     return jax.shard_map(
         per_device,
         mesh=fine,
         in_specs=(
-            P(("dp",) + fsdp, "tensor"),
-            P(None, "tensor", fsdp),
-            P(None, "tensor", None),
+            P(("dp",) + fsdp, tensor),
+            P(None, tensor, fsdp),
+            P(None, tensor, None),
             P(None, None, fsdp),
             P(None, fsdp),
-            P(GROUP, fsdp),
+            P(("dp",) + tensor, fsdp),
         ),
-        out_specs=(P(None, None, fsdp), P(None, "tensor", None), P(None, fsdp)),
+        out_specs=(P(None, None, fsdp), P(None, tensor, None), P(None, fsdp)),
         check_vma=False,
     )

time: 180 us -> 173 us (0.961)
  blocking collectives: 121 us -> 116 us
  starting transfers between devices: 31.6 us -> 29.4 us
  Pallas kernels: 14.3 us -> 16.5 us
    all_to_all x3, blocking collectives: 73.3 us -> 67.7 us  [the longest x1 28.5 us: per_device(): got = lax.all_to_all(payload, WIDTH, 0, 0)]
    ppermute x1, starting transfers between devices: 8.68 us -> 6.4 us  [per_device(): other = lax.ppermute(full, 'core', swap)]
    pallas_call x0 -> x4, Pallas kernels: none -> 2.21 us  [the longest x1 1.68 us: per_device(): call(last_kernel, [shape((2 * rank, columns)), shape((2 * rank, depth))],...]
    unnamed x17 -> x16, local copies, waits for them, and re-layouts: 4.54 us -> 3.79 us
  transfers between devices with their start and end apart: 5 -> 5, of which waited for: 3 -> 4; matrix products, arithmetic and copies ran while one was open for 0% -> 0% of each run, Pallas kernels for 2% -> 2%
where the time goes in v4:
time: 173 us; the launch traced here: 172 us
  blocking collectives  116 us (67%)
  starting transfers between devices  29.4 us (17%)
  Pallas kernels  16.5 us (10%)
  waiting for transfers between devices  5.59 us (3%)
  local copies, waits for them, and re-layouts  3.79 us (2%)
    all_gather x1, blocking collectives, per_device(): g_own = lax.all_gather(tokens, 'z', axis=0, tiled=True)  32.1 us
    all_to_all x1, blocking collectives, per_device(): got = lax.all_to_all(payload, WIDTH, 0, 0)  28.5 us
    all_to_all x1, blocking collectives, per_device(): full = lax.all_to_all(chunks, 'z', 0, 0)  20.8 us
    all_to_all x1, blocking collectives, per_device(): got = lax.all_to_all(chunks, 'z', 0, 0)  18.4 us
    all_to_all x1, blocking collectives, per_device(): got = lax.all_to_all(sends, GROUP, 0, 0)  16.2 us
    ppermute x1, starting transfers between devices, per_device(): g_other = lax.ppermute(g_own, 'core', swap)  10.1 us
    ppermute x1, starting transfers between devices, per_device(): other = lax.ppermute(full, 'core', swap)  6.4 us
    ppermute x1, starting transfers between devices, per_device(): theirs = lax.ppermute(piece, 'dp', swap)  4.65 us
  transfers between devices with their start and end apart: 5, of which 4 were waited for; matrix products, arithmetic and copies ran while one was open for 0% of the time, Pallas kernels for 2%

profile of v4, /device:TPU:1, one launch (start us, length us, event | category | flops | bytes accessed | tf_op | source)
XLA Modules:
  0.0 172.1 jit_solution(7828263169630426332)
XLA Ops:
  0.6 32.1 %all_gather.3.own_ref = bf16[256,1024]{1,0:T(8,128)(2,1)S(1)} all-gather(bf16[16,1024]{1,0:T(8,128)(2,1)} %param.6), channel_id=1, replica_groups=mesh['dp'=2,'z'=16,'core'=2,'y'=2,'x'=4] {'z'}, dimensions={0}, use_global_device_ids=true | all-gather | bytes 557056 | tf_op jit(solution)/shard_map/all_gather | solution.py:347
  32.7 10.1 %collective-permute-start = (bf16[256,1024]{1,0:T(8,128)(2,1)S(1)}, bf16[256,1024]{1,0:T(8,128)(2,1)S(1)}, u32[]{:S(2)}, u32[]{:S(2)}) collective-permute-start(bf16[256,1024]{1,0:T(8,128)(2,1)S(1)} %all_gather.3.own_ref), channel_id=1, source_target_pairs={{0,8},{8,0},{1,9},{9,1},{2,10},{10,2},{3,11},{11,3},{4,12},{12,4},... | collective-permute-start | bytes 1572872 | tf_op jit(solution)/shard_map/ppermute | solution.py:348
  42.8 0.0 copy-start
  42.9 1.9 %copy-done = bf16[2,1024,768]{2,1,0:T(8,128)(2,1)S(1)} copy-done((bf16[2,1024,768]{2,1,0:T(8,128)(2,1)S(1)}, bf16[2,1024,768]{2,1,0:T(8,128)(2,1)}, u32[]{:S(2)}) %copy-start) | copy-done | bytes 3145752
  44.7 0.0 copy-start.2
  44.7 0.9 copy-done.2
  45.7 0.0 copy-start.4
  45.7 0.9 copy-done.4
  46.6 3.3 %shard_map.85 = (f32[128,768]{1,0:T(8,128)S(1)}, f32[48,128]{1,0:T(8,128)S(1)}) custom-call(bf16[2,1024,768]{2,1,0:T(8,128)(2,1)S(1)} %copy-done, bf16[2,64,1024]{2,1,0:T(8,128)(2,1)S(1)} %bitcast.12, bf16[2,64,768]{2,1,0:T(8,128)(2,1)S(1)} %copy-done.2), custom_call_target="tpu_custom_call" | custom-call | flops 603979776 | bytes 4194304 | tf_op jit(solution)/shard_map/pallas_call | solution.py:349
  49.9 0.1 pad_add_fusion.place_ref
  50.0 0.0 collective-permute-done.other_ref
  50.0 4.2 %shard_map.86 = bf16[8,64,1792]{2,1,0:T(8,128)(2,1)S(1)} custom-call(bf16[256,1024]{1,0:T(8,128)(2,1)S(1)} %all_gather.3.own_ref, bf16[256,1024]{1,0:T(8,128)(2,1)S(1)} %collective-permute-done.other_ref, bf16[2,1024,768]{2,1,0:T(8,128)(2,1)S(1)} %copy-done, bf16[128,1024]{1,0:T(8,128)(2,1)S(1)} %bitcast.13, f32[48,128]{1,0:T(8,128)S(1)} %get-tuple-element.20.extra_ref), custom_call_target="tpu_custom_call" | custom-call | flops 1744830464 | bytes 8388608 | tf_op jit(solution)/shard_map/pallas_call | solution.py:356
  54.2 0.0 copy-start.3
  54.2 0.0 copy-start.6
  54.2 0.0 copy-start.7
  54.2 28.5 %all_to_all.25.got_ref = bf16[8,64,1792]{2,1,0:T(8,128)(2,1)S(1)} all-to-all(bf16[8,64,1792]{2,1,0:T(8,128)(2,1)S(1)} %shard_map.86), channel_id=1, replica_groups=mesh['dp'=2,'z'=16,'core'=2,'y'=2,'x'=4] {'x','y'}, dimensions={0} | all-to-all | bytes 3670016 | tf_op jit(solution)/shard_map/all_to_all | solution.py:364
  82.8 0.0 copy-done.3
  82.8 0.0 copy-done.6
  82.8 0.0 copy-done.7
  82.8 0.0 copy-start.1
  82.8 0.0 copy-start.5
  82.8 3.3 %shard_map.87 = (bf16[16,176,128]{2,1,0:T(8,128)(2,1)S(1)}, f32[2,768]{1,0:T(2,128)S(1)}) custom-call(s32[3]{0:T(128)S(1)} %pad_add_fusion.place_ref, bf16[8,64,1792]{2,1,0:T(8,128)(2,1)S(1)} %all_to_all.25.got_ref, bf16[64,768]{1,0:T(8,128)(2,1)S(1)} %copy-done.6, bf16[2,64,768]{2,1,0:T(8,128)(2,1)S(1)} %copy-done.3, f32[2,768]{1,0:T(2,128)S(1)} %copy-done.7, ...), custom_call_target="tpu_custom_call" | custom-call | flops 134217728 | bytes 4194304 | tf_op jit(solution)/shard_map/pallas_call | solution.py:367
  86.2 16.2 %all_to_all.26.got_ref = bf16[16,176,128]{2,1,0:T(8,128)(2,1)S(1)} all-to-all(bf16[16,176,128]{2,1,0:T(8,128)(2,1)S(1)} %get-tuple-element.24), channel_id=1, replica_groups=mesh['dp'=2,'z'=16,'core'=2,'y'=2,'x'=4] {'x','y','dp'}, dimensions={0} | all-to-all | bytes 1441792 | tf_op jit(solution)/shard_map/all_to_all | solution.py:374
  102.4 1.6 shard_map.88
  104.0 0.0 copy-done.1
  104.0 0.0 copy-done.5
  104.0 1.8 %shard_map.89 = (f32[128,512]{1,0:T(8,128)S(1)}, f32[128,512]{1,0:T(8,128)S(1)}) custom-call(s32[3]{0:T(128)S(1)} %pad_add_fusion.place_ref, bf16[16,176,128]{2,1,0:T(8,128)(2,1)S(1)} %all_to_all.26.got_ref, f32[2,768]{1,0:T(2,128)S(1)} %get-tuple-element.26.coeff_ref, bf16[256,1024]{1,0:T(8,128)(2,1)S(1)} %all_gather.3.own_ref, ...), custom_call_target="tpu_custom_call" | custom-call | flops 1073741824 | bytes 8388608 | tf_op jit(solution)/shard_map/pallas_call | solution.py:382
  105.8 4.6 %collective-permute-start.1 = (f32[128,512]{1,0:T(8,128)S(1)}, f32[128,512]{1,0:T(8,128)S(1)}, u32[]{:S(2)}, u32[]{:S(2)}) collective-permute-start(f32[128,512]{1,0:T(8,128)S(1)} %get-tuple-element.28), channel_id=1, source_target_pairs={{0,8},{8,0},{1,9},{9,1},{2,10},{10,2},{3,11},{11,3},{4,12},{12,4},... | collective-permute-start | bytes 786440 | tf_op jit(solution)/shard_map/ppermute | solution.py:391
  110.5 1.1 collective-permute-done.1.theirs_ref
  111.6 0.3 shard_map.90
  111.9 18.4 %all_to_all.27.got_ref = bf16[16,8,640]{2,1,0:T(8,128)(2,1)S(1)} all-to-all(bf16[16,8,640]{2,1,0:T(8,128)(2,1)S(1)} %shard_map.90), channel_id=1, replica_groups=mesh['dp'=2,'z'=16,'core'=2,'y'=2,'x'=4] {'z'}, dimensions={0} | all-to-all | bytes 327680 | tf_op jit(solution)/shard_map/all_to_all | solution.py:394
  130.2 0.1 shard_map.91.mine_ref
  130.4 3.6 %all-to-all-start.3 = ((f32[16,8,768]{2,1,0:T(8,128)}), f32[16,8,768]{2,1,0:T(8,128)S(1)}, u32[]{:S(2)}, u32[]{:S(2)}) async-start(f32[16,8,768]{2,1,0:T(8,128)} %get-tuple-element.31), calls=%async_computation.3 | async-start | bytes 786432 | tf_op jit(solution)/shard_map/all_to_all | solution.py:397
  133.9 4.6 %collective-permute-start.2 = (f32[8,512]{1,0:T(8,128)S(1)}, f32[8,512]{1,0:T(8,128)S(1)}, u32[]{:S(2)}, u32[]{:S(2)}) collective-permute-start(f32[8,512]{1,0:T(8,128)S(1)} %shard_map.91.mine_ref), channel_id=1, source_target_pairs={{0,256},{256,0},{1,257},{257,1},{2,258},{258,2},{3,259},{259,3},{4... | collective-permute-start | bytes 49160 | tf_op jit(solution)/shard_map/ppermute | solution.py:398
  138.6 1.4 collective-permute-done.2.theirs_ref
  140.0 0.1 shard_map.92
  140.1 2.0 %all-to-all-done.3 = f32[16,8,768]{2,1,0:T(8,128)S(1)} async-done(((f32[16,8,768]{2,1,0:T(8,128)}), f32[16,8,768]{2,1,0:T(8,128)S(1)}, u32[]{:S(2)}, u32[]{:S(2)}) %all-to-all-start.3) | async-done | bytes 393248 | tf_op jit(solution)/shard_map/all_to_all | solution.py:397
  142.2 20.8 %all_to_all.28.own_ref = bf16[16,8,640]{2,1,0:T(8,128)(2,1)S(1)} all-to-all(bf16[16,8,640]{2,1,0:T(8,128)(2,1)S(1)} %shard_map.92), channel_id=1, replica_groups=mesh['dp'=2,'z'=16,'core'=2,'y'=2,'x'=4] {'z'}, dimensions={0} | all-to-all | bytes 327680 | tf_op jit(solution)/shard_map/all_to_all | solution.py:401
  163.0 6.4 %collective-permute-start.3 = (bf16[16,8,640]{2,1,0:T(8,128)(2,1)S(1)}, bf16[16,8,640]{2,1,0:T(8,128)(2,1)S(1)}, u32[]{:S(2)}, u32[]{:S(2)}) collective-permute-start(bf16[16,8,640]{2,1,0:T(8,128)(2,1)S(1)} %all_to_all.28.own_ref), channel_id=1, source_target_pairs={{0,8},{8,0},{1,9},{9,1},{2,10},{10,2},{3,11},{11,3},{4,12},{12,4},... | collective-permute-start | bytes 491528 | tf_op jit(solution)/shard_map/ppermute | solution.py:402
  169.4 1.0 collective-permute-done.3.other_ref
  170.4 1.7 shard_map.93
Async XLA Ops:
  32.7 17.3 %collective-permute-start = (bf16[256,1024]{1,0:T(8,128)(2,1)S(1)}, bf16[256,1024]{1,0:T(8,128)(2,1)S(1)}, u32[]{:S(2)}, u32[]{:S(2)}) collective-permute-start(bf16[256,1024]{1,0:T(8,128)(2,1)S(1)} %all_gather.3.own_ref), channel_id=1, source_target_pairs={{0,8},{8,0},{1,9},{9,1},{2,10},{10,2},{3,11},{11,3},{4,12},{12,4},... | collective-permute-start | bytes 1572872 | tf_op jit(solution)/shard_map/ppermute | solution.py:348
  42.8 1.9 %copy-start = (bf16[2,1024,768]{2,1,0:T(8,128)(2,1)S(1)}, bf16[2,1024,768]{2,1,0:T(8,128)(2,1)}, u32[]{:S(2)}) copy-start(bf16[2,1024,768]{2,1,0:T(8,128)(2,1)} %base_ref.5) | copy-start | bytes 9437188
  44.7 0.9 copy-start.2
  45.7 0.9 copy-start.4
  54.2 28.6 %copy-start.3 = (bf16[2,64,768]{2,1,0:T(8,128)(2,1)S(1)}, bf16[2,64,768]{2,1,0:T(8,128)(2,1)}, u32[]{:S(2)}) copy-start(bf16[2,64,768]{2,1,0:T(8,128)(2,1)} %a_ref.5) | copy-start | bytes 589828
  54.2 28.6 %copy-start.6 = (bf16[64,768]{1,0:T(8,128)(2,1)S(1)}, bf16[64,768]{1,0:T(8,128)(2,1)}, u32[]{:S(2)}) copy-start(bf16[64,768]{1,0:T(8,128)(2,1)} %cot_ref.1) | copy-start | bytes 294916
  54.2 28.6 %copy-start.7 = (f32[2,768]{1,0:T(2,128)S(1)}, f32[2,768]{1,0:T(2,128)}, u32[]{:S(2)}) copy-start(f32[2,768]{1,0:T(2,128)} %mag_ref.3) | copy-start | bytes 18436
  82.8 21.2 %copy-start.1 = (bf16[2,1024,768]{2,1,0:T(8,128)(2,1)S(1)}, bf16[2,1024,768]{2,1,0:T(8,128)(2,1)}, u32[]{:S(2)}) copy-start(bf16[2,1024,768]{2,1,0:T(8,128)(2,1)} %base_ref.5) | copy-start | bytes 9437188
  82.8 21.2 %copy-start.5 = (bf16[2,1024,64]{1,2,0:T(8,128)(2,1)S(1)}, bf16[2,1024,64]{1,2,0:T(8,128)(2,1)}, u32[]{:S(2)}) copy-start(bf16[2,1024,64]{1,2,0:T(8,128)(2,1)} %param.8) | copy-start | bytes 786436
  105.8 5.8 %collective-permute-start.1 = (f32[128,512]{1,0:T(8,128)S(1)}, f32[128,512]{1,0:T(8,128)S(1)}, u32[]{:S(2)}, u32[]{:S(2)}) collective-permute-start(f32[128,512]{1,0:T(8,128)S(1)} %get-tuple-element.28), channel_id=1, source_target_pairs={{0,8},{8,0},{1,9},{9,1},{2,10},{10,2},{3,11},{11,3},{4,12},{12,4},... | collective-permute-start | bytes 786440 | tf_op jit(solution)/shard_map/ppermute | solution.py:391
  130.4 11.8 %all-to-all-start.3 = ((f32[16,8,768]{2,1,0:T(8,128)}), f32[16,8,768]{2,1,0:T(8,128)S(1)}, u32[]{:S(2)}, u32[]{:S(2)}) async-start(f32[16,8,768]{2,1,0:T(8,128)} %get-tuple-element.31), calls=%async_computation.3 | async-start | bytes 786432 | tf_op jit(solution)/shard_map/all_to_all | solution.py:397
  133.9 6.1 %collective-permute-start.2 = (f32[8,512]{1,0:T(8,128)S(1)}, f32[8,512]{1,0:T(8,128)S(1)}, u32[]{:S(2)}, u32[]{:S(2)}) collective-permute-start(f32[8,512]{1,0:T(8,128)S(1)} %shard_map.91.mine_ref), channel_id=1, source_target_pairs={{0,256},{256,0},{1,257},{257,1},{2,258},{258,2},{3,259},{259,3},{4... | collective-permute-start | bytes 49160 | tf_op jit(solution)/shard_map/ppermute | solution.py:398
  163.0 7.4 %collective-permute-start.3 = (bf16[16,8,640]{2,1,0:T(8,128)(2,1)S(1)}, bf16[16,8,640]{2,1,0:T(8,128)(2,1)S(1)}, u32[]{:S(2)}, u32[]{:S(2)}) collective-permute-start(bf16[16,8,640]{2,1,0:T(8,128)(2,1)S(1)} %all_to_all.28.own_ref), channel_id=1, source_target_pairs={{0,8},{8,0},{1,9},{9,1},{2,10},{10,2},{3,11},{11,3},{4,12},{12,4},... | collective-permute-start | bytes 491528 | tf_op jit(solution)/shard_map/ppermute | solution.py:402

commit v5 on v4

--- a/solution.py
+++ b/solution.py
@@ -59,7 +59,6 @@
     rank = a_ref.shape[1]
     tiles = columns // 128
     step = 256
-    extra_ref[...] = jnp.zeros_like(extra_ref)
     for k in range(2):
         sq = jnp.zeros((1, columns), F32)
         cross = jnp.zeros((rank, columns), F32)
@@ -71,7 +70,7 @@
             hi, lo = split(combined)
             cross += dot(bt, hi) + dot(bt, lo)
         cross_ref[k * rank : (k + 1) * rank, :] = cross
-        for piece in range(3):
+        for piece in range(2):
             part = sq.astype(BF16).astype(F32)
             sq = sq - part
             for i in range(tiles):
@@ -80,61 +79,60 @@
 
 
 def forward_kernel(own_ref, other_ref, base_ref, bt_ref, extra_ref, out_ref):
-    shards, owned, _ = out_ref.shape
+    shards = out_ref.shape[0]
     columns = base_ref.shape[2]
-    half = owned // 2
-    rank = bt_ref.shape[0]
-    peaks = jnp.zeros((16, 128), F32)
-    line = lax.broadcasted_iota(jnp.int32, (16, 128), 0)
-    row = 0
+    half = own_ref.shape[0] // shards
+    owned = 2 * half
+    tiles = columns // 128
+    peaks = jnp.zeros((8, 128), F32)
+    line = lax.broadcasted_iota(jnp.int32, (8, 128), 0)
     for side, ref in enumerate((own_ref, other_ref)):
-        where = slice(side * half, (side + 1) * half)
         for k in range(3):
-            if k < 2:
-                value = dot(ref[...], base_ref[k])
-                lanes = slice(k * columns, (k + 1) * columns)
-            else:
-                value = dot(ref[...], bt_ref[...], NT)
-                lanes = slice(2 * columns, 2 * columns + rank)
+            value = dot(ref[...], base_ref[k]) if k < 2 else dot(ref[...], bt_ref[...], NT)
             peak = peak_of(value)
             code = encode(value, peak).astype(BF16)
             for owner in range(shards):
-                out_ref[member_of(owner), where, lanes] = code[half * owner : half * (owner + 1)]
-            peaks = jnp.where(line == row, peak, peaks)
-            row += 1
-    tail = jnp.concatenate([extra_ref[...], peaks], axis=0).astype(BF16)
-    out_ref[:, :, 2 * columns + rank :] = jnp.broadcast_to(tail[None], (shards,) + tail.shape)
+                for i in range(value.shape[1] // 128):
+                    at = (tiles * k + i) * owned + side * half
+                    out_ref[member_of(owner), at : at + half, :] = code[
+                        half * owner : half * (owner + 1), 128 * i : 128 * (i + 1)
+                    ]
+            peaks = jnp.where(line == 3 * side + k, peak, peaks)
+    rest = jnp.concatenate([extra_ref[...], peaks], axis=0).astype(BF16)
+    out_ref[:, (2 * tiles + 1) * owned :, :] = jnp.broadcast_to(rest[None], (shards,) + rest.shape)
 
 
 def local_kernel(place_ref, got_ref, cot_ref, a_ref, mag_ref, cross_ref, out_ref, norm_ref):
     dp, core = place_ref[0], place_ref[1]
-    shards, owned, _ = got_ref.shape
+    shards = got_ref.shape[0]
     rank, columns = a_ref.shape[1:]
+    owned = cot_ref.shape[0]
     tiles = columns // 128
     half = owned // 2
-    tail = 2 * columns + 2 * rank
-    peak_rows = 3 * 2 * tiles + 12
-
+    at_extra = (2 * tiles + 1) * owned
+
+    rests = [got_ref[source, at_extra:, :].astype(F32) for source in range(shards)]
     totals = []
     for k in range(3):
-        lanes = slice(k * columns, (k + 1) * columns) if k < 2 else slice(2 * columns, tail)
         sides = []
         for side in range(2):
-            total = None
-            for source in range(shards):
-                peaks = got_ref[source, peak_rows : peak_rows + 16, tail:].astype(F32)
-                at = 3 * side + k
-                value = decode(
-                    got_ref[source, side * half : (side + 1) * half, lanes],
-                    peaks[at : at + 1, 0:1],
-                )
-                total = value if total is None else total + value
-            sides.append(total)
+            row = 4 * tiles + 3 * side + k
+            parts = []
+            for i in range(tiles if k < 2 else 1):
+                at = (tiles * k + i) * owned + side * half
+                total = None
+                for source in range(shards):
+                    value = decode(
+                        got_ref[source, at : at + half, :], rests[source][row : row + 1, 0:1]
+                    )
+                    total = value if total is None else total + value
+                parts.append(total)
+            sides.append(jnp.concatenate(parts, axis=1) if k < 2 else parts[0])
         totals.append(jnp.concatenate(sides, axis=0))
-    extra = got_ref[0, :48, tail:].astype(F32)
+    extra = rests[0]
     for source in range(1, shards):
-        extra += got_ref[source, :48, tail:].astype(F32)
-    pieces = extra[24:36] + extra[12:24] + extra[0:12]
+        extra = extra + rests[source]
+    pieces = extra[2 * tiles : 4 * tiles] + extra[: 2 * tiles]
 
     low = totals[2]
     low_hi, low_lo = split(low)
@@ -165,7 +163,6 @@
     douts = (cot * up * sig * (1.0 + gate * (1.0 - sig)), cot * gate * sig)
     members = out_ref.shape[0]
     rows = 2 * rank // members
-    line = lax.broadcasted_iota(jnp.int32, (rows, 128), 0)
     codes, peaks, back_codes, back_peaks, ms = [], [], [], [], []
     for k in range(2):
         mine = slice(k * rank, (k + 1) * rank)
@@ -181,6 +178,17 @@
         codes.append((encode(grad_a, peaks[k][0]), encode(cross, peaks[k][1])))
         back_peaks.append(peak_of(back))
         back_codes.append(encode(back, back_peaks[k]))
+    m_peaks = [peak_of(m) for m in ms]
+    m_codes = [
+        encode(m, peak)[:, 128 * i : 128 * (i + 1)]
+        for m, peak in zip(ms, m_peaks)
+        for i in range(tiles)
+    ]
+    first_half = lax.broadcasted_iota(jnp.int32, (1, 128), 1) < 64
+    pair = lambda x, y: jnp.where(first_half, x, y)
+    ends = [pair(*back_peaks), pair(*m_peaks), jnp.zeros((1, 128), F32)]
+    spare = m_codes[rows:]
+    at_back = rows * (tiles + tiles // 2 + 1)
     for j in range(members):
         k, at = divmod(j * rows, rank)
         blocks = [
@@ -188,45 +196,26 @@
             for code in codes[k]
             for i in range(code.shape[1] // 128)
         ]
-        tail_block = jnp.zeros((rows, 128), F32)
-        for row, peak in enumerate(peaks[k] + tuple(back_peaks)):
-            tail_block = jnp.where(line == row, peak, tail_block)
-        blocks.append(tail_block)
+        blocks.append(jnp.concatenate(spare + [pair(*peaks[k])] + ends, axis=0))
         for i in range(0, len(blocks), 2):
-            pair = jnp.concatenate(blocks[i : i + 2], axis=0).astype(BF16)
-            out_ref[j, rows * i : rows * (i + 2), :] = pair
+            two = jnp.concatenate(blocks[i : i + 2], axis=0).astype(BF16)
+            out_ref[j, rows * i : rows * (i + 2), :] = two
+    rest = jnp.concatenate([jnp.concatenate(back_codes, axis=1)] + m_codes[:rows], axis=0).astype(BF16)
+    out_ref[:, at_back:, :] = jnp.broadcast_to(rest[None], (members,) + rest.shape)
+
+
+def rows_kernel(place_ref, got_ref, coeff_ref, rows_ref):
+    members, rows, columns = rows_ref.shape
+    tiles = columns // 128
     height = rows * (tiles + tiles // 2 + 1)
-    lines = []
-    for piece in range(2):
-        for k in range(2):
-            part = ms[k].astype(BF16).astype(F32)
-            ms[k] = ms[k] - part
-            lines += [part[:, 128 * i : 128 * (i + 1)] for i in range(tiles)]
-    lines.append(jnp.zeros((32 - len(lines), 128), F32))
-    rest = jnp.concatenate(lines + [jnp.concatenate(back_codes, axis=1)], axis=0).astype(BF16)
-    out_ref[:, height:, :] = jnp.broadcast_to(rest[None], (members,) + rest.shape)
-
-
-def coefficient_kernel(place_ref, got_ref, norm_ref, mag_ref, rows_ref, grad_m_ref, coeff_ref):
-    members, rows, columns = rows_ref.shape
-    tiles = columns // 128
-    height = rows * (tiles + tiles // 2 + 1)
-    m = jnp.sum(got_ref[:, height : height + 32, :].astype(F32), axis=0)
-    m = m[: 2 * tiles] + m[2 * tiles : 4 * tiles]
-    for k in range(2):
-        norm = norm_ref[k : k + 1, :]
-        m_row = jnp.concatenate([m[tiles * k + i : tiles * k + i + 1] for i in range(tiles)], axis=1)
-        grad_m = m_row / norm
-        grad_m_ref[k : k + 1, :] = grad_m
-        coeff_ref[k : k + 1, :] = -grad_m * mag_ref[k : k + 1, :] / (norm * norm)
     coeff = jnp.where(place_ref[2] < 2, coeff_ref[0:1, :], coeff_ref[1:2, :])
     tokens = [jnp.zeros((rows, 128), F32)] * tiles
     crosses = [jnp.zeros((rows, 128), F32)] * tiles
     for j in range(members):
         blocks = got_ref[j, :height, :].astype(F32)
-        peaks = blocks[height - rows :]
-        token = decode(blocks[: rows * tiles], peaks[0:1, 0:1])
-        cross = decode(blocks[rows * tiles : height - rows], peaks[1:2, 0:1])
+        peaks = blocks[height - 4 : height - 3]
+        token = decode(blocks[: rows * tiles], peaks[:, 0:1])
+        cross = decode(blocks[rows * tiles : height - rows], peaks[:, 64:65])
         for i in range(tiles):
             tokens[i] = tokens[i] + token[rows * i : rows * (i + 1)]
         first = j % 2 * (tiles // 2)
@@ -239,22 +228,38 @@
 
 
 def width_kernel(
-    place_ref, got_ref, coeff_ref, own_ref, other_ref, base_ref, bt_ref, a_ref, mine_ref, theirs_ref, sum_ref
+    place_ref, got_ref, norm_ref, mag_ref, own_ref, other_ref, base_ref, bt_ref, a_ref,
+    mine_ref, theirs_ref, grad_m_ref, coeff_ref, sum_ref,
 ):
     dp, core = place_ref[0], place_ref[1]
     members = got_ref.shape[0]
     shards = members // 2
-    rank = a_ref.shape[1]
+    rank, columns = a_ref.shape[1:]
+    tiles = columns // 128
     owned = 2 * own_ref.shape[0] // shards
     half = owned // 2
-    at_back = got_ref.shape[1] - owned
+    height = got_ref.shape[1]
+    at_back = height - 8 - owned
+    line = lax.broadcasted_iota(jnp.int32, (2 * tiles, 1), 0)
+    m = None
+    for j in range(members):
+        ends = got_ref[j, at_back - 16 : at_back, :].astype(F32)[8:]
+        code = jnp.concatenate([got_ref[j, height - 8 :, :].astype(F32), ends[:4]], axis=0)
+        part = decode(code, jnp.where(line < tiles, ends[6:7, 0:1], ends[6:7, 64:65]))
+        m = part if m is None else m + part
+    for k in range(2):
+        norm = norm_ref[k : k + 1, :]
+        m_row = jnp.concatenate([m[tiles * k + i : tiles * k + i + 1] for i in range(tiles)], axis=1)
+        grad_m = m_row / norm
+        grad_m_ref[k : k + 1, :] = grad_m
+        coeff_ref[k : k + 1, :] = -grad_m * mag_ref[k : k + 1, :] / (norm * norm)
     backs = []
     lane = lax.broadcasted_iota(jnp.int32, (1, 2 * rank), 1)
     for j in range(shards):
         source = member_of(j) * 2 + dp
-        peaks = got_ref[source, at_back - 48 : at_back - 32, :].astype(F32)
-        peak = jnp.where(lane < rank, peaks[10:11, 0:1], peaks[11:12, 0:1])
-        backs.append(decode(got_ref[source, at_back:, :], peak))
+        ends = got_ref[source, at_back - 16 : at_back, :].astype(F32)
+        peak = jnp.where(lane < rank, ends[13:14, 0:1], ends[13:14, 64:65])
+        backs.append(decode(got_ref[source, at_back : at_back + owned, :], peak))
     total = None
     for side, ref in enumerate((own_ref, other_ref)):
         back = jnp.concatenate([b[side * half : (side + 1) * half] for b in backs], axis=0)
@@ -348,14 +353,14 @@
     g_other = lax.ppermute(g_own, "core", swap)
     cross, extra = call(
         weights_kernel,
-        [shape((2 * rank, columns)), shape((48, 128))],
+        [shape((2 * rank, columns)), shape((4 * tiles, 128))],
         [VMEM] * 3,
         flops=2 * 2 * depth * columns * rank * 3,
         size=4 * 2**20,
     )(base, bt, a)
     payload = call(
         forward_kernel,
-        shape((shards, own, 2 * columns + 4 * rank), BF16),
+        shape((shards, (2 * tiles + 1) * own + 4 * tiles + 8, 128), BF16),
         [VMEM] * 5,
         flops=2 * shards * own * depth * 2 * (columns + rank),
         size=8 * 2**20,
@@ -363,7 +368,7 @@
     payload, place = lax.optimization_barrier((payload, place))
     got = lax.all_to_all(payload, WIDTH, 0, 0)
 
-    height = rows * (tiles + tiles // 2 + 1) + 32 + own
+    height = rows * (tiles + tiles // 2 + 1) + own + 8
     sends, norm = call(
         local_kernel,
         [shape((members, height, 128), BF16), shape((2, columns))],
@@ -373,20 +378,21 @@
     )(place, got, cotangent, a, magnitude, cross)
     got = lax.all_to_all(sends, GROUP, 0, 0)
 
-    a_rows, grad_m, coeff = call(
-        coefficient_kernel,
-        [shape((members, rows, columns)), shape((2, columns)), shape((2, columns))],
-        [SMEM] + [VMEM] * 3,
-        size=2 * 2**20,
-    )(place, got, norm, magnitude)
-    mine, theirs = call(
+    mine, theirs, grad_m, coeff = call(
         width_kernel,
-        [shape((2 * rank, depth // 2))] * 2,
-        [SMEM] + [VMEM] * 7,
+        [shape((2 * rank, depth // 2))] * 2 + [shape((2, columns))] * 2,
+        [SMEM] + [VMEM] * 8,
         flops=2**30,
         size=8 * 2**20,
         scratch=[pltpu.VMEM((2 * rank, depth), F32)],
-    )(place, got, coeff, g_own, g_other, base, bt, a)
+    )(place, got, norm, magnitude, g_own, g_other, base, bt, a)
+    a_rows = call(
+        rows_kernel,
+        shape((members, rows, columns)),
+        [SMEM] + [VMEM] * 2,
+        flops=2**22,
+        size=2**20,
+    )(place, got, coeff)
 
     theirs = lax.ppermute(theirs, "core", swap)
     dims = (zs, 2 * rank // zs, depth // 2 + 128)

time: 173 us -> 170 us (0.983)
  blocking collectives: 116 us -> 96.1 us
  waiting for transfers between devices: 5.59 us -> 16.3 us
  starting transfers between devices: 29.4 us -> 35.5 us
    all_to_all x1 -> x0, blocking collectives: 18.4 us -> none  [per_device(): got = lax.all_to_all(chunks, 'z', 0, 0)]
    all_to_all x0 -> x1, waiting for transfers between devices: none -> 10.8 us  [per_device(): got = lax.all_to_all(chunks, 'z', 0, 0)]
    all_to_all x0 -> x1, starting transfers between devices: none -> 6.17 us  [per_device(): got = lax.all_to_all(chunks, 'z', 0, 0)]
    unnamed x16 -> x14, local copies, waits for them, and re-layouts: 3.79 us -> 3.79 us
  transfers between devices with their start and end apart: 5 -> 6, of which waited for: 4 -> 5; matrix products, arithmetic and copies ran while one was open for 0% -> 0% of each run, Pallas kernels for 2% -> 3%
where the time goes in v5:
time: 170 us
  blocking collectives  96.1 us (57%)
  starting transfers between devices  35.5 us (21%)
  Pallas kernels  17.3 us (10%)
  waiting for transfers between devices  16.3 us (10%)
  local copies, waits for them, and re-layouts  3.79 us (2%)
    all_gather x1, blocking collectives, per_device(): g_own = lax.all_gather(tokens, 'z', axis=0, tiled=True)  32.1 us
    all_to_all x1, blocking collectives, per_device(): got = lax.all_to_all(payload, WIDTH, 0, 0)  27.4 us
    all_to_all x1, blocking collectives, per_device(): full = lax.all_to_all(chunks, 'z', 0, 0)  20.8 us
    all_to_all x1, blocking collectives, per_device(): got = lax.all_to_all(sends, GROUP, 0, 0)  15.8 us
    all_to_all x1, waiting for transfers between devices, per_device(): got = lax.all_to_all(chunks, 'z', 0, 0)  10.8 us
    ppermute x1, starting transfers between devices, per_device(): g_other = lax.ppermute(g_own, 'core', swap)  10.1 us
    ppermute x1, starting transfers between devices, per_device(): other = lax.ppermute(full, 'core', swap)  6.4 us
    all_to_all x1, starting transfers between devices, per_device(): got = lax.all_to_all(chunks, 'z', 0, 0)  6.17 us
  transfers between devices with their start and end apart: 6, of which 5 were waited for; matrix products, arithmetic and copies ran while one was open for 0% of the time, Pallas kernels for 3%

profile of v5, /device:TPU:1, one launch (start us, length us, event | category | flops | bytes accessed | tf_op | source)
XLA Modules:
  0.0 169.9 jit_solution(10690882788310535397)
XLA Ops:
  0.6 32.1 %all_gather.3.own_ref = bf16[256,1024]{1,0:T(8,128)(2,1)S(1)} all-gather(bf16[16,1024]{1,0:T(8,128)(2,1)} %param.6), channel_id=1, replica_groups=mesh['dp'=2,'z'=16,'core'=2,'y'=2,'x'=4] {'z'}, dimensions={0}, use_global_device_ids=true | all-gather | bytes 557056 | tf_op jit(solution)/shard_map/all_gather | solution.py:352
  32.7 10.1 %collective-permute-start = (bf16[256,1024]{1,0:T(8,128)(2,1)S(1)}, bf16[256,1024]{1,0:T(8,128)(2,1)S(1)}, u32[]{:S(2)}, u32[]{:S(2)}) collective-permute-start(bf16[256,1024]{1,0:T(8,128)(2,1)S(1)} %all_gather.3.own_ref), channel_id=1, source_target_pairs={{0,8},{8,0},{1,9},{9,1},{2,10},{10,2},{3,11},{11,3},{4,12},{12,4},... | collective-permute-start | bytes 1572872 | tf_op jit(solution)/shard_map/ppermute | solution.py:353
  42.8 0.0 copy-start
  42.9 1.9 %copy-done = bf16[2,1024,768]{2,1,0:T(8,128)(2,1)S(1)} copy-done((bf16[2,1024,768]{2,1,0:T(8,128)(2,1)S(1)}, bf16[2,1024,768]{2,1,0:T(8,128)(2,1)}, u32[]{:S(2)}) %copy-start) | copy-done | bytes 3145752
  44.7 0.0 copy-start.2
  44.7 0.9 copy-done.2
  45.7 0.0 copy-start.4
  45.7 0.9 copy-done.4
  46.6 3.2 %shard_map.85 = (f32[128,768]{1,0:T(8,128)S(1)}, f32[24,128]{1,0:T(8,128)S(1)}) custom-call(bf16[2,1024,768]{2,1,0:T(8,128)(2,1)S(1)} %copy-done, bf16[2,64,1024]{2,1,0:T(8,128)(2,1)S(1)} %bitcast.12, bf16[2,64,768]{2,1,0:T(8,128)(2,1)S(1)} %copy-done.2), custom_call_target="tpu_custom_call" | custom-call | flops 603979776 | bytes 4194304 | tf_op jit(solution)/shard_map/pallas_call | solution.py:354
  49.9 0.1 pad_add_fusion.place_ref
  49.9 0.0 collective-permute-done.other_ref
  49.9 4.2 %shard_map.86 = bf16[8,864,128]{2,1,0:T(8,128)(2,1)S(1)} custom-call(bf16[256,1024]{1,0:T(8,128)(2,1)S(1)} %all_gather.3.own_ref, bf16[256,1024]{1,0:T(8,128)(2,1)S(1)} %collective-permute-done.other_ref, bf16[2,1024,768]{2,1,0:T(8,128)(2,1)S(1)} %copy-done, bf16[128,1024]{1,0:T(8,128)(2,1)S(1)} %bitcast.13, f32[24,128]{1,0:T(8,128)S(1)} %get-tuple-element.19.extra_ref), custom_call_target="tpu_custom_call" | custom-call | flops 1744830464 | bytes 8388608 | tf_op jit(solution)/shard_map/pallas_call | solution.py:361
  54.2 0.0 copy-start.3
  54.2 0.0 copy-start.5
  54.2 0.0 copy-start.6
  54.2 27.4 %all_to_all.25.got_ref = bf16[8,864,128]{2,1,0:T(8,128)(2,1)S(1)} all-to-all(bf16[8,864,128]{2,1,0:T(8,128)(2,1)S(1)} %shard_map.86), channel_id=1, replica_groups=mesh['dp'=2,'z'=16,'core'=2,'y'=2,'x'=4] {'x','y'}, dimensions={0} | all-to-all | bytes 3538944 | tf_op jit(solution)/shard_map/all_to_all | solution.py:369
  81.6 0.0 copy-done.3
  81.7 0.0 copy-done.5
  81.7 0.0 copy-done.6
  81.7 0.0 copy-start.1
  81.7 3.4 %shard_map.87 = (bf16[16,152,128]{2,1,0:T(8,128)(2,1)S(1)}, f32[2,768]{1,0:T(2,128)S(1)}) custom-call(s32[3]{0:T(128)S(1)} %pad_add_fusion.place_ref, bf16[8,864,128]{2,1,0:T(8,128)(2,1)S(1)} %all_to_all.25.got_ref, bf16[64,768]{1,0:T(8,128)(2,1)S(1)} %copy-done.5, bf16[2,64,768]{2,1,0:T(8,128)(2,1)S(1)} %copy-done.3, f32[2,768]{1,0:T(2,128)S(1)} %copy-done.6, ...), custom_call_target="tpu_custom_call" | custom-call | flops 134217728 | bytes 4194304 | tf_op jit(solution)/shard_map/pallas_call | solution.py:372
  85.0 15.8 %all_to_all.26.got_ref = bf16[16,152,128]{2,1,0:T(8,128)(2,1)S(1)} all-to-all(bf16[16,152,128]{2,1,0:T(8,128)(2,1)S(1)} %get-tuple-element.23), channel_id=1, replica_groups=mesh['dp'=2,'z'=16,'core'=2,'y'=2,'x'=4] {'x','y','dp'}, dimensions={0} | all-to-all | bytes 1245184 | tf_op jit(solution)/shard_map/all_to_all | solution.py:379
  100.8 0.0 copy-done.1
  100.8 2.0 %shard_map.88 = (f32[128,512]{1,0:T(8,128)S(1)}, f32[128,512]{1,0:T(8,128)S(1)}, f32[2,768]{1,0:T(2,128)}, f32[2,768]{1,0:T(2,128)S(1)}) custom-call(s32[3]{0:T(128)S(1)} %pad_add_fusion.place_ref, bf16[16,152,128]{2,1,0:T(8,128)(2,1)S(1)} %all_to_all.26.got_ref, f32[2,768]{1,0:T(2,128)S(1)} %get-tuple-element.24.norm_ref, f32[2,768]{1,0:T(2,128)S(1)} %copy-done.6, ...), custom_call_target="tpu_custom_call" | custom-call | flops 1073741824 | bytes 8388608 | tf_op jit(solution)/shard_map/pallas_call | solution.py:381
  102.8 4.6 %collective-permute-start.1 = (f32[128,512]{1,0:T(8,128)S(1)}, f32[128,512]{1,0:T(8,128)S(1)}, u32[]{:S(2)}, u32[]{:S(2)}) collective-permute-start(f32[128,512]{1,0:T(8,128)S(1)} %get-tuple-element.26), channel_id=1, source_target_pairs={{0,8},{8,0},{1,9},{9,1},{2,10},{10,2},{3,11},{11,3},{4,12},{12,4},... | collective-permute-start | bytes 786440 | tf_op jit(solution)/shard_map/ppermute | solution.py:397
  107.4 1.1 collective-permute-done.1.theirs_ref
  108.5 0.9 shard_map.89
  109.4 6.2 %all-to-all-start.2 = ((bf16[16,8,640]{2,1,0:T(8,128)(2,1)}), bf16[16,8,640]{2,1,0:T(8,128)(2,1)S(1)}, u32[]{:S(2)}, u32[]{:S(2)}) async-start(bf16[16,8,640]{2,1,0:T(8,128)(2,1)} %shard_map.89), calls=%async_computation.2 | async-start | bytes 327680 | tf_op jit(solution)/shard_map/all_to_all | solution.py:400
  115.6 1.6 shard_map.91
  117.3 10.8 %all-to-all-done.2.got_ref = bf16[16,8,640]{2,1,0:T(8,128)(2,1)S(1)} async-done(((bf16[16,8,640]{2,1,0:T(8,128)(2,1)}), bf16[16,8,640]{2,1,0:T(8,128)(2,1)S(1)}, u32[]{:S(2)}, u32[]{:S(2)}) %all-to-all-start.2) | async-done | bytes 163872 | tf_op jit(solution)/shard_map/all_to_all | solution.py:400
  128.0 0.1 shard_map.90.mine_ref
  128.1 3.6 %all-to-all-start.3 = ((f32[16,8,768]{2,1,0:T(8,128)}), f32[16,8,768]{2,1,0:T(8,128)S(1)}, u32[]{:S(2)}, u32[]{:S(2)}) async-start(f32[16,8,768]{2,1,0:T(8,128)} %shard_map.91), calls=%async_computation.3 | async-start | bytes 786432 | tf_op jit(solution)/shard_map/all_to_all | solution.py:403
  131.7 4.6 %collective-permute-start.2 = (f32[8,512]{1,0:T(8,128)S(1)}, f32[8,512]{1,0:T(8,128)S(1)}, u32[]{:S(2)}, u32[]{:S(2)}) collective-permute-start(f32[8,512]{1,0:T(8,128)S(1)} %shard_map.90.mine_ref), channel_id=1, source_target_pairs={{0,256},{256,0},{1,257},{257,1},{2,258},{258,2},{3,259},{259,3},{4... | collective-permute-start | bytes 49160 | tf_op jit(solution)/shard_map/ppermute | solution.py:404
  136.4 1.4 collective-permute-done.2.theirs_ref
  137.8 0.1 shard_map.92
  137.9 2.0 %all-to-all-done.3 = f32[16,8,768]{2,1,0:T(8,128)S(1)} async-done(((f32[16,8,768]{2,1,0:T(8,128)}), f32[16,8,768]{2,1,0:T(8,128)S(1)}, u32[]{:S(2)}, u32[]{:S(2)}) %all-to-all-start.3) | async-done | bytes 393248 | tf_op jit(solution)/shard_map/all_to_all | solution.py:403
  140.0 20.8 %all_to_all.27.own_ref = bf16[16,8,640]{2,1,0:T(8,128)(2,1)S(1)} all-to-all(bf16[16,8,640]{2,1,0:T(8,128)(2,1)S(1)} %shard_map.92), channel_id=1, replica_groups=mesh['dp'=2,'z'=16,'core'=2,'y'=2,'x'=4] {'z'}, dimensions={0} | all-to-all | bytes 327680 | tf_op jit(solution)/shard_map/all_to_all | solution.py:407
  160.8 6.4 %collective-permute-start.3 = (bf16[16,8,640]{2,1,0:T(8,128)(2,1)S(1)}, bf16[16,8,640]{2,1,0:T(8,128)(2,1)S(1)}, u32[]{:S(2)}, u32[]{:S(2)}) collective-permute-start(bf16[16,8,640]{2,1,0:T(8,128)(2,1)S(1)} %all_to_all.27.own_ref), channel_id=1, source_target_pairs={{0,8},{8,0},{1,9},{9,1},{2,10},{10,2},{3,11},{11,3},{4,12},{12,4},... | collective-permute-start | bytes 491528 | tf_op jit(solution)/shard_map/ppermute | solution.py:408
  167.2 1.0 collective-permute-done.3.other_ref
  168.2 1.7 shard_map.93
Async XLA Ops:
  32.7 17.3 %collective-permute-start = (bf16[256,1024]{1,0:T(8,128)(2,1)S(1)}, bf16[256,1024]{1,0:T(8,128)(2,1)S(1)}, u32[]{:S(2)}, u32[]{:S(2)}) collective-permute-start(bf16[256,1024]{1,0:T(8,128)(2,1)S(1)} %all_gather.3.own_ref), channel_id=1, source_target_pairs={{0,8},{8,0},{1,9},{9,1},{2,10},{10,2},{3,11},{11,3},{4,12},{12,4},... | collective-permute-start | bytes 1572872 | tf_op jit(solution)/shard_map/ppermute | solution.py:353
  42.8 1.9 %copy-start = (bf16[2,1024,768]{2,1,0:T(8,128)(2,1)S(1)}, bf16[2,1024,768]{2,1,0:T(8,128)(2,1)}, u32[]{:S(2)}) copy-start(bf16[2,1024,768]{2,1,0:T(8,128)(2,1)} %base_ref.5) | copy-start | bytes 9437188
  44.7 0.9 copy-start.2
  45.7 0.9 copy-start.4
  54.2 27.5 %copy-start.3 = (bf16[2,64,768]{2,1,0:T(8,128)(2,1)S(1)}, bf16[2,64,768]{2,1,0:T(8,128)(2,1)}, u32[]{:S(2)}) copy-start(bf16[2,64,768]{2,1,0:T(8,128)(2,1)} %a_ref.5) | copy-start | bytes 589828
  54.2 27.5 %copy-start.5 = (bf16[64,768]{1,0:T(8,128)(2,1)S(1)}, bf16[64,768]{1,0:T(8,128)(2,1)}, u32[]{:S(2)}) copy-start(bf16[64,768]{1,0:T(8,128)(2,1)} %cot_ref.1) | copy-start | bytes 294916
  54.2 27.5 %copy-start.6 = (f32[2,768]{1,0:T(2,128)S(1)}, f32[2,768]{1,0:T(2,128)}, u32[]{:S(2)}) copy-start(f32[2,768]{1,0:T(2,128)} %mag_ref.3) | copy-start | bytes 18436
  81.7 19.2 %copy-start.1 = (bf16[2,1024,768]{2,1,0:T(8,128)(2,1)S(1)}, bf16[2,1024,768]{2,1,0:T(8,128)(2,1)}, u32[]{:S(2)}) copy-start(bf16[2,1024,768]{2,1,0:T(8,128)(2,1)} %base_ref.5) | copy-start | bytes 9437188
  102.8 5.7 %collective-permute-start.1 = (f32[128,512]{1,0:T(8,128)S(1)}, f32[128,512]{1,0:T(8,128)S(1)}, u32[]{:S(2)}, u32[]{:S(2)}) collective-permute-start(f32[128,512]{1,0:T(8,128)S(1)} %get-tuple-element.26), channel_id=1, source_target_pairs={{0,8},{8,0},{1,9},{9,1},{2,10},{10,2},{3,11},{11,3},{4,12},{12,4},... | collective-permute-start | bytes 786440 | tf_op jit(solution)/shard_map/ppermute | solution.py:397
  109.4 18.6 %all-to-all-start.2 = ((bf16[16,8,640]{2,1,0:T(8,128)(2,1)}), bf16[16,8,640]{2,1,0:T(8,128)(2,1)S(1)}, u32[]{:S(2)}, u32[]{:S(2)}) async-start(bf16[16,8,640]{2,1,0:T(8,128)(2,1)} %shard_map.89), calls=%async_computation.2 | async-start | bytes 327680 | tf_op jit(solution)/shard_map/all_to_all | solution.py:400
  128.1 11.8 %all-to-all-start.3 = ((f32[16,8,768]{2,1,0:T(8,128)}), f32[16,8,768]{2,1,0:T(8,128)S(1)}, u32[]{:S(2)}, u32[]{:S(2)}) async-start(f32[16,8,768]{2,1,0:T(8,128)} %shard_map.91), calls=%async_computation.3 | async-start | bytes 786432 | tf_op jit(solution)/shard_map/all_to_all | solution.py:403
  131.7 6.1 %collective-permute-start.2 = (f32[8,512]{1,0:T(8,128)S(1)}, f32[8,512]{1,0:T(8,128)S(1)}, u32[]{:S(2)}, u32[]{:S(2)}) collective-permute-start(f32[8,512]{1,0:T(8,128)S(1)} %shard_map.90.mine_ref), channel_id=1, source_target_pairs={{0,256},{256,0},{1,257},{257,1},{2,258},{258,2},{3,259},{259,3},{4... | collective-permute-start | bytes 49160 | tf_op jit(solution)/shard_map/ppermute | solution.py:404
  160.8 7.4 %collective-permute-start.3 = (bf16[16,8,640]{2,1,0:T(8,128)(2,1)S(1)}, bf16[16,8,640]{2,1,0:T(8,128)(2,1)S(1)}, u32[]{:S(2)}, u32[]{:S(2)}) collective-permute-start(bf16[16,8,640]{2,1,0:T(8,128)(2,1)S(1)} %all_to_all.27.own_ref), channel_id=1, source_target_pairs={{0,8},{8,0},{1,9},{9,1},{2,10},{10,2},{3,11},{11,3},{4,12},{12,4},... | collective-permute-start | bytes 491528 | tf_op jit(solution)/shard_map/ppermute | solution.py:408

commit v6 on v5

--- a/solution.py
+++ b/solution.py
@@ -205,7 +205,8 @@
 
 
 def rows_kernel(place_ref, got_ref, coeff_ref, rows_ref):
-    members, rows, columns = rows_ref.shape
+    members = got_ref.shape[0]
+    rows, columns = rows_ref.shape
     tiles = columns // 128
     height = rows * (tiles + tiles // 2 + 1)
     coeff = jnp.where(place_ref[2] < 2, coeff_ref[0:1, :], coeff_ref[1:2, :])
@@ -223,8 +224,7 @@
             crosses[first + i] = crosses[first + i] + cross[rows * i : rows * (i + 1)]
     for i in range(tiles):
         lanes = slice(128 * i, 128 * (i + 1))
-        own = tokens[i] + crosses[i] * coeff[:, lanes]
-        rows_ref[:, :, lanes] = jnp.broadcast_to(own[None], (members, rows, 128))
+        rows_ref[:, lanes] = tokens[i] + crosses[i] * coeff[:, lanes]
 
 
 def width_kernel(
@@ -296,21 +296,33 @@
     return decode(got_ref[:, :, :lanes], peaks[:, 0:1, 0:1])
 
 
-def piece_kernel(got_ref, out_ref):
-    out_ref[...] = jnp.sum(decoded(got_ref), axis=0)
-
-
-def spread_kernel(mine_ref, theirs_ref, out_ref):
+def piece_kernel(got_ref, rows_ref, far_ref, out_ref):
+    rows, width = got_ref.shape[1], got_ref.shape[2] - 128
+    columns = out_ref.shape[1]
+    out_ref[:rows, :width] = jnp.sum(decoded(got_ref), axis=0)
+    out_ref[:rows, width:] = jnp.zeros((rows, columns - width), F32)
+    out_ref[rows : 2 * rows, :] = rows_ref[...]
+    out_ref[2 * rows :, :] = far_ref[...]
+
+
+def spread_kernel(mine_ref, theirs_ref, out_ref, rows_ref):
     zs, rows, lanes = out_ref.shape
-    piece = mine_ref[...] + theirs_ref[...]
+    width = lanes - 128
+    piece = mine_ref[:rows, :width] + theirs_ref[:rows, :width]
     peak = peak_of(piece)
     code = jnp.concatenate([encode(piece, peak), jnp.broadcast_to(peak, (rows, 128))], axis=1)
     out_ref[...] = jnp.broadcast_to(code[None], (zs, rows, lanes)).astype(BF16)
-
-
-def last_kernel(place_ref, own_ref, other_ref, rows_ref, grad_a_ref, grad_b_ref):
-    core = place_ref[1]
-    grad_a_ref[...] = rows_ref[...]
+    rows_ref[: 2 * rows, :] = mine_ref[rows:, :]
+    rows_ref[2 * rows :, :] = theirs_ref[rows:, :]
+
+
+def last_kernel(place_ref, own_ref, other_ref, r0_ref, r1_ref, r2_ref, r3_ref, grad_a_ref, grad_b_ref):
+    core, member = place_ref[1], place_ref[3]
+    count = own_ref.shape[1]
+    for near, ref in enumerate((r0_ref, r1_ref, r2_ref, r3_ref)):
+        for i, far in enumerate((0, 8, 1, 9)):
+            at = pl.multiple_of(jnp.bitwise_xor(member, 2 * near + far) * count, count)
+            grad_a_ref[pl.ds(at, count), :] = ref[count * i : count * (i + 1), :]
     rows, columns = grad_b_ref.shape
     width = columns // 2
     for side, ref in ((core, own_ref), (1 - core, other_ref)):
@@ -347,7 +359,7 @@
     tiles = columns // 128
     swap = [(0, 1), (1, 0)]
     bt = jnp.swapaxes(b, 1, 2)
-    place = jnp.stack([dp, core, lax.axis_index("x")]).astype(jnp.int32)
+    place = jnp.stack([dp, core, lax.axis_index("x"), lax.axis_index(GROUP)]).astype(jnp.int32)
 
     g_own = lax.all_gather(tokens, "z", axis=0, tiled=True)
     g_other = lax.ppermute(g_own, "core", swap)
@@ -388,7 +400,7 @@
     )(place, got, norm, magnitude, g_own, g_other, base, bt, a)
     a_rows = call(
         rows_kernel,
-        shape((members, rows, columns)),
+        shape((rows, columns)),
         [SMEM] + [VMEM] * 2,
         flops=2**22,
         size=2**20,
@@ -398,20 +410,26 @@
     dims = (zs, 2 * rank // zs, depth // 2 + 128)
     chunks = call(sum_kernel, shape(dims, BF16), [VMEM] * 2, size=2**20)(mine, theirs)
     got = lax.all_to_all(chunks, "z", 0, 0)
-    piece = call(piece_kernel, shape((dims[1], depth // 2)), [VMEM], size=2**18)(got)
-    piece, a_rows = lax.optimization_barrier((piece, a_rows))
-    grad_a = lax.all_to_all(a_rows, GROUP, 0, 0).reshape(2 * rank, columns)
+
+    def across(value, flip):
+        return lax.ppermute(value, ("y", "x"), [(i, i ^ flip) for i in range(shards)])
+
+    piece = call(piece_kernel, shape((3 * rows, columns)), [VMEM] * 3, size=2**18)(
+        got, a_rows, across(a_rows, 2)
+    )
     theirs = lax.ppermute(piece, "dp", swap)
-    chunks = call(spread_kernel, shape(dims, BF16), [VMEM] * 2, size=2**18)(piece, theirs)
-    chunks, grad_a = lax.optimization_barrier((chunks, grad_a))
+    chunks, near = call(
+        spread_kernel, [shape(dims, BF16), shape((4 * rows, columns))], [VMEM] * 2, size=2**18
+    )(piece, theirs)
     full = lax.all_to_all(chunks, "z", 0, 0)
+    full, *near = lax.optimization_barrier((full, near, across(near, 4), across(near, 1), across(near, 5)))
     other = lax.ppermute(full, "core", swap)
     grad_a, grad_b = call(
         last_kernel,
         [shape((2 * rank, columns)), shape((2 * rank, depth))],
-        [SMEM] + [VMEM] * 3,
+        [SMEM] + [VMEM] * 6,
         size=2**21,
-    )(place, full, other, grad_a)
+    )(place, full, other, *near)
     grad_b = jnp.swapaxes(grad_b.reshape(2, rank, depth), 1, 2)
     return grad_a.reshape(2, rank, columns), grad_b, grad_m
 

time: 170 us -> 165 us (0.971)
  blocking collectives: 96.1 us -> 75.3 us
  starting transfers between devices: 35.5 us -> 48.5 us
  waiting for transfers between devices: 16.3 us -> 18.8 us
    all_to_all x1 -> x0, blocking collectives: 20.8 us -> none  [per_device(): full = lax.all_to_all(chunks, 'z', 0, 0)]
    ppermute x0 -> x4, starting transfers between devices: none -> 11.2 us  [across(): lax.ppermute(value, ('y', 'x'), [(i, i ^ flip) for i in range(shards)])]
    ppermute x0 -> x4, waiting for transfers between devices: none -> 6.11 us  [across(): lax.ppermute(value, ('y', 'x'), [(i, i ^ flip) for i in range(shards)])]
    all_to_all x1, waiting for transfers between devices: 10.8 us -> 5.13 us  [per_device(): got = lax.all_to_all(chunks, 'z', 0, 0)]
    all_to_all x1, starting transfers between devices: 3.57 us -> 7.61 us  [per_device(): full = lax.all_to_all(chunks, 'z', 0, 0)]
    ppermute x1, waiting for transfers between devices: 1.4 us -> 4.13 us  [per_device(): theirs = lax.ppermute(piece, 'dp', swap)]
    ppermute x1, starting transfers between devices: 4.65 us -> 2.46 us  [per_device(): theirs = lax.ppermute(piece, 'dp', swap)]
  transfers between devices with their start and end apart: 6 -> 10, of which waited for: 5 -> 8; matrix products, arithmetic and copies ran while one was open for 0% -> 0% of each run, Pallas kernels for 3% -> 2%
where the time goes in v6:
time: 165 us
  blocking collectives  75.3 us (46%)
  starting transfers between devices  48.5 us (29%)
  waiting for transfers between devices  18.8 us (11%)
  Pallas kernels  17.2 us (10%)
  local copies, waits for them, and re-layouts  3.79 us (2%)
    all_gather x1, blocking collectives, per_device(): g_own = lax.all_gather(tokens, 'z', axis=0, tiled=True)  32.1 us
    all_to_all x1, blocking collectives, per_device(): got = lax.all_to_all(payload, WIDTH, 0, 0)  27.4 us
    all_to_all x1, blocking collectives, per_device(): got = lax.all_to_all(sends, GROUP, 0, 0)  15.8 us
    ppermute x4, starting transfers between devices, across(): lax.ppermute(value, ('y', 'x'), [(i, i ^ flip) for i in range(shards)])  11.2 us
    ppermute x1, starting transfers between devices, per_device(): g_other = lax.ppermute(g_own, 'core', swap)  10.1 us
    all_to_all x1, starting transfers between devices, per_device(): full = lax.all_to_all(chunks, 'z', 0, 0)  7.61 us
    ppermute x1, starting transfers between devices, per_device(): other = lax.ppermute(full, 'core', swap)  6.44 us
    all_to_all x1, starting transfers between devices, per_device(): got = lax.all_to_all(chunks, 'z', 0, 0)  6.2 us
  transfers between devices with their start and end apart: 10, of which 8 were waited for; matrix products, arithmetic and copies ran while one was open for 0% of the time, Pallas kernels for 2%

profile of v6, /device:TPU:1, one launch (start us, length us, event | category | flops | bytes accessed | tf_op | source)
XLA Modules:
  0.0 164.5 jit_solution(5747343328278236007)
XLA Ops:
  0.6 32.1 %all_gather.3.own_ref = bf16[256,1024]{1,0:T(8,128)(2,1)S(1)} all-gather(bf16[16,1024]{1,0:T(8,128)(2,1)} %param.6), channel_id=1, replica_groups=mesh['dp'=2,'z'=16,'core'=2,'y'=2,'x'=4] {'z'}, dimensions={0}, use_global_device_ids=true | all-gather | bytes 557056 | tf_op jit(solution)/shard_map/all_gather | solution.py:364
  32.7 10.1 %collective-permute-start = (bf16[256,1024]{1,0:T(8,128)(2,1)S(1)}, bf16[256,1024]{1,0:T(8,128)(2,1)S(1)}, u32[]{:S(2)}, u32[]{:S(2)}) collective-permute-start(bf16[256,1024]{1,0:T(8,128)(2,1)S(1)} %all_gather.3.own_ref), channel_id=1, source_target_pairs={{0,8},{8,0},{1,9},{9,1},{2,10},{10,2},{3,11},{11,3},{4,12},{12,4},... | collective-permute-start | bytes 1572872 | tf_op jit(solution)/shard_map/ppermute | solution.py:365
  42.9 0.0 copy-start
  42.9 1.9 %copy-done = bf16[2,1024,768]{2,1,0:T(8,128)(2,1)S(1)} copy-done((bf16[2,1024,768]{2,1,0:T(8,128)(2,1)S(1)}, bf16[2,1024,768]{2,1,0:T(8,128)(2,1)}, u32[]{:S(2)}) %copy-start) | copy-done | bytes 3145752
  44.7 0.0 copy-start.2
  44.7 0.9 copy-done.2
  45.7 0.0 copy-start.4
  45.7 0.9 copy-done.4
  46.6 3.2 %shard_map.85 = (f32[128,768]{1,0:T(8,128)S(1)}, f32[24,128]{1,0:T(8,128)S(1)}) custom-call(bf16[2,1024,768]{2,1,0:T(8,128)(2,1)S(1)} %copy-done, bf16[2,64,1024]{2,1,0:T(8,128)(2,1)S(1)} %bitcast.11, bf16[2,64,768]{2,1,0:T(8,128)(2,1)S(1)} %copy-done.2), custom_call_target="tpu_custom_call" | custom-call | flops 603979776 | bytes 4194304 | tf_op jit(solution)/shard_map/pallas_call | solution.py:366
  49.9 0.1 pad_add_fusion.place_ref
  49.9 0.0 collective-permute-done.other_ref
  49.9 4.2 %shard_map.86 = bf16[8,864,128]{2,1,0:T(8,128)(2,1)S(1)} custom-call(bf16[256,1024]{1,0:T(8,128)(2,1)S(1)} %all_gather.3.own_ref, bf16[256,1024]{1,0:T(8,128)(2,1)S(1)} %collective-permute-done.other_ref, bf16[2,1024,768]{2,1,0:T(8,128)(2,1)S(1)} %copy-done, bf16[128,1024]{1,0:T(8,128)(2,1)S(1)} %bitcast.12, f32[24,128]{1,0:T(8,128)S(1)} %get-tuple-element.22.extra_ref), custom_call_target="tpu_custom_call" | custom-call | flops 1744830464 | bytes 8388608 | tf_op jit(solution)/shard_map/pallas_call | solution.py:373
  54.2 0.0 copy-start.3
  54.2 0.0 copy-start.5
  54.2 0.0 copy-start.6
  54.2 27.4 %all_to_all.20.got_ref = bf16[8,864,128]{2,1,0:T(8,128)(2,1)S(1)} all-to-all(bf16[8,864,128]{2,1,0:T(8,128)(2,1)S(1)} %shard_map.86), channel_id=1, replica_groups=mesh['dp'=2,'z'=16,'core'=2,'y'=2,'x'=4] {'x','y'}, dimensions={0} | all-to-all | bytes 3538944 | tf_op jit(solution)/shard_map/all_to_all | solution.py:381
  81.7 0.0 copy-done.3
  81.7 0.0 copy-done.5
  81.7 0.0 copy-done.6
  81.7 0.0 copy-start.1
  81.7 3.4 %shard_map.87 = (bf16[16,152,128]{2,1,0:T(8,128)(2,1)S(1)}, f32[2,768]{1,0:T(2,128)S(1)}) custom-call(s32[4]{0:T(128)S(1)} %pad_add_fusion.place_ref, bf16[8,864,128]{2,1,0:T(8,128)(2,1)S(1)} %all_to_all.20.got_ref, bf16[64,768]{1,0:T(8,128)(2,1)S(1)} %copy-done.5, bf16[2,64,768]{2,1,0:T(8,128)(2,1)S(1)} %copy-done.3, f32[2,768]{1,0:T(2,128)S(1)} %copy-done.6, ...), custom_call_target="tpu_custom_call" | custom-call | flops 134217728 | bytes 4194304 | tf_op jit(solution)/shard_map/pallas_call | solution.py:384
  85.0 15.8 %all_to_all.21.got_ref = bf16[16,152,128]{2,1,0:T(8,128)(2,1)S(1)} all-to-all(bf16[16,152,128]{2,1,0:T(8,128)(2,1)S(1)} %get-tuple-element.26), channel_id=1, replica_groups=mesh['dp'=2,'z'=16,'core'=2,'y'=2,'x'=4] {'x','y','dp'}, dimensions={0} | all-to-all | bytes 1245184 | tf_op jit(solution)/shard_map/all_to_all | solution.py:391
  100.9 0.0 copy-done.1
  100.9 2.0 %shard_map.88 = (f32[128,512]{1,0:T(8,128)S(1)}, f32[128,512]{1,0:T(8,128)S(1)}, f32[2,768]{1,0:T(2,128)}, f32[2,768]{1,0:T(2,128)S(1)}) custom-call(s32[4]{0:T(128)S(1)} %pad_add_fusion.place_ref, bf16[16,152,128]{2,1,0:T(8,128)(2,1)S(1)} %all_to_all.21.got_ref, f32[2,768]{1,0:T(2,128)S(1)} %get-tuple-element.27.norm_ref, f32[2,768]{1,0:T(2,128)S(1)} %copy-done.6, ...), custom_call_target="tpu_custom_call" | custom-call | flops 1073741824 | bytes 8388608 | tf_op jit(solution)/shard_map/pallas_call | solution.py:393
  102.8 4.5 %collective-permute-start.1 = (f32[128,512]{1,0:T(8,128)S(1)}, f32[128,512]{1,0:T(8,128)S(1)}, u32[]{:S(2)}, u32[]{:S(2)}) collective-permute-start(f32[128,512]{1,0:T(8,128)S(1)} %get-tuple-element.29), channel_id=1, source_target_pairs={{0,8},{8,0},{1,9},{9,1},{2,10},{10,2},{3,11},{11,3},{4,12},{12,4},... | collective-permute-start | bytes 786440 | tf_op jit(solution)/shard_map/ppermute | solution.py:409
  107.4 1.1 collective-permute-done.1.theirs_ref
  108.5 0.9 shard_map.89
  109.4 6.2 %all-to-all-start.2 = ((bf16[16,8,640]{2,1,0:T(8,128)(2,1)}), bf16[16,8,640]{2,1,0:T(8,128)(2,1)S(1)}, u32[]{:S(2)}, u32[]{:S(2)}) async-start(bf16[16,8,640]{2,1,0:T(8,128)(2,1)} %shard_map.89), calls=%async_computation.2 | async-start | bytes 327680 | tf_op jit(solution)/shard_map/all_to_all | solution.py:412
  115.6 0.9 shard_map.90.rows_ref
  116.5 2.8 %collective-permute-start.2 = (f32[8,768]{1,0:T(8,128)S(1)}, f32[8,768]{1,0:T(8,128)S(1)}, u32[]{:S(2)}, u32[]{:S(2)}) collective-permute-start(f32[8,768]{1,0:T(8,128)S(1)} %shard_map.90.rows_ref), channel_id=1, source_target_pairs={{0,2},{1,3},{2,0},{3,1},{4,6},{5,7},{6,4},{7,5},{8,10},{9,11},{10,... | collective-permute-start | bytes 73736 | tf_op jit(solution)/shard_map/ppermute | solution.py:415
  119.3 3.6 %collective-permute-done.2.far_ref = f32[8,768]{1,0:T(8,128)S(1)} collective-permute-done((f32[8,768]{1,0:T(8,128)S(1)}, f32[8,768]{1,0:T(8,128)S(1)}, u32[]{:S(2)}, u32[]{:S(2)}) %collective-permute-start.2) | collective-permute-done | bytes 24608 | tf_op jit(solution)/shard_map/ppermute | solution.py:415
  122.9 5.1 %all-to-all-done.2.got_ref = bf16[16,8,640]{2,1,0:T(8,128)(2,1)S(1)} async-done(((bf16[16,8,640]{2,1,0:T(8,128)(2,1)}), bf16[16,8,640]{2,1,0:T(8,128)(2,1)S(1)}, u32[]{:S(2)}, u32[]{:S(2)}) %all-to-all-start.2) | async-done | bytes 163872 | tf_op jit(solution)/shard_map/all_to_all | solution.py:412
  128.0 0.1 shard_map.91.mine_ref
  128.2 2.5 %collective-permute-start.3 = (f32[24,768]{1,0:T(8,128)S(1)}, f32[24,768]{1,0:T(8,128)S(1)}, u32[]{:S(2)}, u32[]{:S(2)}) collective-permute-start(f32[24,768]{1,0:T(8,128)S(1)} %shard_map.91.mine_ref), channel_id=1, source_target_pairs={{0,256},{256,0},{1,257},{257,1},{2,258},{258,2},{3,259},{259,3},{4... | collective-permute-start | bytes 221192 | tf_op jit(solution)/shard_map/ppermute | solution.py:420
  130.6 4.1 %collective-permute-done.3.theirs_ref = f32[24,768]{1,0:T(8,128)S(1)} collective-permute-done((f32[24,768]{1,0:T(8,128)S(1)}, f32[24,768]{1,0:T(8,128)S(1)}, u32[]{:S(2)}, u32[]{:S(2)}) %collective-permute-start.3) | collective-permute-done | bytes 73760 | tf_op jit(solution)/shard_map/ppermute | solution.py:420
  134.8 0.8 shard_map.92
  135.6 7.6 %all-to-all-start.3 = ((bf16[16,8,640]{2,1,0:T(8,128)(2,1)}), bf16[16,8,640]{2,1,0:T(8,128)(2,1)S(1)}, u32[]{:S(2)}, u32[]{:S(2)}) async-start(bf16[16,8,640]{2,1,0:T(8,128)(2,1)} %get-tuple-element.31), calls=%async_computation.3 | async-start | bytes 327680 | tf_op jit(solution)/shard_map/all_to_all | solution.py:424
  143.2 2.1 %collective-permute-start.6 = (f32[32,768]{1,0:T(8,128)S(1)}, f32[32,768]{1,0:T(8,128)S(1)}, u32[]{:S(2)}, u32[]{:S(2)}) collective-permute-start(f32[32,768]{1,0:T(8,128)S(1)} %get-tuple-element.34.r0_ref), channel_id=1, source_target_pairs={{0,5},{1,4},{2,7},{3,6},{4,1},{5,0},{6,3},{7,2},{8,13},{9,12},{10,... | collective-permute-start | bytes 294920 | tf_op jit(solution)/shard_map/ppermute | solution.py:415
  145.3 3.2 %collective-permute-start.5 = (f32[32,768]{1,0:T(8,128)S(1)}, f32[32,768]{1,0:T(8,128)S(1)}, u32[]{:S(2)}, u32[]{:S(2)}) collective-permute-start(f32[32,768]{1,0:T(8,128)S(1)} %get-tuple-element.34.r0_ref), channel_id=1, source_target_pairs={{0,1},{1,0},{2,3},{3,2},{4,5},{5,4},{6,7},{7,6},{8,9},{9,8},{10,11... | collective-permute-start | bytes 294920 | tf_op jit(solution)/shard_map/ppermute | solution.py:415
  148.5 3.1 %collective-permute-start.4 = (f32[32,768]{1,0:T(8,128)S(1)}, f32[32,768]{1,0:T(8,128)S(1)}, u32[]{:S(2)}, u32[]{:S(2)}) collective-permute-start(f32[32,768]{1,0:T(8,128)S(1)} %get-tuple-element.34.r0_ref), channel_id=1, source_target_pairs={{0,4},{1,5},{2,6},{3,7},{4,0},{5,1},{6,2},{7,3},{8,12},{9,13},{10,... | collective-permute-start | bytes 294920 | tf_op jit(solution)/shard_map/ppermute | solution.py:415
  151.6 0.0 collective-permute-done.6.r3_ref
  151.6 0.1 collective-permute-done.5.r2_ref
  151.8 2.4 %collective-permute-done.4.r1_ref = f32[32,768]{1,0:T(8,128)S(1)} collective-permute-done((f32[32,768]{1,0:T(8,128)S(1)}, f32[32,768]{1,0:T(8,128)S(1)}, u32[]{:S(2)}, u32[]{:S(2)}) %collective-permute-start.4) | collective-permute-done | bytes 98336 | tf_op jit(solution)/shard_map/ppermute | solution.py:415
  154.1 1.2 all-to-all-done.3.own_ref
  155.4 6.4 %collective-permute-start.7 = (bf16[16,8,640]{2,1,0:T(8,128)(2,1)S(1)}, bf16[16,8,640]{2,1,0:T(8,128)(2,1)S(1)}, u32[]{:S(2)}, u32[]{:S(2)}) collective-permute-start(bf16[16,8,640]{2,1,0:T(8,128)(2,1)S(1)} %all-to-all-done.3.own_ref), channel_id=1, source_target_pairs={{0,8},{8,0},{1,9},{9,1},{2,10},{10,2},{3,11},{11,3},{4,12},{12,4},... | collective-permute-start | bytes 491528 | tf_op jit(solution)/shard_map/ppermute | solution.py:426
  161.8 1.0 collective-permute-done.7.other_ref
  162.8 1.7 %shard_map.93 = (f32[128,768]{1,0:T(8,128)}, f32[128,1024]{1,0:T(8,128)}) custom-call(s32[4]{0:T(128)S(1)} %pad_add_fusion.place_ref, bf16[16,8,640]{2,1,0:T(8,128)(2,1)S(1)} %all-to-all-done.3.own_ref, bf16[16,8,640]{2,1,0:T(8,128)(2,1)S(1)} %collective-permute-done.7.other_ref, f32[32,768]{1,0:T(8,128)S(1)} %get-tuple-element.34.r0_ref, ...), custom_call_target="tpu_custom_call" | custom-call | bytes 2097152 | tf_op jit(solution)/shard_map/pallas_call | solution.py:427
Async XLA Ops:
  32.7 17.3 %collective-permute-start = (bf16[256,1024]{1,0:T(8,128)(2,1)S(1)}, bf16[256,1024]{1,0:T(8,128)(2,1)S(1)}, u32[]{:S(2)}, u32[]{:S(2)}) collective-permute-start(bf16[256,1024]{1,0:T(8,128)(2,1)S(1)} %all_gather.3.own_ref), channel_id=1, source_target_pairs={{0,8},{8,0},{1,9},{9,1},{2,10},{10,2},{3,11},{11,3},{4,12},{12,4},... | collective-permute-start | bytes 1572872 | tf_op jit(solution)/shard_map/ppermute | solution.py:365
  42.9 1.9 %copy-start = (bf16[2,1024,768]{2,1,0:T(8,128)(2,1)S(1)}, bf16[2,1024,768]{2,1,0:T(8,128)(2,1)}, u32[]{:S(2)}) copy-start(bf16[2,1024,768]{2,1,0:T(8,128)(2,1)} %base_ref.5) | copy-start | bytes 9437188
  44.7 0.9 copy-start.2
  45.7 0.9 copy-start.4
  54.2 27.5 %copy-start.3 = (bf16[2,64,768]{2,1,0:T(8,128)(2,1)S(1)}, bf16[2,64,768]{2,1,0:T(8,128)(2,1)}, u32[]{:S(2)}) copy-start(bf16[2,64,768]{2,1,0:T(8,128)(2,1)} %a_ref.5) | copy-start | bytes 589828
  54.2 27.5 %copy-start.5 = (bf16[64,768]{1,0:T(8,128)(2,1)S(1)}, bf16[64,768]{1,0:T(8,128)(2,1)}, u32[]{:S(2)}) copy-start(bf16[64,768]{1,0:T(8,128)(2,1)} %cot_ref.1) | copy-start | bytes 294916
  54.2 27.5 %copy-start.6 = (f32[2,768]{1,0:T(2,128)S(1)}, f32[2,768]{1,0:T(2,128)}, u32[]{:S(2)}) copy-start(f32[2,768]{1,0:T(2,128)} %mag_ref.3) | copy-start | bytes 18436
  81.7 19.2 %copy-start.1 = (bf16[2,1024,768]{2,1,0:T(8,128)(2,1)S(1)}, bf16[2,1024,768]{2,1,0:T(8,128)(2,1)}, u32[]{:S(2)}) copy-start(bf16[2,1024,768]{2,1,0:T(8,128)(2,1)} %base_ref.5) | copy-start | bytes 9437188
  102.8 5.7 %collective-permute-start.1 = (f32[128,512]{1,0:T(8,128)S(1)}, f32[128,512]{1,0:T(8,128)S(1)}, u32[]{:S(2)}, u32[]{:S(2)}) collective-permute-start(f32[128,512]{1,0:T(8,128)S(1)} %get-tuple-element.29), channel_id=1, source_target_pairs={{0,8},{8,0},{1,9},{9,1},{2,10},{10,2},{3,11},{11,3},{4,12},{12,4},... | collective-permute-start | bytes 786440 | tf_op jit(solution)/shard_map/ppermute | solution.py:409
  109.4 18.6 %all-to-all-start.2 = ((bf16[16,8,640]{2,1,0:T(8,128)(2,1)}), bf16[16,8,640]{2,1,0:T(8,128)(2,1)S(1)}, u32[]{:S(2)}, u32[]{:S(2)}) async-start(bf16[16,8,640]{2,1,0:T(8,128)(2,1)} %shard_map.89), calls=%async_computation.2 | async-start | bytes 327680 | tf_op jit(solution)/shard_map/all_to_all | solution.py:412
  116.5 6.4 %collective-permute-start.2 = (f32[8,768]{1,0:T(8,128)S(1)}, f32[8,768]{1,0:T(8,128)S(1)}, u32[]{:S(2)}, u32[]{:S(2)}) collective-permute-start(f32[8,768]{1,0:T(8,128)S(1)} %shard_map.90.rows_ref), channel_id=1, source_target_pairs={{0,2},{1,3},{2,0},{3,1},{4,6},{5,7},{6,4},{7,5},{8,10},{9,11},{10,... | collective-permute-start | bytes 73736 | tf_op jit(solution)/shard_map/ppermute | solution.py:415
  128.2 6.6 %collective-permute-start.3 = (f32[24,768]{1,0:T(8,128)S(1)}, f32[24,768]{1,0:T(8,128)S(1)}, u32[]{:S(2)}, u32[]{:S(2)}) collective-permute-start(f32[24,768]{1,0:T(8,128)S(1)} %shard_map.91.mine_ref), channel_id=1, source_target_pairs={{0,256},{256,0},{1,257},{257,1},{2,258},{258,2},{3,259},{259,3},{4... | collective-permute-start | bytes 221192 | tf_op jit(solution)/shard_map/ppermute | solution.py:420
  135.6 19.8 %all-to-all-start.3 = ((bf16[16,8,640]{2,1,0:T(8,128)(2,1)}), bf16[16,8,640]{2,1,0:T(8,128)(2,1)S(1)}, u32[]{:S(2)}, u32[]{:S(2)}) async-start(bf16[16,8,640]{2,1,0:T(8,128)(2,1)} %get-tuple-element.31), calls=%async_computation.3 | async-start | bytes 327680 | tf_op jit(solution)/shard_map/all_to_all | solution.py:424
  143.2 8.4 %collective-permute-start.6 = (f32[32,768]{1,0:T(8,128)S(1)}, f32[32,768]{1,0:T(8,128)S(1)}, u32[]{:S(2)}, u32[]{:S(2)}) collective-permute-start(f32[32,768]{1,0:T(8,128)S(1)} %get-tuple-element.34.r0_ref), channel_id=1, source_target_pairs={{0,5},{1,4},{2,7},{3,6},{4,1},{5,0},{6,3},{7,2},{8,13},{9,12},{10,... | collective-permute-start | bytes 294920 | tf_op jit(solution)/shard_map/ppermute | solution.py:415
  145.3 6.4 %collective-permute-start.5 = (f32[32,768]{1,0:T(8,128)S(1)}, f32[32,768]{1,0:T(8,128)S(1)}, u32[]{:S(2)}, u32[]{:S(2)}) collective-permute-start(f32[32,768]{1,0:T(8,128)S(1)} %get-tuple-element.34.r0_ref), channel_id=1, source_target_pairs={{0,1},{1,0},{2,3},{3,2},{4,5},{5,4},{6,7},{7,6},{8,9},{9,8},{10,11... | collective-permute-start | bytes 294920 | tf_op jit(solution)/shard_map/ppermute | solution.py:415
  148.5 5.7 %collective-permute-start.4 = (f32[32,768]{1,0:T(8,128)S(1)}, f32[32,768]{1,0:T(8,128)S(1)}, u32[]{:S(2)}, u32[]{:S(2)}) collective-permute-start(f32[32,768]{1,0:T(8,128)S(1)} %get-tuple-element.34.r0_ref), channel_id=1, source_target_pairs={{0,4},{1,5},{2,6},{3,7},{4,0},{5,1},{6,2},{7,3},{8,12},{9,13},{10,... | collective-permute-start | bytes 294920 | tf_op jit(solution)/shard_map/ppermute | solution.py:415
  155.4 7.5 %collective-permute-start.7 = (bf16[16,8,640]{2,1,0:T(8,128)(2,1)S(1)}, bf16[16,8,640]{2,1,0:T(8,128)(2,1)S(1)}, u32[]{:S(2)}, u32[]{:S(2)}) collective-permute-start(bf16[16,8,640]{2,1,0:T(8,128)(2,1)S(1)} %all-to-all-done.3.own_ref), channel_id=1, source_target_pairs={{0,8},{8,0},{1,9},{9,1},{2,10},{10,2},{3,11},{11,3},{4,12},{12,4},... | collective-permute-start | bytes 491528 | tf_op jit(solution)/shard_map/ppermute | solution.py:426

commit v7 on v6

--- a/solution.py
+++ b/solution.py
@@ -1,3 +1,4 @@
+import functools
 import math
 
 import jax
@@ -11,9 +12,9 @@
 BF16 = jnp.bfloat16
 WIDTH = ("x", "y")
 GROUP = ("x", "y", "dp")
-PARAMS = pltpu.CompilerParams(vmem_limit_bytes=24 * 2**20)
 VMEM = pl.BlockSpec(memory_space=pltpu.VMEM)
 SMEM = pl.BlockSpec(memory_space=pltpu.SMEM)
+STEP = 512
 
 BEND = 4096.0
 POWER = 250.0 / math.log2(1.0 + BEND)
@@ -54,51 +55,109 @@
 TN = ((0,), (0,))
 
 
-def weights_kernel(base_ref, bt_ref, a_ref, cross_ref, extra_ref):
+def coded(value, put):
+    peak = peak_of(value)
+    code = encode(value, peak).astype(BF16)
+    for i in range(value.shape[1] // 128):
+        put(i, code[:, 128 * i : 128 * (i + 1)])
+    return peak
+
+
+def own_work(own_ref, base_ref, bt_ref, a_ref, part_ref, cross_ref, info_ref):
     depth, columns = base_ref.shape[1:]
     rank = a_ref.shape[1]
     tiles = columns // 128
-    step = 256
+    shards = part_ref.shape[0]
+    half = own_ref.shape[0] // shards
+
+    def put_at(first):
+        def put(i, code):
+            at = (first + i) * half
+            for owner in range(shards):
+                part_ref[member_of(owner), at : at + half, :] = code[half * owner : half * (owner + 1)]
+
+        return put
+
+    line = lax.broadcasted_iota(jnp.int32, (8, 128), 0)
+    bt = bt_ref[...].reshape(2 * rank, depth)
+    peak = coded(dot(own_ref[...], bt, NT), put_at(2 * tiles))
+    peaks = jnp.where(line == 2, peak, jnp.zeros((8, 128), F32))
     for k in range(2):
-        sq = jnp.zeros((1, columns), F32)
+        sq = jnp.zeros((8, columns), F32)
         cross = jnp.zeros((rank, columns), F32)
-        for at in range(0, depth, step):
-            rows = slice(at, at + step)
+        for at in range(0, depth, STEP):
+            rows = slice(at, at + STEP)
             bt = bt_ref[k, :, rows]
             combined = base_ref[k, rows, :].astype(F32) + dot(bt, a_ref[k], TN)
-            sq += jnp.sum(combined * combined, axis=0, keepdims=True)
+            sq += jnp.sum((combined * combined).reshape(STEP // 8, 8, columns), axis=0)
             hi, lo = split(combined)
             cross += dot(bt, hi) + dot(bt, lo)
         cross_ref[k * rank : (k + 1) * rank, :] = cross
+        sq = jnp.sum(sq, axis=0, keepdims=True)
         for piece in range(2):
             part = sq.astype(BF16).astype(F32)
             sq = sq - part
             for i in range(tiles):
                 row = 2 * tiles * piece + tiles * k + i
-                extra_ref[row : row + 1, :] = part[:, 128 * i : 128 * (i + 1)]
-
-
-def forward_kernel(own_ref, other_ref, base_ref, bt_ref, extra_ref, out_ref):
+                info_ref[row : row + 1, :] = part[:, 128 * i : 128 * (i + 1)]
+        peak = coded(dot(own_ref[...], base_ref[k]), put_at(tiles * k))
+        peaks = jnp.where(line == k, peak, peaks)
+    info_ref[4 * tiles :, :] = peaks
+
+
+def early_kernel(place_ref, *refs):
+    @pl.when(place_ref[1] == 1)
+    def _():
+        own_work(*refs)
+
+
+def late_kernel(place_ref, *refs):
+    @pl.when(place_ref[1] == 0)
+    def _():
+        own_work(*refs)
+
+
+def forward_kernel(
+    place_ref, early_part, early_cross, early_info, late_part, late_cross, late_info, other_ref,
+    base_ref, bt_ref, out_ref, cross_ref, info_ref,
+):
     shards = out_ref.shape[0]
     columns = base_ref.shape[2]
-    half = own_ref.shape[0] // shards
+    half = other_ref.shape[0] // shards
     owned = 2 * half
     tiles = columns // 128
-    peaks = jnp.zeros((8, 128), F32)
-    line = lax.broadcasted_iota(jnp.int32, (8, 128), 0)
-    for side, ref in enumerate((own_ref, other_ref)):
-        for k in range(3):
-            value = dot(ref[...], base_ref[k]) if k < 2 else dot(ref[...], bt_ref[...], NT)
-            peak = peak_of(value)
-            code = encode(value, peak).astype(BF16)
+    info_rows = info_ref.shape[0]
+
+    def take(part_ref, cross_in, info_in):
+        for i in range(2 * tiles + 1):
+            out_ref[:, owned * i : owned * i + half, :] = part_ref[:, half * i : half * (i + 1), :]
+        cross_ref[...] = cross_in[...]
+        info_ref[...] = info_in[...]
+
+    @pl.when(place_ref[1] == 1)
+    def _():
+        take(early_part, early_cross, early_info)
+
+    @pl.when(place_ref[1] == 0)
+    def _():
+        take(late_part, late_cross, late_info)
+
+    def put_at(first):
+        def put(i, code):
+            at = (first + i) * owned + half
             for owner in range(shards):
-                for i in range(value.shape[1] // 128):
-                    at = (tiles * k + i) * owned + side * half
-                    out_ref[member_of(owner), at : at + half, :] = code[
-                        half * owner : half * (owner + 1), 128 * i : 128 * (i + 1)
-                    ]
-            peaks = jnp.where(line == 3 * side + k, peak, peaks)
-    rest = jnp.concatenate([extra_ref[...], peaks], axis=0).astype(BF16)
+                out_ref[member_of(owner), at : at + half, :] = code[half * owner : half * (owner + 1)]
+
+        return put
+
+    line = lax.broadcasted_iota(jnp.int32, (info_rows, 128), 0)
+    info = info_ref[...]
+    peak = coded(dot(other_ref[...], bt_ref[...], NT), put_at(2 * tiles))
+    info = jnp.where(line == info_rows - 3, peak, info)
+    for k in range(2):
+        peak = coded(dot(other_ref[...], base_ref[k]), put_at(tiles * k))
+        info = jnp.where(line == info_rows - 5 + k, peak, info)
+    rest = info.astype(BF16)
     out_ref[:, (2 * tiles + 1) * owned :, :] = jnp.broadcast_to(rest[None], (shards,) + rest.shape)
 
 
@@ -337,7 +396,7 @@
         in_specs=in_specs,
         out_specs=[VMEM] * len(outs) if isinstance(outs, (list, tuple)) else VMEM,
         scratch_shapes=scratch,
-        compiler_params=PARAMS,
+        compiler_params=pltpu.CompilerParams(vmem_limit_bytes=24 * 2**20),
         cost_estimate=pl.CostEstimate(flops=flops, bytes_accessed=size, transcendentals=0),
     )
 
@@ -362,22 +421,36 @@
     place = jnp.stack([dp, core, lax.axis_index("x"), lax.axis_index(GROUP)]).astype(jnp.int32)
 
     g_own = lax.all_gather(tokens, "z", axis=0, tiled=True)
+    g_own, place = lax.optimization_barrier((g_own, place))
+    info_rows = 4 * tiles + 8
+    outs = [
+        shape((shards, (2 * tiles + 1) * own // 2, 128), BF16),
+        shape((2 * rank, columns)),
+        shape((info_rows, 128)),
+    ]
+    early, late = (
+        functools.partial(
+            call,
+            kernel,
+            outs,
+            [SMEM] + [VMEM] * 4,
+            flops=2**30,
+            size=4 * 2**20,
+        )()
+        for kernel in (early_kernel, late_kernel)
+    )
+    first = early(place, g_own, base, bt, a)
+    g_own, first = lax.optimization_barrier((g_own, first))
     g_other = lax.ppermute(g_own, "core", swap)
-    cross, extra = call(
-        weights_kernel,
-        [shape((2 * rank, columns)), shape((4 * tiles, 128))],
-        [VMEM] * 3,
-        flops=2 * 2 * depth * columns * rank * 3,
-        size=4 * 2**20,
-    )(base, bt, a)
-    payload = call(
+    second = late(place, g_own, base, bt, a)
+    payload, cross = call(
         forward_kernel,
-        shape((shards, (2 * tiles + 1) * own + 4 * tiles + 8, 128), BF16),
-        [VMEM] * 5,
-        flops=2 * shards * own * depth * 2 * (columns + rank),
+        [shape((shards, (2 * tiles + 1) * own + info_rows, 128), BF16), outs[1]],
+        [SMEM] + [VMEM] * 9,
+        flops=2**30,
         size=8 * 2**20,
-    )(g_own, g_other, base, bt.reshape(2 * rank, depth), extra)
-    payload, place = lax.optimization_barrier((payload, place))
+        scratch=[pltpu.VMEM((info_rows, 128), F32)],
+    )(place, *first, *second, g_other, base, bt.reshape(2 * rank, depth))
     got = lax.all_to_all(payload, WIDTH, 0, 0)
 
     height = rows * (tiles + tiles // 2 + 1) + own + 8

time: 165 us -> 162 us (0.982)
  blocking collectives: 75.3 us -> 70.2 us
    ppermute x1, starting transfers between devices: 10.1 us -> 5.67 us  [per_device(): g_other = lax.ppermute(g_own, 'core', swap)]
    ppermute x1, starting transfers between devices: 4.52 us -> 8.61 us  [per_device(): theirs = lax.ppermute(theirs, 'core', swap)]
    all_to_all x1, blocking collectives: 27.4 us -> 23.7 us  [per_device(): got = lax.all_to_all(payload, WIDTH, 0, 0)]
    pallas_call x2 -> x3, Pallas kernels: 7.45 us -> 8.63 us  [the longest x1 5.29 us: per_device(): first = early(place, g_own, base, bt, a)]
    unnamed x14 -> x16, local copies, waits for them, and re-layouts: 3.79 us -> 3.8 us
  transfers between devices with their start and end apart: 10 -> 10, of which waited for: 8 -> 9; matrix products, arithmetic and copies ran while one was open for 0% -> 0% of each run, Pallas kernels for 2% -> 1%
where the time goes in v7:
time: 162 us; the launch traced here: 161 us
  blocking collectives  70.2 us (43%)
  starting transfers between devices  48.2 us (30%)
  waiting for transfers between devices  19.7 us (12%)
  Pallas kernels  18.4 us (11%)
  local copies, waits for them, and re-layouts  3.8 us (2%)
    all_gather x1, blocking collectives, per_device(): g_own = lax.all_gather(tokens, 'z', axis=0, tiled=True)  32.1 us
    all_to_all x1, blocking collectives, per_device(): got = lax.all_to_all(payload, WIDTH, 0, 0)  23.7 us
    all_to_all x1, blocking collectives, per_device(): got = lax.all_to_all(sends, GROUP, 0, 0)  14.4 us
    ppermute x4, starting transfers between devices, across(): lax.ppermute(value, ('y', 'x'), [(i, i ^ flip) for i in range(shards)])  11.2 us
    ppermute x1, starting transfers between devices, per_device(): theirs = lax.ppermute(theirs, 'core', swap)  8.61 us
    all_to_all x1, starting transfers between devices, per_device(): full = lax.all_to_all(chunks, 'z', 0, 0)  7.61 us
    ppermute x1, starting transfers between devices, per_device(): other = lax.ppermute(full, 'core', swap)  6.44 us
    all_to_all x1, starting transfers between devices, per_device(): got = lax.all_to_all(chunks, 'z', 0, 0)  6.18 us
  transfers between devices with their start and end apart: 10, of which 9 were waited for; matrix products, arithmetic and copies ran while one was open for 0% of the time, Pallas kernels for 1%

profile of v7, /device:TPU:1, one launch (start us, length us, event | category | flops | bytes accessed | tf_op | source)
XLA Modules:
  0.0 161.2 jit_solution(3091686292455636257)
XLA Ops:
  0.6 32.1 %all_gather.3.refs_0_.own_ref = bf16[256,1024]{1,0:T(8,128)(2,1)S(1)} all-gather(bf16[16,1024]{1,0:T(8,128)(2,1)} %param.6), channel_id=1, replica_groups=mesh['dp'=2,'z'=16,'core'=2,'y'=2,'x'=4] {'z'}, dimensions={0}, use_global_device_ids=true | all-gather | bytes 557056 | tf_op jit(solution)/shard_map/all_gather | solution.py:423
  32.7 0.1 pad_add_fusion.place_ref
  32.8 0.0 copy-start
  32.8 1.9 %copy-done = bf16[2,1024,768]{2,1,0:T(8,128)(2,1)S(1)} copy-done((bf16[2,1024,768]{2,1,0:T(8,128)(2,1)S(1)}, bf16[2,1024,768]{2,1,0:T(8,128)(2,1)}, u32[]{:S(2)}) %copy-start) | copy-done | bytes 3145752
  34.7 0.9 copy-done.2
  35.6 0.9 copy-done.4
  36.5 5.3 %shard_map.85 = (bf16[8,416,128]{2,1,0:T(8,128)(2,1)S(1)}, f32[128,768]{1,0:T(8,128)S(1)}, f32[32,128]{1,0:T(8,128)S(1)}) custom-call(s32[4]{0:T(128)S(1)} %pad_add_fusion.place_ref, bf16[256,1024]{1,0:T(8,128)(2,1)S(1)} %all_gather.3.refs_0_.own_ref, bf16[2,1024,768]{2,1,0:T(8,128)(2,1)S(1)} %copy-done, bf16[2,64,1024]{2,1,0:T(8,128)(2,1)S(1)} %bitcast.11, ...), custom_call_target="tpu_custom_call" | custom-call | flops 1073741824 | bytes 4194304 | tf_op jit(solution)/shard_map/pallas_call | solution.py:442
  41.8 0.0 copy-start.1
  41.9 0.0 copy-start.3
  41.9 5.7 %collective-permute-start = (bf16[256,1024]{1,0:T(8,128)(2,1)S(1)}, bf16[256,1024]{1,0:T(8,128)(2,1)S(1)}, u32[]{:S(2)}, u32[]{:S(2)}) collective-permute-start(bf16[256,1024]{1,0:T(8,128)(2,1)S(1)} %all_gather.3.refs_0_.own_ref), channel_id=1, source_target_pairs={{0,8},{8,0},{1,9},{9,1},{2,10},{10,2},{3,11},{11,3},{4,12},{12,4},... | collective-permute-start | bytes 1572872 | tf_op jit(solution)/shard_map/ppermute | solution.py:444
  47.6 0.6 shard_map.86
  48.1 1.0 collective-permute-done.other_ref
  49.1 0.0 copy-done.1
  49.1 0.0 copy-done.3
  49.1 2.8 %shard_map.87 = (bf16[8,864,128]{2,1,0:T(8,128)(2,1)S(1)}, f32[128,768]{1,0:T(8,128)S(1)}) custom-call(s32[4]{0:T(128)S(1)} %pad_add_fusion.place_ref, bf16[8,416,128]{2,1,0:T(8,128)(2,1)S(1)} %get-tuple-element.37.early_part, f32[128,768]{1,0:T(8,128)S(1)} %get-tuple-element.38.early_cross, f32[32,128]{1,0:T(8,128)S(1)} %get-tuple-element.39.early_info, ...), custom_call_target="tpu_custom_call" | custom-call | flops 1073741824 | bytes 8388608 | tf_op jit(solution)/shard_map/pallas_call | solution.py:446
  51.9 0.0 copy-start.5
  51.9 0.0 copy-start.6
  51.9 0.0 copy-start.7
  51.9 23.7 %all_to_all.20.got_ref = bf16[8,864,128]{2,1,0:T(8,128)(2,1)S(1)} all-to-all(bf16[8,864,128]{2,1,0:T(8,128)(2,1)S(1)} %get-tuple-element.44), channel_id=1, replica_groups=mesh['dp'=2,'z'=16,'core'=2,'y'=2,'x'=4] {'x','y'}, dimensions={0} | all-to-all | bytes 3538944 | tf_op jit(solution)/shard_map/all_to_all | solution.py:454
  75.6 0.0 copy-done.5
  75.7 0.0 copy-done.6
  75.7 0.0 copy-done.7
  75.7 3.4 %shard_map.88 = (bf16[16,152,128]{2,1,0:T(8,128)(2,1)S(1)}, f32[2,768]{1,0:T(2,128)S(1)}) custom-call(s32[4]{0:T(128)S(1)} %pad_add_fusion.place_ref, bf16[8,864,128]{2,1,0:T(8,128)(2,1)S(1)} %all_to_all.20.got_ref, bf16[64,768]{1,0:T(8,128)(2,1)S(1)} %copy-done.6, bf16[2,64,768]{2,1,0:T(8,128)(2,1)S(1)} %copy-done.5, f32[2,768]{1,0:T(2,128)S(1)} %copy-done.7, ...), custom_call_target="tpu_custom_call" | custom-call | flops 134217728 | bytes 4194304 | tf_op jit(solution)/shard_map/pallas_call | solution.py:457
  79.0 14.4 %all_to_all.21.got_ref = bf16[16,152,128]{2,1,0:T(8,128)(2,1)S(1)} all-to-all(bf16[16,152,128]{2,1,0:T(8,128)(2,1)S(1)} %get-tuple-element.46), channel_id=1, replica_groups=mesh['dp'=2,'z'=16,'core'=2,'y'=2,'x'=4] {'x','y','dp'}, dimensions={0} | all-to-all | bytes 1245184 | tf_op jit(solution)/shard_map/all_to_all | solution.py:464
  93.5 2.0 %shard_map.89 = (f32[128,512]{1,0:T(8,128)S(1)}, f32[128,512]{1,0:T(8,128)S(1)}, f32[2,768]{1,0:T(2,128)}, f32[2,768]{1,0:T(2,128)S(1)}) custom-call(s32[4]{0:T(128)S(1)} %pad_add_fusion.place_ref, bf16[16,152,128]{2,1,0:T(8,128)(2,1)S(1)} %all_to_all.21.got_ref, f32[2,768]{1,0:T(2,128)S(1)} %get-tuple-element.47.norm_ref, f32[2,768]{1,0:T(2,128)S(1)} %copy-done.7, ...), custom_call_target="tpu_custom_call" | custom-call | flops 1073741824 | bytes 8388608 | tf_op jit(solution)/shard_map/pallas_call | solution.py:466
  95.5 8.6 %collective-permute-start.1 = (f32[128,512]{1,0:T(8,128)S(1)}, f32[128,512]{1,0:T(8,128)S(1)}, u32[]{:S(2)}, u32[]{:S(2)}) collective-permute-start(f32[128,512]{1,0:T(8,128)S(1)} %get-tuple-element.49), channel_id=1, source_target_pairs={{0,8},{8,0},{1,9},{9,1},{2,10},{10,2},{3,11},{11,3},{4,12},{12,4},... | collective-permute-start | bytes 786440 | tf_op jit(solution)/shard_map/ppermute | solution.py:482
  104.1 1.1 collective-permute-done.1.theirs_ref
  105.2 0.9 shard_map.90
  106.1 6.2 %all-to-all-start.2 = ((bf16[16,8,640]{2,1,0:T(8,128)(2,1)}), bf16[16,8,640]{2,1,0:T(8,128)(2,1)S(1)}, u32[]{:S(2)}, u32[]{:S(2)}) async-start(bf16[16,8,640]{2,1,0:T(8,128)(2,1)} %shard_map.90), calls=%async_computation.2 | async-start | bytes 327680 | tf_op jit(solution)/shard_map/all_to_all | solution.py:485
  112.3 0.9 shard_map.91.rows_ref
  113.2 2.8 %collective-permute-start.2 = (f32[8,768]{1,0:T(8,128)S(1)}, f32[8,768]{1,0:T(8,128)S(1)}, u32[]{:S(2)}, u32[]{:S(2)}) collective-permute-start(f32[8,768]{1,0:T(8,128)S(1)} %shard_map.91.rows_ref), channel_id=1, source_target_pairs={{0,2},{1,3},{2,0},{3,1},{4,6},{5,7},{6,4},{7,5},{8,10},{9,11},{10,... | collective-permute-start | bytes 73736 | tf_op jit(solution)/shard_map/ppermute | solution.py:488
  116.0 3.6 %collective-permute-done.2.far_ref = f32[8,768]{1,0:T(8,128)S(1)} collective-permute-done((f32[8,768]{1,0:T(8,128)S(1)}, f32[8,768]{1,0:T(8,128)S(1)}, u32[]{:S(2)}, u32[]{:S(2)}) %collective-permute-start.2) | collective-permute-done | bytes 24608 | tf_op jit(solution)/shard_map/ppermute | solution.py:488
  119.6 5.1 %all-to-all-done.2.got_ref = bf16[16,8,640]{2,1,0:T(8,128)(2,1)S(1)} async-done(((bf16[16,8,640]{2,1,0:T(8,128)(2,1)}), bf16[16,8,640]{2,1,0:T(8,128)(2,1)S(1)}, u32[]{:S(2)}, u32[]{:S(2)}) %all-to-all-start.2) | async-done | bytes 163872 | tf_op jit(solution)/shard_map/all_to_all | solution.py:485
  124.7 0.1 shard_map.92.mine_ref
  124.9 2.5 %collective-permute-start.3 = (f32[24,768]{1,0:T(8,128)S(1)}, f32[24,768]{1,0:T(8,128)S(1)}, u32[]{:S(2)}, u32[]{:S(2)}) collective-permute-start(f32[24,768]{1,0:T(8,128)S(1)} %shard_map.92.mine_ref), channel_id=1, source_target_pairs={{0,256},{256,0},{1,257},{257,1},{2,258},{258,2},{3,259},{259,3},{4... | collective-permute-start | bytes 221192 | tf_op jit(solution)/shard_map/ppermute | solution.py:493
  127.3 4.1 %collective-permute-done.3.theirs_ref = f32[24,768]{1,0:T(8,128)S(1)} collective-permute-done((f32[24,768]{1,0:T(8,128)S(1)}, f32[24,768]{1,0:T(8,128)S(1)}, u32[]{:S(2)}, u32[]{:S(2)}) %collective-permute-start.3) | collective-permute-done | bytes 73760 | tf_op jit(solution)/shard_map/ppermute | solution.py:493
  131.5 0.8 shard_map.93
  132.3 7.6 %all-to-all-start.3 = ((bf16[16,8,640]{2,1,0:T(8,128)(2,1)}), bf16[16,8,640]{2,1,0:T(8,128)(2,1)S(1)}, u32[]{:S(2)}, u32[]{:S(2)}) async-start(bf16[16,8,640]{2,1,0:T(8,128)(2,1)} %get-tuple-element.51), calls=%async_computation.3 | async-start | bytes 327680 | tf_op jit(solution)/shard_map/all_to_all | solution.py:497
  139.9 2.1 %collective-permute-start.6 = (f32[32,768]{1,0:T(8,128)S(1)}, f32[32,768]{1,0:T(8,128)S(1)}, u32[]{:S(2)}, u32[]{:S(2)}) collective-permute-start(f32[32,768]{1,0:T(8,128)S(1)} %get-tuple-element.54.r0_ref), channel_id=1, source_target_pairs={{0,5},{1,4},{2,7},{3,6},{4,1},{5,0},{6,3},{7,2},{8,13},{9,12},{10,... | collective-permute-start | bytes 294920 | tf_op jit(solution)/shard_map/ppermute | solution.py:488
  142.0 3.2 %collective-permute-start.5 = (f32[32,768]{1,0:T(8,128)S(1)}, f32[32,768]{1,0:T(8,128)S(1)}, u32[]{:S(2)}, u32[]{:S(2)}) collective-permute-start(f32[32,768]{1,0:T(8,128)S(1)} %get-tuple-element.54.r0_ref), channel_id=1, source_target_pairs={{0,1},{1,0},{2,3},{3,2},{4,5},{5,4},{6,7},{7,6},{8,9},{9,8},{10,11... | collective-permute-start | bytes 294920 | tf_op jit(solution)/shard_map/ppermute | solution.py:488
  145.2 3.1 %collective-permute-start.4 = (f32[32,768]{1,0:T(8,128)S(1)}, f32[32,768]{1,0:T(8,128)S(1)}, u32[]{:S(2)}, u32[]{:S(2)}) collective-permute-start(f32[32,768]{1,0:T(8,128)S(1)} %get-tuple-element.54.r0_ref), channel_id=1, source_target_pairs={{0,4},{1,5},{2,6},{3,7},{4,0},{5,1},{6,2},{7,3},{8,12},{9,13},{10,... | collective-permute-start | bytes 294920 | tf_op jit(solution)/shard_map/ppermute | solution.py:488
  148.3 0.0 collective-permute-done.6.r3_ref
  148.3 0.2 collective-permute-done.5.r2_ref
  148.5 2.4 %collective-permute-done.4.r1_ref = f32[32,768]{1,0:T(8,128)S(1)} collective-permute-done((f32[32,768]{1,0:T(8,128)S(1)}, f32[32,768]{1,0:T(8,128)S(1)}, u32[]{:S(2)}, u32[]{:S(2)}) %collective-permute-start.4) | collective-permute-done | bytes 98336 | tf_op jit(solution)/shard_map/ppermute | solution.py:488
  150.8 1.2 all-to-all-done.3.own_ref
  152.1 6.4 %collective-permute-start.7 = (bf16[16,8,640]{2,1,0:T(8,128)(2,1)S(1)}, bf16[16,8,640]{2,1,0:T(8,128)(2,1)S(1)}, u32[]{:S(2)}, u32[]{:S(2)}) collective-permute-start(bf16[16,8,640]{2,1,0:T(8,128)(2,1)S(1)} %all-to-all-done.3.own_ref), channel_id=1, source_target_pairs={{0,8},{8,0},{1,9},{9,1},{2,10},{10,2},{3,11},{11,3},{4,12},{12,4},... | collective-permute-start | bytes 491528 | tf_op jit(solution)/shard_map/ppermute | solution.py:499
  158.5 1.0 collective-permute-done.7.other_ref
  159.5 1.7 %shard_map.94 = (f32[128,768]{1,0:T(8,128)}, f32[128,1024]{1,0:T(8,128)}) custom-call(s32[4]{0:T(128)S(1)} %pad_add_fusion.place_ref, bf16[16,8,640]{2,1,0:T(8,128)(2,1)S(1)} %all-to-all-done.3.own_ref, bf16[16,8,640]{2,1,0:T(8,128)(2,1)S(1)} %collective-permute-done.7.other_ref, f32[32,768]{1,0:T(8,128)S(1)} %get-tuple-element.54.r0_ref, ...), custom_call_target="tpu_custom_call" | custom-call | bytes 2097152 | tf_op jit(solution)/shard_map/pallas_call | solution.py:500
  (2 shorter events, 0.0 us)
Async XLA Ops:
  32.8 1.9 %copy-start = (bf16[2,1024,768]{2,1,0:T(8,128)(2,1)S(1)}, bf16[2,1024,768]{2,1,0:T(8,128)(2,1)}, u32[]{:S(2)}) copy-start(bf16[2,1024,768]{2,1,0:T(8,128)(2,1)} %base_ref.3) | copy-start | bytes 9437188
  34.7 0.9 copy-start.2
  35.6 0.9 copy-start.4
  41.8 7.2 %copy-start.1 = (bf16[2,1024,768]{2,1,0:T(8,128)(2,1)S(1)}, bf16[2,1024,768]{2,1,0:T(8,128)(2,1)}, u32[]{:S(2)}) copy-start(bf16[2,1024,768]{2,1,0:T(8,128)(2,1)} %base_ref.3) | copy-start | bytes 9437188
  41.9 7.2 %copy-start.3 = (bf16[2,1024,64]{1,2,0:T(8,128)(2,1)S(1)}, bf16[2,1024,64]{1,2,0:T(8,128)(2,1)}, u32[]{:S(2)}) copy-start(bf16[2,1024,64]{1,2,0:T(8,128)(2,1)} %param.8) | copy-start | bytes 786436
  41.9 7.2 %collective-permute-start = (bf16[256,1024]{1,0:T(8,128)(2,1)S(1)}, bf16[256,1024]{1,0:T(8,128)(2,1)S(1)}, u32[]{:S(2)}, u32[]{:S(2)}) collective-permute-start(bf16[256,1024]{1,0:T(8,128)(2,1)S(1)} %all_gather.3.refs_0_.own_ref), channel_id=1, source_target_pairs={{0,8},{8,0},{1,9},{9,1},{2,10},{10,2},{3,11},{11,3},{4,12},{12,4},... | collective-permute-start | bytes 1572872 | tf_op jit(solution)/shard_map/ppermute | solution.py:444
  51.9 23.8 %copy-start.5 = (bf16[2,64,768]{2,1,0:T(8,128)(2,1)S(1)}, bf16[2,64,768]{2,1,0:T(8,128)(2,1)}, u32[]{:S(2)}) copy-start(bf16[2,64,768]{2,1,0:T(8,128)(2,1)} %a_ref.3) | copy-start | bytes 589828
  51.9 23.8 %copy-start.6 = (bf16[64,768]{1,0:T(8,128)(2,1)S(1)}, bf16[64,768]{1,0:T(8,128)(2,1)}, u32[]{:S(2)}) copy-start(bf16[64,768]{1,0:T(8,128)(2,1)} %cot_ref.1) | copy-start | bytes 294916
  51.9 23.8 %copy-start.7 = (f32[2,768]{1,0:T(2,128)S(1)}, f32[2,768]{1,0:T(2,128)}, u32[]{:S(2)}) copy-start(f32[2,768]{1,0:T(2,128)} %mag_ref.3) | copy-start | bytes 18436
  95.5 9.8 %collective-permute-start.1 = (f32[128,512]{1,0:T(8,128)S(1)}, f32[128,512]{1,0:T(8,128)S(1)}, u32[]{:S(2)}, u32[]{:S(2)}) collective-permute-start(f32[128,512]{1,0:T(8,128)S(1)} %get-tuple-element.49), channel_id=1, source_target_pairs={{0,8},{8,0},{1,9},{9,1},{2,10},{10,2},{3,11},{11,3},{4,12},{12,4},... | collective-permute-start | bytes 786440 | tf_op jit(solution)/shard_map/ppermute | solution.py:482
  106.1 18.6 %all-to-all-start.2 = ((bf16[16,8,640]{2,1,0:T(8,128)(2,1)}), bf16[16,8,640]{2,1,0:T(8,128)(2,1)S(1)}, u32[]{:S(2)}, u32[]{:S(2)}) async-start(bf16[16,8,640]{2,1,0:T(8,128)(2,1)} %shard_map.90), calls=%async_computation.2 | async-start | bytes 327680 | tf_op jit(solution)/shard_map/all_to_all | solution.py:485
  113.2 6.4 %collective-permute-start.2 = (f32[8,768]{1,0:T(8,128)S(1)}, f32[8,768]{1,0:T(8,128)S(1)}, u32[]{:S(2)}, u32[]{:S(2)}) collective-permute-start(f32[8,768]{1,0:T(8,128)S(1)} %shard_map.91.rows_ref), channel_id=1, source_target_pairs={{0,2},{1,3},{2,0},{3,1},{4,6},{5,7},{6,4},{7,5},{8,10},{9,11},{10,... | collective-permute-start | bytes 73736 | tf_op jit(solution)/shard_map/ppermute | solution.py:488
  124.9 6.6 %collective-permute-start.3 = (f32[24,768]{1,0:T(8,128)S(1)}, f32[24,768]{1,0:T(8,128)S(1)}, u32[]{:S(2)}, u32[]{:S(2)}) collective-permute-start(f32[24,768]{1,0:T(8,128)S(1)} %shard_map.92.mine_ref), channel_id=1, source_target_pairs={{0,256},{256,0},{1,257},{257,1},{2,258},{258,2},{3,259},{259,3},{4... | collective-permute-start | bytes 221192 | tf_op jit(solution)/shard_map/ppermute | solution.py:493
  132.3 19.8 %all-to-all-start.3 = ((bf16[16,8,640]{2,1,0:T(8,128)(2,1)}), bf16[16,8,640]{2,1,0:T(8,128)(2,1)S(1)}, u32[]{:S(2)}, u32[]{:S(2)}) async-start(bf16[16,8,640]{2,1,0:T(8,128)(2,1)} %get-tuple-element.51), calls=%async_computation.3 | async-start | bytes 327680 | tf_op jit(solution)/shard_map/all_to_all | solution.py:497
  139.9 8.4 %collective-permute-start.6 = (f32[32,768]{1,0:T(8,128)S(1)}, f32[32,768]{1,0:T(8,128)S(1)}, u32[]{:S(2)}, u32[]{:S(2)}) collective-permute-start(f32[32,768]{1,0:T(8,128)S(1)} %get-tuple-element.54.r0_ref), channel_id=1, source_target_pairs={{0,5},{1,4},{2,7},{3,6},{4,1},{5,0},{6,3},{7,2},{8,13},{9,12},{10,... | collective-permute-start | bytes 294920 | tf_op jit(solution)/shard_map/ppermute | solution.py:488
  142.0 6.4 %collective-permute-start.5 = (f32[32,768]{1,0:T(8,128)S(1)}, f32[32,768]{1,0:T(8,128)S(1)}, u32[]{:S(2)}, u32[]{:S(2)}) collective-permute-start(f32[32,768]{1,0:T(8,128)S(1)} %get-tuple-element.54.r0_ref), channel_id=1, source_target_pairs={{0,1},{1,0},{2,3},{3,2},{4,5},{5,4},{6,7},{7,6},{8,9},{9,8},{10,11... | collective-permute-start | bytes 294920 | tf_op jit(solution)/shard_map/ppermute | solution.py:488
  145.2 5.7 %collective-permute-start.4 = (f32[32,768]{1,0:T(8,128)S(1)}, f32[32,768]{1,0:T(8,128)S(1)}, u32[]{:S(2)}, u32[]{:S(2)}) collective-permute-start(f32[32,768]{1,0:T(8,128)S(1)} %get-tuple-element.54.r0_ref), channel_id=1, source_target_pairs={{0,4},{1,5},{2,6},{3,7},{4,0},{5,1},{6,2},{7,3},{8,12},{9,13},{10,... | collective-permute-start | bytes 294920 | tf_op jit(solution)/shard_map/ppermute | solution.py:488
  152.1 7.5 %collective-permute-start.7 = (bf16[16,8,640]{2,1,0:T(8,128)(2,1)S(1)}, bf16[16,8,640]{2,1,0:T(8,128)(2,1)S(1)}, u32[]{:S(2)}, u32[]{:S(2)}) collective-permute-start(bf16[16,8,640]{2,1,0:T(8,128)(2,1)S(1)} %all-to-all-done.3.own_ref), channel_id=1, source_target_pairs={{0,8},{8,0},{1,9},{9,1},{2,10},{10,2},{3,11},{11,3},{4,12},{12,4},... | collective-permute-start | bytes 491528 | tf_op jit(solution)/shard_map/ppermute | solution.py:499

commit v8 on v7

--- a/solution.py
+++ b/solution.py
@@ -16,19 +16,21 @@
 SMEM = pl.BlockSpec(memory_space=pltpu.SMEM)
 STEP = 512
 
-BEND = 4096.0
+BEND = 1024.0
 POWER = 250.0 / math.log2(1.0 + BEND)
-SHIFT = 125.0 * math.log(2.0)
+SHIFT = 125.0
+LN2 = math.log(2.0)
 
 
 def encode(x, peak):
-    size = jnp.exp(POWER * jnp.log(1.0 + jnp.abs(x) * (BEND / peak)) - SHIFT)
+    size = jnp.exp2(jnp.log(1.0 + jnp.abs(x) * (BEND / peak)) * (POWER / LN2) - SHIFT)
     return jnp.where(x < 0, -size, size)
 
 
 def decode(code, peak):
     code = code.astype(F32)
-    size = (jnp.exp((jnp.log(jnp.abs(code)) + SHIFT) * (1.0 / POWER)) - 1.0) * (peak / BEND)
+    scale = peak / BEND
+    size = jnp.exp2(jnp.log(jnp.abs(code)) * (1.0 / (POWER * LN2)) + SHIFT / POWER) * scale - scale
     return jnp.where(code < 0, -size, size)
 
 
@@ -63,9 +65,10 @@
     return peak
 
 
-def own_work(own_ref, base_ref, bt_ref, a_ref, part_ref, cross_ref, info_ref):
+def own_work(own_ref, base_ref, low_ref, part_ref, cross_ref, info_ref):
     depth, columns = base_ref.shape[1:]
-    rank = a_ref.shape[1]
+    rank = low_ref.shape[1]
+    bt_ref, a_ref = low_ref.at[:, :, :depth], low_ref.at[:, :, depth:]
     tiles = columns // 128
     shards = part_ref.shape[0]
     half = own_ref.shape[0] // shards
@@ -84,15 +87,17 @@
     peaks = jnp.where(line == 2, peak, jnp.zeros((8, 128), F32))
     for k in range(2):
         sq = jnp.zeros((8, columns), F32)
-        cross = jnp.zeros((rank, columns), F32)
         for at in range(0, depth, STEP):
             rows = slice(at, at + STEP)
-            bt = bt_ref[k, :, rows]
-            combined = base_ref[k, rows, :].astype(F32) + dot(bt, a_ref[k], TN)
+            combined = base_ref[k, rows, :].astype(F32) + dot(bt_ref[k, :, rows], a_ref[k], TN)
             sq += jnp.sum((combined * combined).reshape(STEP // 8, 8, columns), axis=0)
-            hi, lo = split(combined)
-            cross += dot(bt, hi) + dot(bt, lo)
-        cross_ref[k * rank : (k + 1) * rank, :] = cross
+        bt = bt_ref[k]
+        square = dot(bt, bt, NT)
+        hi, lo = split(square)
+        rest = (square - hi.astype(F32) - lo.astype(F32)).astype(BF16)
+        cross_ref[k * rank : (k + 1) * rank, :] = dot(bt, base_ref[k]) + (
+            dot(hi, a_ref[k]) + (dot(lo, a_ref[k]) + dot(rest, a_ref[k]))
+        )
         sq = jnp.sum(sq, axis=0, keepdims=True)
         for piece in range(2):
             part = sq.astype(BF16).astype(F32)
@@ -118,29 +123,28 @@
 
 
 def forward_kernel(
-    place_ref, early_part, early_cross, early_info, late_part, late_cross, late_info, other_ref,
-    base_ref, bt_ref, out_ref, cross_ref, info_ref,
+    place_ref, early_part, early_info, late_part, late_info, other_ref, base_ref, low_ref, out_ref, info_ref
 ):
     shards = out_ref.shape[0]
-    columns = base_ref.shape[2]
+    depth, columns = base_ref.shape[1:]
+    bt = low_ref[:, :, :depth].reshape(2 * low_ref.shape[1], depth)
     half = other_ref.shape[0] // shards
     owned = 2 * half
     tiles = columns // 128
     info_rows = info_ref.shape[0]
 
-    def take(part_ref, cross_in, info_in):
+    def take(part_ref, info_in):
         for i in range(2 * tiles + 1):
             out_ref[:, owned * i : owned * i + half, :] = part_ref[:, half * i : half * (i + 1), :]
-        cross_ref[...] = cross_in[...]
         info_ref[...] = info_in[...]
 
     @pl.when(place_ref[1] == 1)
     def _():
-        take(early_part, early_cross, early_info)
+        take(early_part, early_info)
 
     @pl.when(place_ref[1] == 0)
     def _():
-        take(late_part, late_cross, late_info)
+        take(late_part, late_info)
 
     def put_at(first):
         def put(i, code):
@@ -152,7 +156,7 @@
 
     line = lax.broadcasted_iota(jnp.int32, (info_rows, 128), 0)
     info = info_ref[...]
-    peak = coded(dot(other_ref[...], bt_ref[...], NT), put_at(2 * tiles))
+    peak = coded(dot(other_ref[...], bt, NT), put_at(2 * tiles))
     info = jnp.where(line == info_rows - 3, peak, info)
     for k in range(2):
         peak = coded(dot(other_ref[...], base_ref[k]), put_at(tiles * k))
@@ -161,10 +165,14 @@
     out_ref[:, (2 * tiles + 1) * owned :, :] = jnp.broadcast_to(rest[None], (shards,) + rest.shape)
 
 
-def local_kernel(place_ref, got_ref, cot_ref, a_ref, mag_ref, cross_ref, out_ref, norm_ref):
+def local_kernel(
+    place_ref, got_ref, cot_ref, low_ref, mag_ref, early_cross, late_cross, out_ref, norm_ref
+):
     dp, core = place_ref[0], place_ref[1]
     shards = got_ref.shape[0]
-    rank, columns = a_ref.shape[1:]
+    columns = cot_ref.shape[1]
+    rank = low_ref.shape[1]
+    a_ref = low_ref.at[:, :, low_ref.shape[2] - columns :]
     owned = cot_ref.shape[0]
     tiles = columns // 128
     half = owned // 2
@@ -232,7 +240,8 @@
         )
         back = dot(hi, a_ref[k], NT) + dot(lo, a_ref[k], NT)
         width = columns // 2
-        cross = cross_ref[mine, pl.ds(pl.multiple_of(dp * width, width), width)]
+        lanes = pl.ds(pl.multiple_of(dp * width, width), width)
+        cross = jnp.where(core == 1, early_cross[mine, lanes], late_cross[mine, lanes])
         peaks.append((peak_of(grad_a), peak_of(cross)))
         codes.append((encode(grad_a, peaks[k][0]), encode(cross, peaks[k][1])))
         back_peaks.append(peak_of(back))
@@ -287,13 +296,14 @@
 
 
 def width_kernel(
-    place_ref, got_ref, norm_ref, mag_ref, own_ref, other_ref, base_ref, bt_ref, a_ref,
+    place_ref, got_ref, norm_ref, mag_ref, own_ref, other_ref, base_ref, low_ref,
     mine_ref, theirs_ref, grad_m_ref, coeff_ref, sum_ref,
 ):
     dp, core = place_ref[0], place_ref[1]
     members = got_ref.shape[0]
     shards = members // 2
-    rank, columns = a_ref.shape[1:]
+    depth, columns = base_ref.shape[1:]
+    rank = low_ref.shape[1]
     tiles = columns // 128
     owned = 2 * own_ref.shape[0] // shards
     half = owned // 2
@@ -327,13 +337,14 @@
         part = both[: 2 * rank] + both[2 * rank :]
         total = part if total is None else total + part
     sum_ref[...] = total
-    a = a_ref[dp]
+    a = low_ref[dp, :, depth:]
+    bt = low_ref[dp, :, :depth]
     hi, lo = split(a.astype(F32) * coeff_ref[pl.ds(dp, 1), :])
     weighted = jnp.concatenate([hi, lo], axis=0)
     both = dot(weighted, base_ref[dp], NT)
     small = dot(weighted, a, NT)
     small_hi, small_lo = split(small[:rank] + small[rank:])
-    value = (both[:rank] + both[rank:]) + (dot(small_hi, bt_ref[dp]) + dot(small_lo, bt_ref[dp]))
+    value = (both[:rank] + both[rank:]) + (dot(small_hi, bt) + dot(small_lo, bt))
     mine = pl.ds(pl.multiple_of(dp * rank, rank), rank)
     sum_ref[mine, :] += value
     width = mine_ref.shape[1]
@@ -417,7 +428,7 @@
     rows = 2 * rank // members
     tiles = columns // 128
     swap = [(0, 1), (1, 0)]
-    bt = jnp.swapaxes(b, 1, 2)
+    low = jnp.concatenate([jnp.swapaxes(b, 1, 2), a], axis=2)
     place = jnp.stack([dp, core, lax.axis_index("x"), lax.axis_index(GROUP)]).astype(jnp.int32)
 
     g_own = lax.all_gather(tokens, "z", axis=0, tiled=True)
@@ -433,44 +444,44 @@
             call,
             kernel,
             outs,
-            [SMEM] + [VMEM] * 4,
+            [SMEM] + [VMEM] * 3,
             flops=2**30,
             size=4 * 2**20,
         )()
         for kernel in (early_kernel, late_kernel)
     )
-    first = early(place, g_own, base, bt, a)
+    first = early(place, g_own, base, low)
     g_own, first = lax.optimization_barrier((g_own, first))
     g_other = lax.ppermute(g_own, "core", swap)
-    second = late(place, g_own, base, bt, a)
-    payload, cross = call(
+    second = late(place, g_own, base, low)
+    payload = call(
         forward_kernel,
-        [shape((shards, (2 * tiles + 1) * own + info_rows, 128), BF16), outs[1]],
-        [SMEM] + [VMEM] * 9,
+        shape((shards, (2 * tiles + 1) * own + info_rows, 128), BF16),
+        [SMEM] + [VMEM] * 7,
         flops=2**30,
         size=8 * 2**20,
         scratch=[pltpu.VMEM((info_rows, 128), F32)],
-    )(place, *first, *second, g_other, base, bt.reshape(2 * rank, depth))
+    )(place, first[0], first[2], second[0], second[2], g_other, base, low)
     got = lax.all_to_all(payload, WIDTH, 0, 0)
 
     height = rows * (tiles + tiles // 2 + 1) + own + 8
     sends, norm = call(
         local_kernel,
         [shape((members, height, 128), BF16), shape((2, columns))],
-        [SMEM] + [VMEM] * 5,
+        [SMEM] + [VMEM] * 6,
         flops=2**27,
         size=4 * 2**20,
-    )(place, got, cotangent, a, magnitude, cross)
+    )(place, got, cotangent, low, magnitude, first[1], second[1])
     got = lax.all_to_all(sends, GROUP, 0, 0)
 
     mine, theirs, grad_m, coeff = call(
         width_kernel,
         [shape((2 * rank, depth // 2))] * 2 + [shape((2, columns))] * 2,
-        [SMEM] + [VMEM] * 8,
+        [SMEM] + [VMEM] * 7,
         flops=2**30,
         size=8 * 2**20,
         scratch=[pltpu.VMEM((2 * rank, depth), F32)],
-    )(place, got, norm, magnitude, g_own, g_other, base, bt, a)
+    )(place, got, norm, magnitude, g_own, g_other, base, low)
     a_rows = call(
         rows_kernel,
         shape((rows, columns)),

time: 162 us -> 161 us (level)
  local copies, waits for them, and re-layouts: 3.8 us -> 1.9 us
    unnamed x16 -> x8, local copies, waits for them, and re-layouts: 3.8 us -> 1.9 us
where the time goes in v8:
time: 161 us; the launch traced here: 160 us
  blocking collectives  71 us (44%)
  starting transfers between devices  48.1 us (30%)
  waiting for transfers between devices  19.7 us (12%)
  Pallas kernels  17.4 us (11%)
  local copies, waits for them, and re-layouts  1.9 us (1%)
    all_gather x1, blocking collectives, per_device(): g_own = lax.all_gather(tokens, 'z', axis=0, tiled=True)  32.1 us
    all_to_all x1, blocking collectives, per_device(): got = lax.all_to_all(payload, WIDTH, 0, 0)  24.3 us
    all_to_all x1, blocking collectives, per_device(): got = lax.all_to_all(sends, GROUP, 0, 0)  14.6 us
    ppermute x4, starting transfers between devices, across(): lax.ppermute(value, ('y', 'x'), [(i, i ^ flip) for i in range(shards)])  11.2 us
    ppermute x1, starting transfers between devices, per_device(): theirs = lax.ppermute(theirs, 'core', swap)  8.01 us
    all_to_all x1, starting transfers between devices, per_device(): full = lax.all_to_all(chunks, 'z', 0, 0)  7.61 us
    ppermute x1, starting transfers between devices, per_device(): other = lax.ppermute(full, 'core', swap)  6.44 us
    ppermute x1, starting transfers between devices, per_device(): g_other = lax.ppermute(g_own, 'core', swap)  6.17 us
  transfers between devices with their start and end apart: 10, of which 9 were waited for; matrix products, arithmetic and copies ran while one was open for 0% of the time, Pallas kernels for 1%

profile of v8, /device:TPU:1, one launch (start us, length us, event | category | flops | bytes accessed | tf_op | source)
XLA Modules:
  0.0 160.1 jit_solution(9077996912604781111)
XLA Ops:
  0.6 32.1 %all_gather.3.refs_0_.own_ref = bf16[256,1024]{1,0:T(8,128)(2,1)S(1)} all-gather(bf16[16,1024]{1,0:T(8,128)(2,1)} %param.6), channel_id=1, replica_groups=mesh['dp'=2,'z'=16,'core'=2,'y'=2,'x'=4] {'z'}, dimensions={0}, use_global_device_ids=true | all-gather | bytes 557056 | tf_op jit(solution)/shard_map/all_gather | solution.py:434
  32.7 0.1 pad_add_fusion.place_ref
  32.8 1.1 pad_maximum_fusion.refs_2_.low_ref
  33.9 0.0 copy-start
  33.9 1.9 %copy-done = bf16[2,1024,768]{2,1,0:T(8,128)(2,1)S(1)} copy-done((bf16[2,1024,768]{2,1,0:T(8,128)(2,1)S(1)}, bf16[2,1024,768]{2,1,0:T(8,128)(2,1)}, u32[]{:S(2)}) %copy-start) | copy-done | bytes 3145752
  35.8 4.8 %shard_map.85 = (bf16[8,416,128]{2,1,0:T(8,128)(2,1)S(1)}, f32[128,768]{1,0:T(8,128)S(1)}, f32[32,128]{1,0:T(8,128)S(1)}) custom-call(s32[4]{0:T(128)S(1)} %pad_add_fusion.place_ref, bf16[256,1024]{1,0:T(8,128)(2,1)S(1)} %all_gather.3.refs_0_.own_ref, bf16[2,1024,768]{2,1,0:T(8,128)(2,1)S(1)} %copy-done, bf16[2,64,1792]{2,1,0:T(8,128)(2,1)S(1)} %pad_maximum_fusion.refs_2_.low_ref), custom_call_target="tpu_custom_call" | custom-call | flops 1073741824 | bytes 4194304 | tf_op jit(solution)/shard_map/pallas_call | solution.py:453
  40.6 0.0 copy-start.1
  40.6 6.2 %collective-permute-start = (bf16[256,1024]{1,0:T(8,128)(2,1)S(1)}, bf16[256,1024]{1,0:T(8,128)(2,1)S(1)}, u32[]{:S(2)}, u32[]{:S(2)}) collective-permute-start(bf16[256,1024]{1,0:T(8,128)(2,1)S(1)} %all_gather.3.refs_0_.own_ref), channel_id=1, source_target_pairs={{0,8},{8,0},{1,9},{9,1},{2,10},{10,2},{3,11},{11,3},{4,12},{12,4},... | collective-permute-start | bytes 1572872 | tf_op jit(solution)/shard_map/ppermute | solution.py:455
  46.8 0.6 shard_map.86
  47.3 1.0 collective-permute-done.other_ref
  48.3 0.0 copy-done.1
  48.3 2.7 %shard_map.87 = bf16[8,864,128]{2,1,0:T(8,128)(2,1)S(1)} custom-call(s32[4]{0:T(128)S(1)} %pad_add_fusion.place_ref, bf16[8,416,128]{2,1,0:T(8,128)(2,1)S(1)} %get-tuple-element.35.early_part, f32[32,128]{1,0:T(8,128)S(1)} %get-tuple-element.36.early_info, bf16[8,416,128]{2,1,0:T(8,128)(2,1)S(1)} %get-tuple-element.38.late_part, ...), custom_call_target="tpu_custom_call" | custom-call | flops 1073741824 | bytes 8388608 | tf_op jit(solution)/shard_map/pallas_call | solution.py:457
  50.9 0.0 copy-start.2
  50.9 0.0 copy-start.3
  51.0 24.3 %all_to_all.20.got_ref = bf16[8,864,128]{2,1,0:T(8,128)(2,1)S(1)} all-to-all(bf16[8,864,128]{2,1,0:T(8,128)(2,1)S(1)} %shard_map.87), channel_id=1, replica_groups=mesh['dp'=2,'z'=16,'core'=2,'y'=2,'x'=4] {'x','y'}, dimensions={0} | all-to-all | bytes 3538944 | tf_op jit(solution)/shard_map/all_to_all | solution.py:465
  75.3 0.0 copy-done.2
  75.3 0.0 copy-done.3
  75.3 3.2 %shard_map.88 = (bf16[16,152,128]{2,1,0:T(8,128)(2,1)S(1)}, f32[2,768]{1,0:T(2,128)S(1)}) custom-call(s32[4]{0:T(128)S(1)} %pad_add_fusion.place_ref, bf16[8,864,128]{2,1,0:T(8,128)(2,1)S(1)} %all_to_all.20.got_ref, bf16[64,768]{1,0:T(8,128)(2,1)S(1)} %copy-done.2, bf16[2,64,1792]{2,1,0:T(8,128)(2,1)S(1)} %pad_maximum_fusion.refs_2_.low_ref, ...), custom_call_target="tpu_custom_call" | custom-call | flops 134217728 | bytes 4194304 | tf_op jit(solution)/shard_map/pallas_call | solution.py:468
  78.5 14.6 %all_to_all.21.got_ref = bf16[16,152,128]{2,1,0:T(8,128)(2,1)S(1)} all-to-all(bf16[16,152,128]{2,1,0:T(8,128)(2,1)S(1)} %get-tuple-element.42), channel_id=1, replica_groups=mesh['dp'=2,'z'=16,'core'=2,'y'=2,'x'=4] {'x','y','dp'}, dimensions={0} | all-to-all | bytes 1245184 | tf_op jit(solution)/shard_map/all_to_all | solution.py:475
  93.1 1.8 %shard_map.89 = (f32[128,512]{1,0:T(8,128)S(1)}, f32[128,512]{1,0:T(8,128)S(1)}, f32[2,768]{1,0:T(2,128)}, f32[2,768]{1,0:T(2,128)S(1)}) custom-call(s32[4]{0:T(128)S(1)} %pad_add_fusion.place_ref, bf16[16,152,128]{2,1,0:T(8,128)(2,1)S(1)} %all_to_all.21.got_ref, f32[2,768]{1,0:T(2,128)S(1)} %get-tuple-element.43.norm_ref, f32[2,768]{1,0:T(2,128)S(1)} %copy-done.3, ...), custom_call_target="tpu_custom_call" | custom-call | flops 1073741824 | bytes 8388608 | tf_op jit(solution)/shard_map/pallas_call | solution.py:477
  95.0 8.0 %collective-permute-start.1 = (f32[128,512]{1,0:T(8,128)S(1)}, f32[128,512]{1,0:T(8,128)S(1)}, u32[]{:S(2)}, u32[]{:S(2)}) collective-permute-start(f32[128,512]{1,0:T(8,128)S(1)} %get-tuple-element.45), channel_id=1, source_target_pairs={{0,8},{8,0},{1,9},{9,1},{2,10},{10,2},{3,11},{11,3},{4,12},{12,4},... | collective-permute-start | bytes 786440 | tf_op jit(solution)/shard_map/ppermute | solution.py:493
  103.0 1.1 collective-permute-done.1.theirs_ref
  104.1 0.9 shard_map.90
  105.0 6.2 %all-to-all-start.2 = ((bf16[16,8,640]{2,1,0:T(8,128)(2,1)}), bf16[16,8,640]{2,1,0:T(8,128)(2,1)S(1)}, u32[]{:S(2)}, u32[]{:S(2)}) async-start(bf16[16,8,640]{2,1,0:T(8,128)(2,1)} %shard_map.90), calls=%async_computation.2 | async-start | bytes 327680 | tf_op jit(solution)/shard_map/all_to_all | solution.py:496
  111.2 0.9 shard_map.91.rows_ref
  112.1 2.8 %collective-permute-start.2 = (f32[8,768]{1,0:T(8,128)S(1)}, f32[8,768]{1,0:T(8,128)S(1)}, u32[]{:S(2)}, u32[]{:S(2)}) collective-permute-start(f32[8,768]{1,0:T(8,128)S(1)} %shard_map.91.rows_ref), channel_id=1, source_target_pairs={{0,2},{1,3},{2,0},{3,1},{4,6},{5,7},{6,4},{7,5},{8,10},{9,11},{10,... | collective-permute-start | bytes 73736 | tf_op jit(solution)/shard_map/ppermute | solution.py:499
  114.9 3.6 %collective-permute-done.2.far_ref = f32[8,768]{1,0:T(8,128)S(1)} collective-permute-done((f32[8,768]{1,0:T(8,128)S(1)}, f32[8,768]{1,0:T(8,128)S(1)}, u32[]{:S(2)}, u32[]{:S(2)}) %collective-permute-start.2) | collective-permute-done | bytes 24608 | tf_op jit(solution)/shard_map/ppermute | solution.py:499
  118.4 5.2 %all-to-all-done.2.got_ref = bf16[16,8,640]{2,1,0:T(8,128)(2,1)S(1)} async-done(((bf16[16,8,640]{2,1,0:T(8,128)(2,1)}), bf16[16,8,640]{2,1,0:T(8,128)(2,1)S(1)}, u32[]{:S(2)}, u32[]{:S(2)}) %all-to-all-start.2) | async-done | bytes 163872 | tf_op jit(solution)/shard_map/all_to_all | solution.py:496
  123.6 0.1 shard_map.92.mine_ref
  123.7 2.5 %collective-permute-start.3 = (f32[24,768]{1,0:T(8,128)S(1)}, f32[24,768]{1,0:T(8,128)S(1)}, u32[]{:S(2)}, u32[]{:S(2)}) collective-permute-start(f32[24,768]{1,0:T(8,128)S(1)} %shard_map.92.mine_ref), channel_id=1, source_target_pairs={{0,256},{256,0},{1,257},{257,1},{2,258},{258,2},{3,259},{259,3},{4... | collective-permute-start | bytes 221192 | tf_op jit(solution)/shard_map/ppermute | solution.py:504
  126.2 4.1 %collective-permute-done.3.theirs_ref = f32[24,768]{1,0:T(8,128)S(1)} collective-permute-done((f32[24,768]{1,0:T(8,128)S(1)}, f32[24,768]{1,0:T(8,128)S(1)}, u32[]{:S(2)}, u32[]{:S(2)}) %collective-permute-start.3) | collective-permute-done | bytes 73760 | tf_op jit(solution)/shard_map/ppermute | solution.py:504
  130.3 0.8 shard_map.93
  131.1 7.6 %all-to-all-start.3 = ((bf16[16,8,640]{2,1,0:T(8,128)(2,1)}), bf16[16,8,640]{2,1,0:T(8,128)(2,1)S(1)}, u32[]{:S(2)}, u32[]{:S(2)}) async-start(bf16[16,8,640]{2,1,0:T(8,128)(2,1)} %get-tuple-element.47), calls=%async_computation.3 | async-start | bytes 327680 | tf_op jit(solution)/shard_map/all_to_all | solution.py:508
  138.8 2.1 %collective-permute-start.6 = (f32[32,768]{1,0:T(8,128)S(1)}, f32[32,768]{1,0:T(8,128)S(1)}, u32[]{:S(2)}, u32[]{:S(2)}) collective-permute-start(f32[32,768]{1,0:T(8,128)S(1)} %get-tuple-element.50.r0_ref), channel_id=1, source_target_pairs={{0,5},{1,4},{2,7},{3,6},{4,1},{5,0},{6,3},{7,2},{8,13},{9,12},{10,... | collective-permute-start | bytes 294920 | tf_op jit(solution)/shard_map/ppermute | solution.py:499
  140.9 3.2 %collective-permute-start.5 = (f32[32,768]{1,0:T(8,128)S(1)}, f32[32,768]{1,0:T(8,128)S(1)}, u32[]{:S(2)}, u32[]{:S(2)}) collective-permute-start(f32[32,768]{1,0:T(8,128)S(1)} %get-tuple-element.50.r0_ref), channel_id=1, source_target_pairs={{0,1},{1,0},{2,3},{3,2},{4,5},{5,4},{6,7},{7,6},{8,9},{9,8},{10,11... | collective-permute-start | bytes 294920 | tf_op jit(solution)/shard_map/ppermute | solution.py:499
  144.1 3.1 %collective-permute-start.4 = (f32[32,768]{1,0:T(8,128)S(1)}, f32[32,768]{1,0:T(8,128)S(1)}, u32[]{:S(2)}, u32[]{:S(2)}) collective-permute-start(f32[32,768]{1,0:T(8,128)S(1)} %get-tuple-element.50.r0_ref), channel_id=1, source_target_pairs={{0,4},{1,5},{2,6},{3,7},{4,0},{5,1},{6,2},{7,3},{8,12},{9,13},{10,... | collective-permute-start | bytes 294920 | tf_op jit(solution)/shard_map/ppermute | solution.py:499
  147.2 0.0 collective-permute-done.6.r3_ref
  147.2 0.2 collective-permute-done.5.r2_ref
  147.3 2.4 %collective-permute-done.4.r1_ref = f32[32,768]{1,0:T(8,128)S(1)} collective-permute-done((f32[32,768]{1,0:T(8,128)S(1)}, f32[32,768]{1,0:T(8,128)S(1)}, u32[]{:S(2)}, u32[]{:S(2)}) %collective-permute-start.4) | collective-permute-done | bytes 98336 | tf_op jit(solution)/shard_map/ppermute | solution.py:499
  149.7 1.2 all-to-all-done.3.own_ref
  150.9 6.4 %collective-permute-start.7 = (bf16[16,8,640]{2,1,0:T(8,128)(2,1)S(1)}, bf16[16,8,640]{2,1,0:T(8,128)(2,1)S(1)}, u32[]{:S(2)}, u32[]{:S(2)}) collective-permute-start(bf16[16,8,640]{2,1,0:T(8,128)(2,1)S(1)} %all-to-all-done.3.own_ref), channel_id=1, source_target_pairs={{0,8},{8,0},{1,9},{9,1},{2,10},{10,2},{3,11},{11,3},{4,12},{12,4},... | collective-permute-start | bytes 491528 | tf_op jit(solution)/shard_map/ppermute | solution.py:510
  157.4 1.0 collective-permute-done.7.other_ref
  158.4 1.7 %shard_map.94 = (f32[128,768]{1,0:T(8,128)}, f32[128,1024]{1,0:T(8,128)}) custom-call(s32[4]{0:T(128)S(1)} %pad_add_fusion.place_ref, bf16[16,8,640]{2,1,0:T(8,128)(2,1)S(1)} %all-to-all-done.3.own_ref, bf16[16,8,640]{2,1,0:T(8,128)(2,1)S(1)} %collective-permute-done.7.other_ref, f32[32,768]{1,0:T(8,128)S(1)} %get-tuple-element.50.r0_ref, ...), custom_call_target="tpu_custom_call" | custom-call | bytes 2097152 | tf_op jit(solution)/shard_map/pallas_call | solution.py:511
Async XLA Ops:
  33.9 1.9 %copy-start = (bf16[2,1024,768]{2,1,0:T(8,128)(2,1)S(1)}, bf16[2,1024,768]{2,1,0:T(8,128)(2,1)}, u32[]{:S(2)}) copy-start(bf16[2,1024,768]{2,1,0:T(8,128)(2,1)} %base_ref.3) | copy-start | bytes 9437188
  40.6 7.7 %copy-start.1 = (bf16[2,1024,768]{2,1,0:T(8,128)(2,1)S(1)}, bf16[2,1024,768]{2,1,0:T(8,128)(2,1)}, u32[]{:S(2)}) copy-start(bf16[2,1024,768]{2,1,0:T(8,128)(2,1)} %base_ref.3) | copy-start | bytes 9437188
  40.6 7.7 %collective-permute-start = (bf16[256,1024]{1,0:T(8,128)(2,1)S(1)}, bf16[256,1024]{1,0:T(8,128)(2,1)S(1)}, u32[]{:S(2)}, u32[]{:S(2)}) collective-permute-start(bf16[256,1024]{1,0:T(8,128)(2,1)S(1)} %all_gather.3.refs_0_.own_ref), channel_id=1, source_target_pairs={{0,8},{8,0},{1,9},{9,1},{2,10},{10,2},{3,11},{11,3},{4,12},{12,4},... | collective-permute-start | bytes 1572872 | tf_op jit(solution)/shard_map/ppermute | solution.py:455
  50.9 24.4 %copy-start.2 = (bf16[64,768]{1,0:T(8,128)(2,1)S(1)}, bf16[64,768]{1,0:T(8,128)(2,1)}, u32[]{:S(2)}) copy-start(bf16[64,768]{1,0:T(8,128)(2,1)} %cot_ref.1) | copy-start | bytes 294916
  50.9 24.4 %copy-start.3 = (f32[2,768]{1,0:T(2,128)S(1)}, f32[2,768]{1,0:T(2,128)}, u32[]{:S(2)}) copy-start(f32[2,768]{1,0:T(2,128)} %mag_ref.3) | copy-start | bytes 18436
  95.0 9.2 %collective-permute-start.1 = (f32[128,512]{1,0:T(8,128)S(1)}, f32[128,512]{1,0:T(8,128)S(1)}, u32[]{:S(2)}, u32[]{:S(2)}) collective-permute-start(f32[128,512]{1,0:T(8,128)S(1)} %get-tuple-element.45), channel_id=1, source_target_pairs={{0,8},{8,0},{1,9},{9,1},{2,10},{10,2},{3,11},{11,3},{4,12},{12,4},... | collective-permute-start | bytes 786440 | tf_op jit(solution)/shard_map/ppermute | solution.py:493
  105.0 18.6 %all-to-all-start.2 = ((bf16[16,8,640]{2,1,0:T(8,128)(2,1)}), bf16[16,8,640]{2,1,0:T(8,128)(2,1)S(1)}, u32[]{:S(2)}, u32[]{:S(2)}) async-start(bf16[16,8,640]{2,1,0:T(8,128)(2,1)} %shard_map.90), calls=%async_computation.2 | async-start | bytes 327680 | tf_op jit(solution)/shard_map/all_to_all | solution.py:496
  112.1 6.4 %collective-permute-start.2 = (f32[8,768]{1,0:T(8,128)S(1)}, f32[8,768]{1,0:T(8,128)S(1)}, u32[]{:S(2)}, u32[]{:S(2)}) collective-permute-start(f32[8,768]{1,0:T(8,128)S(1)} %shard_map.91.rows_ref), channel_id=1, source_target_pairs={{0,2},{1,3},{2,0},{3,1},{4,6},{5,7},{6,4},{7,5},{8,10},{9,11},{10,... | collective-permute-start | bytes 73736 | tf_op jit(solution)/shard_map/ppermute | solution.py:499
  123.7 6.6 %collective-permute-start.3 = (f32[24,768]{1,0:T(8,128)S(1)}, f32[24,768]{1,0:T(8,128)S(1)}, u32[]{:S(2)}, u32[]{:S(2)}) collective-permute-start(f32[24,768]{1,0:T(8,128)S(1)} %shard_map.92.mine_ref), channel_id=1, source_target_pairs={{0,256},{256,0},{1,257},{257,1},{2,258},{258,2},{3,259},{259,3},{4... | collective-permute-start | bytes 221192 | tf_op jit(solution)/shard_map/ppermute | solution.py:504
  131.1 19.8 %all-to-all-start.3 = ((bf16[16,8,640]{2,1,0:T(8,128)(2,1)}), bf16[16,8,640]{2,1,0:T(8,128)(2,1)S(1)}, u32[]{:S(2)}, u32[]{:S(2)}) async-start(bf16[16,8,640]{2,1,0:T(8,128)(2,1)} %get-tuple-element.47), calls=%async_computation.3 | async-start | bytes 327680 | tf_op jit(solution)/shard_map/all_to_all | solution.py:508
  138.8 8.4 %collective-permute-start.6 = (f32[32,768]{1,0:T(8,128)S(1)}, f32[32,768]{1,0:T(8,128)S(1)}, u32[]{:S(2)}, u32[]{:S(2)}) collective-permute-start(f32[32,768]{1,0:T(8,128)S(1)} %get-tuple-element.50.r0_ref), channel_id=1, source_target_pairs={{0,5},{1,4},{2,7},{3,6},{4,1},{5,0},{6,3},{7,2},{8,13},{9,12},{10,... | collective-permute-start | bytes 294920 | tf_op jit(solution)/shard_map/ppermute | solution.py:499
  140.9 6.4 %collective-permute-start.5 = (f32[32,768]{1,0:T(8,128)S(1)}, f32[32,768]{1,0:T(8,128)S(1)}, u32[]{:S(2)}, u32[]{:S(2)}) collective-permute-start(f32[32,768]{1,0:T(8,128)S(1)} %get-tuple-element.50.r0_ref), channel_id=1, source_target_pairs={{0,1},{1,0},{2,3},{3,2},{4,5},{5,4},{6,7},{7,6},{8,9},{9,8},{10,11... | collective-permute-start | bytes 294920 | tf_op jit(solution)/shard_map/ppermute | solution.py:499
  144.1 5.7 %collective-permute-start.4 = (f32[32,768]{1,0:T(8,128)S(1)}, f32[32,768]{1,0:T(8,128)S(1)}, u32[]{:S(2)}, u32[]{:S(2)}) collective-permute-start(f32[32,768]{1,0:T(8,128)S(1)} %get-tuple-element.50.r0_ref), channel_id=1, source_target_pairs={{0,4},{1,5},{2,6},{3,7},{4,0},{5,1},{6,2},{7,3},{8,12},{9,13},{10,... | collective-permute-start | bytes 294920 | tf_op jit(solution)/shard_map/ppermute | solution.py:499
  150.9 7.5 %collective-permute-start.7 = (bf16[16,8,640]{2,1,0:T(8,128)(2,1)S(1)}, bf16[16,8,640]{2,1,0:T(8,128)(2,1)S(1)}, u32[]{:S(2)}, u32[]{:S(2)}) collective-permute-start(bf16[16,8,640]{2,1,0:T(8,128)(2,1)S(1)} %all-to-all-done.3.own_ref), channel_id=1, source_target_pairs={{0,8},{8,0},{1,9},{9,1},{2,10},{10,2},{3,11},{11,3},{4,12},{12,4},... | collective-permute-start | bytes 491528 | tf_op jit(solution)/shard_map/ppermute | solution.py:510

commit v9 on v8

--- a/solution.py
+++ b/solution.py
@@ -272,9 +272,21 @@
     out_ref[:, at_back:, :] = jnp.broadcast_to(rest[None], (members,) + rest.shape)
 
 
+def packed(value):
+    peak = peak_of(value)
+    tail = jnp.broadcast_to(peak, (value.shape[0], 128))
+    return jnp.concatenate([encode(value, peak), tail], axis=1).astype(BF16)
+
+
+def unpacked(code):
+    width = code.shape[1] - 128
+    return decode(code[:, :width], code[0:1, width : width + 1].astype(F32))
+
+
 def rows_kernel(place_ref, got_ref, coeff_ref, rows_ref):
     members = got_ref.shape[0]
-    rows, columns = rows_ref.shape
+    rows = rows_ref.shape[0]
+    columns = coeff_ref.shape[1]
     tiles = columns // 128
     height = rows * (tiles + tiles // 2 + 1)
     coeff = jnp.where(place_ref[2] < 2, coeff_ref[0:1, :], coeff_ref[1:2, :])
@@ -290,9 +302,8 @@
         first = j % 2 * (tiles // 2)
         for i in range(tiles // 2):
             crosses[first + i] = crosses[first + i] + cross[rows * i : rows * (i + 1)]
-    for i in range(tiles):
-        lanes = slice(128 * i, 128 * (i + 1))
-        rows_ref[:, lanes] = tokens[i] + crosses[i] * coeff[:, lanes]
+    own = jnp.concatenate(tokens, axis=1) + jnp.concatenate(crosses, axis=1) * coeff
+    rows_ref[...] = packed(own)
 
 
 def width_kernel(
@@ -367,32 +378,30 @@
 
 
 def piece_kernel(got_ref, rows_ref, far_ref, out_ref):
-    rows, width = got_ref.shape[1], got_ref.shape[2] - 128
-    columns = out_ref.shape[1]
-    out_ref[:rows, :width] = jnp.sum(decoded(got_ref), axis=0)
-    out_ref[:rows, width:] = jnp.zeros((rows, columns - width), F32)
-    out_ref[rows : 2 * rows, :] = rows_ref[...]
-    out_ref[2 * rows :, :] = far_ref[...]
+    width = got_ref.shape[2]
+    lanes = rows_ref.shape[1]
+    out_ref[:, :width] = packed(jnp.sum(decoded(got_ref), axis=0))
+    out_ref[:, width : width + lanes] = rows_ref[...]
+    out_ref[:, width + lanes :] = far_ref[...]
 
 
 def spread_kernel(mine_ref, theirs_ref, out_ref, rows_ref):
-    zs, rows, lanes = out_ref.shape
-    width = lanes - 128
-    piece = mine_ref[:rows, :width] + theirs_ref[:rows, :width]
-    peak = peak_of(piece)
-    code = jnp.concatenate([encode(piece, peak), jnp.broadcast_to(peak, (rows, 128))], axis=1)
-    out_ref[...] = jnp.broadcast_to(code[None], (zs, rows, lanes)).astype(BF16)
-    rows_ref[: 2 * rows, :] = mine_ref[rows:, :]
-    rows_ref[2 * rows :, :] = theirs_ref[rows:, :]
+    width = out_ref.shape[2]
+    lanes = rows_ref.shape[1] // 2
+    code = packed(unpacked(mine_ref[:, :width]) + unpacked(theirs_ref[:, :width]))
+    out_ref[...] = jnp.broadcast_to(code[None], out_ref.shape)
+    rows_ref[:, :lanes] = mine_ref[:, width:]
+    rows_ref[:, lanes:] = theirs_ref[:, width:]
 
 
 def last_kernel(place_ref, own_ref, other_ref, r0_ref, r1_ref, r2_ref, r3_ref, grad_a_ref, grad_b_ref):
     core, member = place_ref[1], place_ref[3]
     count = own_ref.shape[1]
+    lanes = r0_ref.shape[1] // 4
     for near, ref in enumerate((r0_ref, r1_ref, r2_ref, r3_ref)):
         for i, far in enumerate((0, 8, 1, 9)):
             at = pl.multiple_of(jnp.bitwise_xor(member, 2 * near + far) * count, count)
-            grad_a_ref[pl.ds(at, count), :] = ref[count * i : count * (i + 1), :]
+            grad_a_ref[pl.ds(at, count), :] = unpacked(ref[:, lanes * i : lanes * (i + 1)])
     rows, columns = grad_b_ref.shape
     width = columns // 2
     for side, ref in ((core, own_ref), (1 - core, other_ref)):
@@ -484,7 +493,7 @@
     )(place, got, norm, magnitude, g_own, g_other, base, low)
     a_rows = call(
         rows_kernel,
-        shape((rows, columns)),
+        shape((rows, columns + 128), BF16),
         [SMEM] + [VMEM] * 2,
         flops=2**22,
         size=2**20,
@@ -498,12 +507,12 @@
     def across(value, flip):
         return lax.ppermute(value, ("y", "x"), [(i, i ^ flip) for i in range(shards)])
 
-    piece = call(piece_kernel, shape((3 * rows, columns)), [VMEM] * 3, size=2**18)(
-        got, a_rows, across(a_rows, 2)
-    )
+    piece = call(
+        piece_kernel, shape((rows, dims[2] + 2 * (columns + 128)), BF16), [VMEM] * 3, size=2**18
+    )(got, a_rows, across(a_rows, 2))
     theirs = lax.ppermute(piece, "dp", swap)
     chunks, near = call(
-        spread_kernel, [shape(dims, BF16), shape((4 * rows, columns))], [VMEM] * 2, size=2**18
+        spread_kernel, [shape(dims, BF16), shape((rows, 4 * (columns + 128)), BF16)], [VMEM] * 2, size=2**18
     )(piece, theirs)
     full = lax.all_to_all(chunks, "z", 0, 0)
     full, *near = lax.optimization_barrier((full, near, across(near, 4), across(near, 1), across(near, 5)))

time: 161 us -> 161 us (level)
  transfers between devices with their start and end apart: 10 -> 10, of which waited for: 9 -> 8; matrix products, arithmetic and copies ran while one was open for 0% -> 0% of each run, Pallas kernels for 1% -> 1%
where the time goes in v9:
time: 161 us; the launch traced here: 160 us
  blocking collectives  71 us (44%)
  starting transfers between devices  48.1 us (30%)
  waiting for transfers between devices  19.2 us (12%)
  Pallas kernels  17.7 us (11%)
  local copies, waits for them, and re-layouts  1.9 us (1%)
    all_gather x1, blocking collectives, per_device(): g_own = lax.all_gather(tokens, 'z', axis=0, tiled=True)  32.1 us
    all_to_all x1, blocking collectives, per_device(): got = lax.all_to_all(payload, WIDTH, 0, 0)  24.3 us
    all_to_all x1, blocking collectives, per_device(): got = lax.all_to_all(sends, GROUP, 0, 0)  14.6 us
    ppermute x4, starting transfers between devices, across(): lax.ppermute(value, ('y', 'x'), [(i, i ^ flip) for i in range(shards)])  11.2 us
    ppermute x1, starting transfers between devices, per_device(): theirs = lax.ppermute(theirs, 'core', swap)  8.01 us
    all_to_all x1, starting transfers between devices, per_device(): full = lax.all_to_all(chunks, 'z', 0, 0)  7.61 us
    ppermute x1, starting transfers between devices, per_device(): other = lax.ppermute(full, 'core', swap)  6.44 us
    ppermute x1, starting transfers between devices, per_device(): g_other = lax.ppermute(g_own, 'core', swap)  6.17 us
  transfers between devices with their start and end apart: 10, of which 8 were waited for; matrix products, arithmetic and copies ran while one was open for 0% of the time, Pallas kernels for 1%

profile of v9, /device:TPU:1, one launch (start us, length us, event | category | flops | bytes accessed | tf_op | source)
XLA Modules:
  0.0 159.9 jit_solution(13812829049342168262)
XLA Ops:
  0.6 32.1 %all_gather.3.refs_0_.own_ref = bf16[256,1024]{1,0:T(8,128)(2,1)S(1)} all-gather(bf16[16,1024]{1,0:T(8,128)(2,1)} %param.6), channel_id=1, replica_groups=mesh['dp'=2,'z'=16,'core'=2,'y'=2,'x'=4] {'z'}, dimensions={0}, use_global_device_ids=true | all-gather | bytes 557056 | tf_op jit(solution)/shard_map/all_gather | solution.py:443
  32.7 0.1 pad_add_fusion.place_ref
  32.8 1.1 pad_maximum_fusion.refs_2_.low_ref
  33.9 0.0 copy-start
  33.9 1.9 %copy-done = bf16[2,1024,768]{2,1,0:T(8,128)(2,1)S(1)} copy-done((bf16[2,1024,768]{2,1,0:T(8,128)(2,1)S(1)}, bf16[2,1024,768]{2,1,0:T(8,128)(2,1)}, u32[]{:S(2)}) %copy-start) | copy-done | bytes 3145752
  35.8 4.8 %shard_map.85 = (bf16[8,416,128]{2,1,0:T(8,128)(2,1)S(1)}, f32[128,768]{1,0:T(8,128)S(1)}, f32[32,128]{1,0:T(8,128)S(1)}) custom-call(s32[4]{0:T(128)S(1)} %pad_add_fusion.place_ref, bf16[256,1024]{1,0:T(8,128)(2,1)S(1)} %all_gather.3.refs_0_.own_ref, bf16[2,1024,768]{2,1,0:T(8,128)(2,1)S(1)} %copy-done, bf16[2,64,1792]{2,1,0:T(8,128)(2,1)S(1)} %pad_maximum_fusion.refs_2_.low_ref), custom_call_target="tpu_custom_call" | custom-call | flops 1073741824 | bytes 4194304 | tf_op jit(solution)/shard_map/pallas_call | solution.py:462
  40.6 0.0 copy-start.1
  40.6 6.2 %collective-permute-start = (bf16[256,1024]{1,0:T(8,128)(2,1)S(1)}, bf16[256,1024]{1,0:T(8,128)(2,1)S(1)}, u32[]{:S(2)}, u32[]{:S(2)}) collective-permute-start(bf16[256,1024]{1,0:T(8,128)(2,1)S(1)} %all_gather.3.refs_0_.own_ref), channel_id=1, source_target_pairs={{0,8},{8,0},{1,9},{9,1},{2,10},{10,2},{3,11},{11,3},{4,12},{12,4},... | collective-permute-start | bytes 1572872 | tf_op jit(solution)/shard_map/ppermute | solution.py:464
  46.8 0.6 shard_map.86
  47.3 1.0 collective-permute-done.other_ref
  48.3 0.0 copy-done.1
  48.3 2.7 %shard_map.87 = bf16[8,864,128]{2,1,0:T(8,128)(2,1)S(1)} custom-call(s32[4]{0:T(128)S(1)} %pad_add_fusion.place_ref, bf16[8,416,128]{2,1,0:T(8,128)(2,1)S(1)} %get-tuple-element.35.early_part, f32[32,128]{1,0:T(8,128)S(1)} %get-tuple-element.36.early_info, bf16[8,416,128]{2,1,0:T(8,128)(2,1)S(1)} %get-tuple-element.38.late_part, ...), custom_call_target="tpu_custom_call" | custom-call | flops 1073741824 | bytes 8388608 | tf_op jit(solution)/shard_map/pallas_call | solution.py:466
  50.9 0.0 copy-start.2
  50.9 0.0 copy-start.3
  51.0 24.3 %all_to_all.20.got_ref = bf16[8,864,128]{2,1,0:T(8,128)(2,1)S(1)} all-to-all(bf16[8,864,128]{2,1,0:T(8,128)(2,1)S(1)} %shard_map.87), channel_id=1, replica_groups=mesh['dp'=2,'z'=16,'core'=2,'y'=2,'x'=4] {'x','y'}, dimensions={0} | all-to-all | bytes 3538944 | tf_op jit(solution)/shard_map/all_to_all | solution.py:474
  75.3 0.0 copy-done.2
  75.3 0.0 copy-done.3
  75.3 3.2 %shard_map.88 = (bf16[16,152,128]{2,1,0:T(8,128)(2,1)S(1)}, f32[2,768]{1,0:T(2,128)S(1)}) custom-call(s32[4]{0:T(128)S(1)} %pad_add_fusion.place_ref, bf16[8,864,128]{2,1,0:T(8,128)(2,1)S(1)} %all_to_all.20.got_ref, bf16[64,768]{1,0:T(8,128)(2,1)S(1)} %copy-done.2, bf16[2,64,1792]{2,1,0:T(8,128)(2,1)S(1)} %pad_maximum_fusion.refs_2_.low_ref, ...), custom_call_target="tpu_custom_call" | custom-call | flops 134217728 | bytes 4194304 | tf_op jit(solution)/shard_map/pallas_call | solution.py:477
  78.5 14.6 %all_to_all.21.got_ref = bf16[16,152,128]{2,1,0:T(8,128)(2,1)S(1)} all-to-all(bf16[16,152,128]{2,1,0:T(8,128)(2,1)S(1)} %get-tuple-element.42), channel_id=1, replica_groups=mesh['dp'=2,'z'=16,'core'=2,'y'=2,'x'=4] {'x','y','dp'}, dimensions={0} | all-to-all | bytes 1245184 | tf_op jit(solution)/shard_map/all_to_all | solution.py:484
  93.1 1.8 %shard_map.89 = (f32[128,512]{1,0:T(8,128)S(1)}, f32[128,512]{1,0:T(8,128)S(1)}, f32[2,768]{1,0:T(2,128)}, f32[2,768]{1,0:T(2,128)S(1)}) custom-call(s32[4]{0:T(128)S(1)} %pad_add_fusion.place_ref, bf16[16,152,128]{2,1,0:T(8,128)(2,1)S(1)} %all_to_all.21.got_ref, f32[2,768]{1,0:T(2,128)S(1)} %get-tuple-element.43.norm_ref, f32[2,768]{1,0:T(2,128)S(1)} %copy-done.3, ...), custom_call_target="tpu_custom_call" | custom-call | flops 1073741824 | bytes 8388608 | tf_op jit(solution)/shard_map/pallas_call | solution.py:486
  95.0 8.0 %collective-permute-start.1 = (f32[128,512]{1,0:T(8,128)S(1)}, f32[128,512]{1,0:T(8,128)S(1)}, u32[]{:S(2)}, u32[]{:S(2)}) collective-permute-start(f32[128,512]{1,0:T(8,128)S(1)} %get-tuple-element.45), channel_id=1, source_target_pairs={{0,8},{8,0},{1,9},{9,1},{2,10},{10,2},{3,11},{11,3},{4,12},{12,4},... | collective-permute-start | bytes 786440 | tf_op jit(solution)/shard_map/ppermute | solution.py:502
  103.0 1.1 collective-permute-done.1.theirs_ref
  104.1 0.9 shard_map.90
  105.0 6.2 %all-to-all-start.2 = ((bf16[16,8,640]{2,1,0:T(8,128)(2,1)}), bf16[16,8,640]{2,1,0:T(8,128)(2,1)S(1)}, u32[]{:S(2)}, u32[]{:S(2)}) async-start(bf16[16,8,640]{2,1,0:T(8,128)(2,1)} %shard_map.90), calls=%async_computation.2 | async-start | bytes 327680 | tf_op jit(solution)/shard_map/all_to_all | solution.py:505
  111.2 1.0 shard_map.91.rows_ref
  112.2 2.8 %collective-permute-start.2 = (bf16[8,896]{1,0:T(8,128)(2,1)S(1)}, bf16[8,896]{1,0:T(8,128)(2,1)S(1)}, u32[]{:S(2)}, u32[]{:S(2)}) collective-permute-start(bf16[8,896]{1,0:T(8,128)(2,1)S(1)} %shard_map.91.rows_ref), channel_id=1, source_target_pairs={{0,2},{1,3},{2,0},{3,1},{4,6},{5,7},{6,4},{7,5},{8,10},{9,11},{10,... | collective-permute-start | bytes 43016 | tf_op jit(solution)/shard_map/ppermute | solution.py:508
  115.0 3.4 %collective-permute-done.2.far_ref = bf16[8,896]{1,0:T(8,128)(2,1)S(1)} collective-permute-done((bf16[8,896]{1,0:T(8,128)(2,1)S(1)}, bf16[8,896]{1,0:T(8,128)(2,1)S(1)}, u32[]{:S(2)}, u32[]{:S(2)}) %collective-permute-start.2) | collective-permute-done | bytes 14368 | tf_op jit(solution)/shard_map/ppermute | solution.py:508
  118.4 5.2 %all-to-all-done.2.got_ref = bf16[16,8,640]{2,1,0:T(8,128)(2,1)S(1)} async-done(((bf16[16,8,640]{2,1,0:T(8,128)(2,1)}), bf16[16,8,640]{2,1,0:T(8,128)(2,1)S(1)}, u32[]{:S(2)}, u32[]{:S(2)}) %all-to-all-start.2) | async-done | bytes 163872 | tf_op jit(solution)/shard_map/all_to_all | solution.py:505
  123.6 0.2 shard_map.92.mine_ref
  123.9 2.5 %collective-permute-start.3 = (bf16[8,2432]{1,0:T(8,128)(2,1)S(1)}, bf16[8,2432]{1,0:T(8,128)(2,1)S(1)}, u32[]{:S(2)}, u32[]{:S(2)}) collective-permute-start(bf16[8,2432]{1,0:T(8,128)(2,1)S(1)} %shard_map.92.mine_ref), channel_id=1, source_target_pairs={{0,256},{256,0},{1,257},{257,1},{2,258},{258,2},{3,259},{259,3},{4... | collective-permute-start | bytes 116744 | tf_op jit(solution)/shard_map/ppermute | solution.py:513
  126.3 3.7 %collective-permute-done.3.theirs_ref = bf16[8,2432]{1,0:T(8,128)(2,1)S(1)} collective-permute-done((bf16[8,2432]{1,0:T(8,128)(2,1)S(1)}, bf16[8,2432]{1,0:T(8,128)(2,1)S(1)}, u32[]{:S(2)}, u32[]{:S(2)}) %collective-permute-start.3) | collective-permute-done | bytes 38944 | tf_op jit(solution)/shard_map/ppermute | solution.py:513
  130.1 0.8 shard_map.93
  130.9 7.6 %all-to-all-start.3 = ((bf16[16,8,640]{2,1,0:T(8,128)(2,1)}), bf16[16,8,640]{2,1,0:T(8,128)(2,1)S(1)}, u32[]{:S(2)}, u32[]{:S(2)}) async-start(bf16[16,8,640]{2,1,0:T(8,128)(2,1)} %get-tuple-element.47), calls=%async_computation.3 | async-start | bytes 327680 | tf_op jit(solution)/shard_map/all_to_all | solution.py:517
  138.5 2.1 %collective-permute-start.6 = (bf16[8,3584]{1,0:T(8,128)(2,1)S(1)}, bf16[8,3584]{1,0:T(8,128)(2,1)S(1)}, u32[]{:S(2)}, u32[]{:S(2)}) collective-permute-start(bf16[8,3584]{1,0:T(8,128)(2,1)S(1)} %get-tuple-element.50.r0_ref), channel_id=1, source_target_pairs={{0,5},{1,4},{2,7},{3,6},{4,1},{5,0},{6,3},{7,2},{8,13},{9,12},{10,... | collective-permute-start | bytes 172040 | tf_op jit(solution)/shard_map/ppermute | solution.py:508
  140.7 3.2 %collective-permute-start.5 = (bf16[8,3584]{1,0:T(8,128)(2,1)S(1)}, bf16[8,3584]{1,0:T(8,128)(2,1)S(1)}, u32[]{:S(2)}, u32[]{:S(2)}) collective-permute-start(bf16[8,3584]{1,0:T(8,128)(2,1)S(1)} %get-tuple-element.50.r0_ref), channel_id=1, source_target_pairs={{0,1},{1,0},{2,3},{3,2},{4,5},{5,4},{6,7},{7,6},{8,9},{9,8},{10,11... | collective-permute-start | bytes 172040 | tf_op jit(solution)/shard_map/ppermute | solution.py:508
  143.8 3.1 %collective-permute-start.4 = (bf16[8,3584]{1,0:T(8,128)(2,1)S(1)}, bf16[8,3584]{1,0:T(8,128)(2,1)S(1)}, u32[]{:S(2)}, u32[]{:S(2)}) collective-permute-start(bf16[8,3584]{1,0:T(8,128)(2,1)S(1)} %get-tuple-element.50.r0_ref), channel_id=1, source_target_pairs={{0,4},{1,5},{2,6},{3,7},{4,0},{5,1},{6,2},{7,3},{8,12},{9,13},{10,... | collective-permute-start | bytes 172040 | tf_op jit(solution)/shard_map/ppermute | solution.py:508
  146.9 0.0 collective-permute-done.6.r3_ref
  146.9 0.0 collective-permute-done.5.r2_ref
  147.0 2.1 %collective-permute-done.4.r1_ref = bf16[8,3584]{1,0:T(8,128)(2,1)S(1)} collective-permute-done((bf16[8,3584]{1,0:T(8,128)(2,1)S(1)}, bf16[8,3584]{1,0:T(8,128)(2,1)S(1)}, u32[]{:S(2)}, u32[]{:S(2)}) %collective-permute-start.4) | collective-permute-done | bytes 57376 | tf_op jit(solution)/shard_map/ppermute | solution.py:508
  149.1 1.7 %all-to-all-done.3.own_ref = bf16[16,8,640]{2,1,0:T(8,128)(2,1)S(1)} async-done(((bf16[16,8,640]{2,1,0:T(8,128)(2,1)}), bf16[16,8,640]{2,1,0:T(8,128)(2,1)S(1)}, u32[]{:S(2)}, u32[]{:S(2)}) %all-to-all-start.3) | async-done | bytes 163872 | tf_op jit(solution)/shard_map/all_to_all | solution.py:517
  150.7 6.4 %collective-permute-start.7 = (bf16[16,8,640]{2,1,0:T(8,128)(2,1)S(1)}, bf16[16,8,640]{2,1,0:T(8,128)(2,1)S(1)}, u32[]{:S(2)}, u32[]{:S(2)}) collective-permute-start(bf16[16,8,640]{2,1,0:T(8,128)(2,1)S(1)} %all-to-all-done.3.own_ref), channel_id=1, source_target_pairs={{0,8},{8,0},{1,9},{9,1},{2,10},{10,2},{3,11},{11,3},{4,12},{12,4},... | collective-permute-start | bytes 491528 | tf_op jit(solution)/shard_map/ppermute | solution.py:519
  157.2 1.0 collective-permute-done.7.other_ref
  158.2 1.8 %shard_map.94 = (f32[128,768]{1,0:T(8,128)}, f32[128,1024]{1,0:T(8,128)}) custom-call(s32[4]{0:T(128)S(1)} %pad_add_fusion.place_ref, bf16[16,8,640]{2,1,0:T(8,128)(2,1)S(1)} %all-to-all-done.3.own_ref, bf16[16,8,640]{2,1,0:T(8,128)(2,1)S(1)} %collective-permute-done.7.other_ref, bf16[8,3584]{1,0:T(8,128)(2,1)S(1)} %get-tuple-element.50.r0_ref, ...), custom_call_target="tpu_custom_call" | custom-call | bytes 2097152 | tf_op jit(solution)/shard_map/pallas_call | solution.py:520
Async XLA Ops:
  33.9 1.9 %copy-start = (bf16[2,1024,768]{2,1,0:T(8,128)(2,1)S(1)}, bf16[2,1024,768]{2,1,0:T(8,128)(2,1)}, u32[]{:S(2)}) copy-start(bf16[2,1024,768]{2,1,0:T(8,128)(2,1)} %base_ref.3) | copy-start | bytes 9437188
  40.6 7.7 %copy-start.1 = (bf16[2,1024,768]{2,1,0:T(8,128)(2,1)S(1)}, bf16[2,1024,768]{2,1,0:T(8,128)(2,1)}, u32[]{:S(2)}) copy-start(bf16[2,1024,768]{2,1,0:T(8,128)(2,1)} %base_ref.3) | copy-start | bytes 9437188
  40.6 7.7 %collective-permute-start = (bf16[256,1024]{1,0:T(8,128)(2,1)S(1)}, bf16[256,1024]{1,0:T(8,128)(2,1)S(1)}, u32[]{:S(2)}, u32[]{:S(2)}) collective-permute-start(bf16[256,1024]{1,0:T(8,128)(2,1)S(1)} %all_gather.3.refs_0_.own_ref), channel_id=1, source_target_pairs={{0,8},{8,0},{1,9},{9,1},{2,10},{10,2},{3,11},{11,3},{4,12},{12,4},... | collective-permute-start | bytes 1572872 | tf_op jit(solution)/shard_map/ppermute | solution.py:464
  50.9 24.4 %copy-start.2 = (bf16[64,768]{1,0:T(8,128)(2,1)S(1)}, bf16[64,768]{1,0:T(8,128)(2,1)}, u32[]{:S(2)}) copy-start(bf16[64,768]{1,0:T(8,128)(2,1)} %cot_ref.1) | copy-start | bytes 294916
  50.9 24.4 %copy-start.3 = (f32[2,768]{1,0:T(2,128)S(1)}, f32[2,768]{1,0:T(2,128)}, u32[]{:S(2)}) copy-start(f32[2,768]{1,0:T(2,128)} %mag_ref.3) | copy-start | bytes 18436
  95.0 9.2 %collective-permute-start.1 = (f32[128,512]{1,0:T(8,128)S(1)}, f32[128,512]{1,0:T(8,128)S(1)}, u32[]{:S(2)}, u32[]{:S(2)}) collective-permute-start(f32[128,512]{1,0:T(8,128)S(1)} %get-tuple-element.45), channel_id=1, source_target_pairs={{0,8},{8,0},{1,9},{9,1},{2,10},{10,2},{3,11},{11,3},{4,12},{12,4},... | collective-permute-start | bytes 786440 | tf_op jit(solution)/shard_map/ppermute | solution.py:502
  105.0 18.6 %all-to-all-start.2 = ((bf16[16,8,640]{2,1,0:T(8,128)(2,1)}), bf16[16,8,640]{2,1,0:T(8,128)(2,1)S(1)}, u32[]{:S(2)}, u32[]{:S(2)}) async-start(bf16[16,8,640]{2,1,0:T(8,128)(2,1)} %shard_map.90), calls=%async_computation.2 | async-start | bytes 327680 | tf_op jit(solution)/shard_map/all_to_all | solution.py:505
  112.2 6.3 %collective-permute-start.2 = (bf16[8,896]{1,0:T(8,128)(2,1)S(1)}, bf16[8,896]{1,0:T(8,128)(2,1)S(1)}, u32[]{:S(2)}, u32[]{:S(2)}) collective-permute-start(bf16[8,896]{1,0:T(8,128)(2,1)S(1)} %shard_map.91.rows_ref), channel_id=1, source_target_pairs={{0,2},{1,3},{2,0},{3,1},{4,6},{5,7},{6,4},{7,5},{8,10},{9,11},{10,... | collective-permute-start | bytes 43016 | tf_op jit(solution)/shard_map/ppermute | solution.py:508
  123.9 6.2 %collective-permute-start.3 = (bf16[8,2432]{1,0:T(8,128)(2,1)S(1)}, bf16[8,2432]{1,0:T(8,128)(2,1)S(1)}, u32[]{:S(2)}, u32[]{:S(2)}) collective-permute-start(bf16[8,2432]{1,0:T(8,128)(2,1)S(1)} %shard_map.92.mine_ref), channel_id=1, source_target_pairs={{0,256},{256,0},{1,257},{257,1},{2,258},{258,2},{3,259},{259,3},{4... | collective-permute-start | bytes 116744 | tf_op jit(solution)/shard_map/ppermute | solution.py:513
  130.9 19.8 %all-to-all-start.3 = ((bf16[16,8,640]{2,1,0:T(8,128)(2,1)}), bf16[16,8,640]{2,1,0:T(8,128)(2,1)S(1)}, u32[]{:S(2)}, u32[]{:S(2)}) async-start(bf16[16,8,640]{2,1,0:T(8,128)(2,1)} %get-tuple-element.47), calls=%async_computation.3 | async-start | bytes 327680 | tf_op jit(solution)/shard_map/all_to_all | solution.py:517
  138.5 8.4 %collective-permute-start.6 = (bf16[8,3584]{1,0:T(8,128)(2,1)S(1)}, bf16[8,3584]{1,0:T(8,128)(2,1)S(1)}, u32[]{:S(2)}, u32[]{:S(2)}) collective-permute-start(bf16[8,3584]{1,0:T(8,128)(2,1)S(1)} %get-tuple-element.50.r0_ref), channel_id=1, source_target_pairs={{0,5},{1,4},{2,7},{3,6},{4,1},{5,0},{6,3},{7,2},{8,13},{9,12},{10,... | collective-permute-start | bytes 172040 | tf_op jit(solution)/shard_map/ppermute | solution.py:508
  140.7 6.3 %collective-permute-start.5 = (bf16[8,3584]{1,0:T(8,128)(2,1)S(1)}, bf16[8,3584]{1,0:T(8,128)(2,1)S(1)}, u32[]{:S(2)}, u32[]{:S(2)}) collective-permute-start(bf16[8,3584]{1,0:T(8,128)(2,1)S(1)} %get-tuple-element.50.r0_ref), channel_id=1, source_target_pairs={{0,1},{1,0},{2,3},{3,2},{4,5},{5,4},{6,7},{7,6},{8,9},{9,8},{10,11... | collective-permute-start | bytes 172040 | tf_op jit(solution)/shard_map/ppermute | solution.py:508
  143.8 5.2 %collective-permute-start.4 = (bf16[8,3584]{1,0:T(8,128)(2,1)S(1)}, bf16[8,3584]{1,0:T(8,128)(2,1)S(1)}, u32[]{:S(2)}, u32[]{:S(2)}) collective-permute-start(bf16[8,3584]{1,0:T(8,128)(2,1)S(1)} %get-tuple-element.50.r0_ref), channel_id=1, source_target_pairs={{0,4},{1,5},{2,6},{3,7},{4,0},{5,1},{6,2},{7,3},{8,12},{9,13},{10,... | collective-permute-start | bytes 172040 | tf_op jit(solution)/shard_map/ppermute | solution.py:508
  150.7 7.5 %collective-permute-start.7 = (bf16[16,8,640]{2,1,0:T(8,128)(2,1)S(1)}, bf16[16,8,640]{2,1,0:T(8,128)(2,1)S(1)}, u32[]{:S(2)}, u32[]{:S(2)}) collective-permute-start(bf16[16,8,640]{2,1,0:T(8,128)(2,1)S(1)} %all-to-all-done.3.own_ref), channel_id=1, source_target_pairs={{0,8},{8,0},{1,9},{9,1},{2,10},{10,2},{3,11},{11,3},{4,12},{12,4},... | collective-permute-start | bytes 491528 | tf_op jit(solution)/shard_map/ppermute | solution.py:519
